TPU v7x, 32 devices: a whole 2x2x4 slice. The times are simulated.
32 devices in a mesh: groups: 2 (over y), tp: 4 (over z), dp: 4 (over x, core).
Axes of the slice: x: 2, y: 2, z: 4, core: 2. Of those that a mesh axis runs over, the one named last changes fastest.
Arguments:
- tokens: bfloat16 [4, 32, 8192], P(None, ('groups', 'dp'), 'tp'), parts along dimension 1, may hold values from -6 to 6
- lengths: int32 [32], P(('groups', 'dp')), parts along dimension 0, may hold values from 1 to 192, as said below
- cache_keys: bfloat16 [32, 192, 1024], P(('groups', 'dp'), 'tp'), parts along dimension 0, may hold values from -64 to 64
- cache_values: bfloat16 [32, 192, 1024], P(('groups', 'dp'), 'tp'), parts along dimension 0, may hold values from -6 to 6
- q_weight: bfloat16 [8192, 8192], P('dp', 'tp'), may hold values from -0.0625 to 0.0625
- kv_weight: bfloat16 [8192, 2048], P('tp'), may hold values from -0.0625 to 0.0625
- o_weight: bfloat16 [8192, 8192], P('tp', 'dp'), may hold values from -0.0625 to 0.0625
- adapters: bfloat16 [4, 64, 8192], P(None, None, ('tp', 'dp')), may hold values from -0.1875 to 0.1875
- layout: int32 [16], replicated, may hold values from 0 to 15, each once
Outputs:
- mixed: bfloat16 [4, 32, 8192], P(None, ('groups', 'dp'), 'tp'), parts along dimension 1
There are 2 independent parts, one for each index of `groups`. A program takes and returns all parts, laid end to end along the dimension named above; an argument that names none is the same for every part. Nothing has to cross between parts.
Inputs may be any that keep to these rules, and one draw needn't show every extreme that they name: `lengths`: one sequence has exactly 192 cached positions.
All inputs are finite; a program needn't handle non-finite values.
Results may differ from a plain program's by a relative error of at most 0.008.
The roundings to bfloat16 on the way count: a program that leaves them out, or rounds other values in their place, can miss the bound.
Values may be sent and summed in bfloat16 or wider, within the bound.
No kernel may reach another device: no remote copies, remote signals or barrier semaphores. Data moves between devices by JAX's collectives and lax.ppermute only.
A program may use at most 256 MiB of HBM per device.

v0:
```python
import jax
import jax.numpy as jnp
from jax import lax
from jax.sharding import PartitionSpec as P

HD = 128


def joined_2(array, axis, combine):
    everything = jax.tree.map(lambda part: lax.all_gather(part, axis), array)
    leading = jax.tree.map(lambda part: part[0], everything)

    def turn(k, so_far):
        return combine(so_far, jax.tree.map(lambda part: part[k], everything))

    return lax.fori_loop(1, lax.axis_size(axis), turn, leading)


def join_partials(first, second):
    top_a, total_a, summed_a = first
    top_b, total_b, summed_b = second
    top = jnp.maximum(top_a, top_b)
    factor_a = jnp.exp(top_a - top)
    factor_b = jnp.exp(top_b - top)
    return (
        top,
        total_a * factor_a + total_b * factor_b,
        summed_a * factor_a[..., None] + summed_b * factor_b[..., None],
    )


def pick_columns(stacked, inverse, factor, start, count):
    piece_cols = stacked.shape[3]
    block_ids = lax.dynamic_slice_in_dim(inverse, start // piece_cols, count // piece_cols, 0)
    chosen = jnp.take(stacked[factor], block_ids, axis=1)
    return chosen.reshape(stacked.shape[1], count)


def on_device(
    tokens, lengths, cache_keys, cache_values, q_weight, kv_weight, o_weight, adapters, layout
):
    tp_index = lax.axis_index("tp")
    dp_index = lax.axis_index("dp")
    steps, seq_dev, feat_dev = tokens.shape
    rank = adapters.shape[1]
    shards = layout.shape[0]
    rows = steps * seq_dev
    scale = HD ** (-0.5)
    gathered = lax.all_gather(adapters, ("tp", "dp"), axis=2, tiled=True)
    width = gathered.shape[2]
    piece_cols = width // shards
    stacked = gathered.reshape(4, rank, shards, piece_cols)
    block_numbers = jnp.arange(shards, dtype=jnp.int32)
    inverse = jnp.sum(
        jnp.where(layout[None, :] == block_numbers[:, None], block_numbers[None, :], 0), axis=1
    )
    kv_part = jnp.dot(tokens.reshape(rows, feat_dev), kv_weight, preferred_element_type=jnp.float32)
    new_kv = lax.psum(kv_part, "tp").astype(jnp.bfloat16)
    full_tokens = lax.all_gather(tokens, "tp", axis=2, tiled=True)
    q_rows = q_weight.shape[0]
    q_cols = q_weight.shape[1]
    o_cols = o_weight.shape[1]
    col_start = tp_index * q_cols
    q_down_part = pick_columns(stacked, inverse, 0, dp_index * q_rows, q_rows)
    q_up_part = pick_columns(stacked, inverse, 1, col_start, q_cols)
    o_down_part = pick_columns(stacked, inverse, 2, col_start, q_cols)
    o_up_part = pick_columns(stacked, inverse, 3, dp_index * o_cols, o_cols)
    q_merged = (
        q_weight.astype(jnp.float32)
        + jnp.einsum("rf,rc->fc", q_down_part, q_up_part, preferred_element_type=jnp.float32)
    ).astype(jnp.bfloat16)
    o_merged = (
        o_weight.astype(jnp.float32)
        + jnp.einsum("rf,rc->fc", o_down_part, o_up_part, preferred_element_type=jnp.float32)
    ).astype(jnp.bfloat16)
    flat_tokens = full_tokens.reshape(rows, width)
    q_total = jnp.dot(
        flat_tokens,
        lax.all_gather(q_merged, "dp", axis=0, tiled=True),
        preferred_element_type=jnp.float32,
    )
    queries = q_total.astype(jnp.bfloat16).reshape(steps, seq_dev, q_cols)
    all_queries = lax.all_gather(queries, "tp", axis=2, tiled=True)
    heads = all_queries.shape[2] // HD
    kv_heads = cache_keys.shape[2] // HD
    group = heads // kv_heads
    head_dev = q_cols // HD
    span = cache_keys.shape[1]
    grouped = all_queries.reshape(steps, seq_dev, kv_heads, group, HD)
    keys_local = cache_keys.reshape(seq_dev, span, kv_heads, HD)
    values_local = cache_values.reshape(seq_dev, span, kv_heads, HD)
    positions = tp_index * span + jnp.arange(span, dtype=jnp.int32)
    valid = (positions[None, :] < lengths[:, None])[None, :, None, None, :]
    scores = (
        jnp.einsum("sbkgd,bpkd->sbkgp", grouped, keys_local, preferred_element_type=jnp.float32)
        * scale
    )
    scores = jnp.where(valid, scores, -1e30)
    local_top = jnp.max(scores, axis=-1)
    weights = jnp.where(valid, jnp.exp(scores - local_top[..., None]), 0.0)
    local_total = jnp.sum(weights, axis=-1).reshape(steps, seq_dev, heads)
    local_sum = jnp.einsum("sbkgp,bpkd->sbkgd", weights, values_local.astype(jnp.float32)).reshape(
        steps, seq_dev, heads, HD
    )
    local_top = local_top.reshape(steps, seq_dev, heads)
    joined = joined_2((local_top, local_total, local_sum), "tp", join_partials)
    own_top = lax.dynamic_slice_in_dim(joined[0], tp_index * head_dev, head_dev, 2)
    own_total = lax.dynamic_slice_in_dim(joined[1], tp_index * head_dev, head_dev, 2)
    own_sum = lax.dynamic_slice_in_dim(joined[2], tp_index * head_dev, head_dev, 2)
    fresh = new_kv.reshape(steps, seq_dev, 2, kv_heads, HD)
    fresh_keys = lax.dynamic_slice_in_dim(
        jnp.repeat(fresh[:, :, 0], group, axis=2), tp_index * head_dev, head_dev, 2
    )
    fresh_values = lax.dynamic_slice_in_dim(
        jnp.repeat(fresh[:, :, 1], group, axis=2), tp_index * head_dev, head_dev, 2
    )
    own_queries = queries.reshape(steps, seq_dev, head_dev, HD)
    fresh_scores = (
        jnp.einsum("sbhd,tbhd->sbht", own_queries, fresh_keys, preferred_element_type=jnp.float32)
        * scale
    )
    causal = (
        jnp.arange(steps, dtype=jnp.int32)[:, None] >= jnp.arange(steps, dtype=jnp.int32)[None, :]
    )[:, None, None, :]
    fresh_scores = jnp.where(causal, fresh_scores, -1e30)
    top = jnp.maximum(own_top, jnp.max(fresh_scores, axis=-1))
    cache_factor = jnp.exp(own_top - top)
    fresh_weights = jnp.exp(fresh_scores - top[..., None])
    total = own_total * cache_factor + jnp.sum(fresh_weights, axis=-1)
    summed = own_sum * cache_factor[..., None] + jnp.einsum(
        "sbht,tbhd->sbhd", fresh_weights, fresh_values.astype(jnp.float32)
    )
    attn = (summed / total[..., None]).astype(jnp.bfloat16).reshape(rows, q_cols)
    blocks_in = o_cols // q_cols
    out_blocks = o_merged.reshape(q_cols, blocks_in, q_cols)
    partial_out = jnp.einsum(
        "snc,cjf->jnsf",
        lax.all_gather(attn.reshape(steps, seq_dev, q_cols), "dp", axis=1, tiled=True),
        out_blocks,
        preferred_element_type=jnp.float32,
    )
    dp_size = lax.axis_size("dp")
    tp_size = lax.axis_size("tp")
    arranged = partial_out.reshape(blocks_in * dp_size, seq_dev, steps, q_cols)
    spread_terms = jnp.zeros((tp_size * dp_size, seq_dev, steps, q_cols), jnp.float32)
    spread_terms = lax.dynamic_update_slice_in_dim(
        spread_terms, arranged, dp_index * blocks_in * dp_size, 0
    )
    own_rows = lax.psum_scatter(spread_terms, ("tp", "dp"), scatter_dimension=0, tiled=True)
    mixed = jnp.transpose(own_rows.reshape(seq_dev, steps, q_cols), (1, 0, 2)).astype(jnp.bfloat16)
    return mixed


def solution(mesh):
    return jax.shard_map(
        on_device,
        mesh=mesh,
        in_specs=(
            P(None, ("groups", "dp"), "tp"),
            P(("groups", "dp")),
            P(("groups", "dp"), "tp", None),
            P(("groups", "dp"), "tp", None),
            P("dp", "tp"),
            P("tp", None),
            P("tp", "dp"),
            P(None, None, ("tp", "dp")),
            P(),
        ),
        out_specs=P(None, ("groups", "dp"), "tp"),
        check_vma=False,
    )
```

profile of v0, /device:TPU:0, one launch (start us, length us, event | category | flops | bytes accessed | tf_op | source)
XLA Modules:
  0.0 472.8 jit_solution(2039699616438301984)
XLA Ops:
  7.3 0.8 select_reduce_fusion
  8.2 57.2 %all-gather.4.cloned.1.call-done = bf16[4,64,8192]{2,1,0:T(8,128)(2,1)} async-done(((bf16[4,64,512]{2,1,0:T(8,128)(2,1)}), bf16[4,64,8192]{2,1,0:T(8,128)(2,1)}) %all-gather.4.cloned.1.call-update) | async-done | bytes 4194320 | tf_op jit(solution)/shard_map/all_gather | solution.py:49
  65.5 2.6 fusion.34
  70.3 1.6 copy.113
  72.4 1.8 gather_fusion.2
  76.5 9.0 %add_convert_fusion = bf16[2048,2048]{1,0:T(8,128)(2,1)} fusion(bf16[2048,2048]{1,0:T(8,128)(2,1)} %param.17, bf16[64,2048]{1,0:T(8,128)(2,1)S(1)} %bitcast.145, bf16[64,2048]{1,0:T(8,128)(2,1)S(1)} %bitcast.149), kind=kOutput, calls=%fused_computation.12 | convolution fusion | flops 549453824 | bytes 17301504 | tf_op jit(solution)/shard_map/rf,rc->fc/dot_general | solution.py:70
  86.3 13.9 %all_gather.26 = bf16[4,4,8192]{2,1,0:T(4,128)(2,1)S(1)} all-gather(bf16[4,4,2048]{2,1,0:T(4,128)(2,1)S(1)} %copy-done.2), channel_id=1, replica_groups=mesh['groups'=2,'tp'=4,'dp'=4] {'tp'}, dimensions={2}, use_global_device_ids=true | all-gather | bytes 327680 | tf_op jit(solution)/shard_map/all_gather | solution.py:59
  100.6 184.8 %all-gather.6.cloned.1.call-done = bf16[8192,2048]{1,0:T(8,128)(2,1)} async-done(((bf16[2048,2048]{1,0:T(8,128)(2,1)}), bf16[8192,2048]{1,0:T(8,128)(2,1)}) %all-gather.6.cloned.1.call-update) | async-done | bytes 33554448 | tf_op jit(solution)/shard_map/all_gather | solution.py:79
  285.3 12.8 %convolution_convert_fusion = bf16[2048,16]{0,1:T(8,128)(2,1)S(1)} fusion(bf16[16,8192]{1,0:T(8,128)(2,1)S(1)} %reshape.114, bf16[8192,2048]{1,0:T(8,128)(2,1)} %all-gather.6.cloned.1.call-done), kind=kOutput, calls=%fused_computation.17 | convolution fusion | flops 536903680 | bytes 33882112 | tf_op jit(solution)/shard_map/dot_general | solution.py:77
  298.2 14.1 %all_gather.27 = bf16[4,4,8192]{2,1,0:T(4,128)(2,1)S(1)} all-gather(bf16[4,4,2048]{2,1,0:T(4,128)(2,1)S(1)} %reshape.115), channel_id=1, replica_groups=mesh['groups'=2,'tp'=4,'dp'=4] {'tp'}, dimensions={2}, use_global_device_ids=true | all-gather | bytes 327680 | tf_op jit(solution)/shard_map/all_gather | solution.py:83
  313.4 0.8 copy.171
  314.3 4.6 fusion.37
  318.9 25.2 %all-reduce.3 = bf16[16,2048]{1,0:T(8,128)(2,1)S(1)} all-reduce(f32[16,2048]{1,0:T(8,128)S(1)} %fusion.37), channel_id=1, replica_groups=mesh['groups'=2,'tp'=4,'dp'=4] {'tp'}, use_global_device_ids=true, to_apply=%region_5.7 | all-reduce | flops 32768 | bytes 196608 | tf_op jit(solution)/shard_map/psum | solution.py:58
  345.6 13.3 %all_gather.29 = f32[4,4,4,64]{3,2,1,0:T(4,128)S(1)} all-gather(f32[1,4,4,64]{3,2,1,0:T(4,128)S(1)} %all_gather_reshape.10), channel_id=1, replica_groups=mesh['groups'=2,'tp'=4,'dp'=4] {'tp'}, dimensions={0}, use_global_device_ids=true | all-gather | bytes 20480 | tf_op jit(solution)/shard_map/all_gather | solution.py:10
  358.9 13.1 %all_gather.28 = f32[4,4,4,64]{3,2,1,0:T(4,128)S(1)} all-gather(f32[1,4,4,64]{3,2,1,0:T(4,128)S(1)} %all_gather_reshape.9), channel_id=1, replica_groups=mesh['groups'=2,'tp'=4,'dp'=4] {'tp'}, dimensions={0}, use_global_device_ids=true | all-gather | bytes 20480 | tf_op jit(solution)/shard_map/all_gather | solution.py:10
  372.4 1.1 slice_bitcast_fusion
  373.5 4.8 %while.19 = (s32[]{:T(128)}, f32[4,4,64]{2,1,0:T(4,128)S(1)}, f32[4,4,64]{2,1,0:T(4,128)S(1)}, f32[4,4,64,128]{3,2,1,0:T(8,128)S(1)}, f32[4,4,4,64]{3,2,1,0:T(4,...) while((s32[]{:T(128)}, f32[4,4,64]{2,1,0:T(4,128)S(1)}, ...), condition=%wide.region_4.6_spmd, body=%wide.region_3.5_spmd.sunk | while | flops 399365 | bytes 1613975 | solution.py:16
  373.5 1.5 fusion.49
  375.1 1.5 fusion.49
  376.8 1.5 fusion.49
  379.5 5.8 %all_gather.31 = bf16[4,16,2048]{2,0,1:T(4,128)(2,1)S(1)} all-gather(bf16[4,4,2048]{2,0,1:T(4,128)(2,1)S(1)} %fusion.15), channel_id=1, replica_groups=mesh['groups'=2,'tp'=4,'dp'=4] {'dp'}, dimensions={1}, use_global_device_ids=true | all-gather | bytes 327680 | tf_op jit(solution)/shard_map/all_gather | solution.py:138
  385.3 7.2 %fusion.5 = f32[1,16,4,2048]{3,1,2,0:T(8,128)S(1)} fusion(bf16[64,2048]{1,0:T(8,128)(2,1)S(1)} %bitcast.157, bf16[64,2048]{1,0:T(8,128)(2,1)S(1)} %bitcast.158, bf16[2048,2048]{1,0:T(8,128)(2,1)} %param.19, bf16[4,16,2048]{2,0,1:T(4,128)(2,1)S(1)} %all_gather.31), kind=kOutput, calls=%fused_computation.16 | convolution fusion | flops 1086324736 | bytes 9699328 | tf_op jit(solution)/shard_map/snc,cjf->jnsf/dot_general | solution.py:136
  393.2 71.8 %all-reduce.4 = bf16[16,4,4,2048]{3,1,2,0:T(4,128)(2,1)S(1)} all-reduce(f32[16,4,4,2048]{3,1,2,0:T(4,128)S(1)} %copy_dynamic-update-slice_fusion), channel_id=2, replica_groups=mesh['groups'=2,'tp'=4,'dp'=4] {'tp','dp'}, use_global_device_ids=true, to_apply=%region_8.10.clone | all-reduce | flops 524288 | bytes 3145728
  465.0 1.3 fusion.25
  (77 shorter events, 11.8 us)
Async XLA Ops:
  6.5 58.9 %all-gather.4.cloned.1.call-start = ((), (), s32[]{:S(2)}) async-start(), calls=%async_computation | async-start | bytes 4456448 | tf_op jit(solution)/shard_map/all_gather | solution.py:49
  7.3 278.1 %all-gather.6.cloned.1.call-start = ((), (), s32[]{:S(2)}) async-start(), calls=%async_computation.1 | async-start | bytes 41943040 | tf_op jit(solution)/shard_map/all_gather | solution.py:79
  85.5 0.8 copy-start.2
  85.5 14.8 %copy-start = (bf16[4,48,1024]{2,1,0:T(8,128)(2,1)S(1)}, bf16[4,48,1024]{2,1,0:T(8,128)(2,1)}, u32[]{:S(2)}) copy-start(bf16[4,48,1024]{2,1,0:T(8,128)(2,1)} %param.15) | copy-start | bytes 1179652
  85.5 14.9 %copy-start.1 = (bf16[4,48,1024]{2,1,0:T(8,128)(2,1)S(1)}, bf16[4,48,1024]{2,1,0:T(8,128)(2,1)}, u32[]{:S(2)}) copy-start(bf16[4,48,1024]{2,1,0:T(8,128)(2,1)} %param.16) | copy-start | bytes 1179652
  85.5 15.0 %copy-start.3 = (s32[4]{0:T(128)S(1)}, s32[4]{0:T(128)}, u32[]{:S(2)}) copy-start(s32[4]{0:T(128)} %param.14) | copy-start | bytes 52
  85.5 286.9 %all-gather.8.cloned.1.call-start = ((), (), s32[]{:S(2)}) async-start(), calls=%async_computation.2 | async-start | bytes 2621440 | tf_op jit(solution)/shard_map/all_gather | solution.py:10
  314.3 30.0 %copy-start.4 = (u32[32]{0:T(128)S(1)}, u32[32]{0:T(128)}, u32[]{:S(2)}) copy-start(u32[32]{0:T(128)} %constant.107) | copy-start | bytes 388
Sparse Core Ops, SparseCore 0:
  9.5 55.9 all-gather.3
  85.6 199.6 all-gather.5
  314.4 50.2 all-gather.7
where the time goes:
time: 473 us
  waiting for transfers between devices  243 us (51%)
  blocking collectives  157 us (33%)
  matrix products  34.9 us (7%)
  local copies, waits for them, and re-layouts  17.8 us (4%)
  between operations  13.6 us (3%)
  other arithmetic  6.45 us (1%)
    all_gather x1, waiting for transfers between devices, on_device(): lax.all_gather(q_merged, 'dp', axis=0, tiled=True)  185 us
    unnamed x1, blocking collectives  71.8 us
    all_gather x1, waiting for transfers between devices, on_device(): gathered = lax.all_gather(adapters, ('tp', 'dp'), axis=2, tiled=True)  57.2 us
    all_gather x2, blocking collectives, joined_2(): everything = jax.tree.map(lambda part: lax.all_gather(part, axis), array)  26.4 us
    psum x1, blocking collectives, on_device(): new_kv = lax.psum(kv_part, 'tp').astype(jnp.bfloat16)  25.2 us
    all_gather x1, blocking collectives, on_device(): all_queries = lax.all_gather(queries, 'tp', axis=2, tiled=True)  14.1 us
    all_gather x1, blocking collectives, on_device(): full_tokens = lax.all_gather(tokens, 'tp', axis=2, tiled=True)  13.9 us
    dot_general x1, matrix products, on_device(): jnp.dot(flat_tokens, lax.all_gather(q_merged, 'dp', axis=0, tiled=True),...  12.8 us
  transfers between devices with their start and end apart: 3, of which 2 were waited for; matrix products, arithmetic and copies ran while one was open for 2% of the time, Pallas kernels for 0%

commit v1 on v0

--- a/solution.py
+++ b/solution.py
@@ -1,9 +1,187 @@
+import functools
+
 import jax
 import jax.numpy as jnp
 from jax import lax
+from jax.experimental import pallas as pl
+from jax.experimental.pallas import tpu as pltpu
 from jax.sharding import PartitionSpec as P
 
 HD = 128
+F32 = jnp.float32
+BF16 = jnp.bfloat16
+SIDE = 4
+MIB = 1 << 20
+
+
+def along_tp(x, k):
+    return lax.ppermute(x, "tp", [(i, (i + k) % SIDE) for i in range(SIDE)])
+
+
+def across_dp(x, k):
+    return lax.ppermute(x, "dp", [(i, i ^ k) for i in range(SIDE)])
+
+
+def to_holder(x, m):
+    pairs = [(t * SIDE + d, d * SIDE + (t ^ m)) for t in range(SIDE) for d in range(SIDE)]
+    return lax.ppermute(x, ("tp", "dp"), pairs)
+
+
+def all_blocks(x):
+    rows = [x] + [along_tp(x, k) for k in range(1, SIDE)]
+    blocks = []
+    for row in rows:
+        far = across_dp(row, 2)
+        blocks += [row, across_dp(row, 1), far, across_dp(far, 1)]
+    return rows, blocks
+
+
+def block_slots(inverse, first, t, d):
+    source = lax.dynamic_slice_in_dim(inverse, first, SIDE, 0)
+    return ((t - source // SIDE) % SIDE) * SIDE + ((source % SIDE) ^ d)
+
+
+def pick(slots_ref, blocks, down_ref, up_ref, sem, first_down, first_up):
+    for n in range(2 * SIDE):
+        factor, dst = (0, down_ref) if n < SIDE else (1, up_ref)
+        for s, block in enumerate(blocks):
+
+            @pl.when(slots_ref[n] == s)
+            def _(block=block, factor=factor, dst=dst, n=n):
+                pltpu.make_async_copy(block.at[factor], dst.at[n % SIDE], sem.at[n]).start()
+
+    for n in range(2 * SIDE):
+        factor, dst = (0, down_ref) if n < SIDE else (1, up_ref)
+        pltpu.make_async_copy(blocks[0].at[factor], dst.at[n % SIDE], sem.at[n]).wait()
+
+
+def merged_rows(w_ref, down_ref, up, i, width):
+    delta = lax.dot_general(down_ref[i], up, (((0,), (0,)), ((), ())), preferred_element_type=F32)
+    return (w_ref[i * width : (i + 1) * width, :].astype(F32) + delta).astype(BF16)
+
+
+def merge_dot_kernel(slots_ref, *refs):
+    blocks = refs[:16]
+    w_ref, x0, x1, x2, x3, out_ref, down_ref, up_ref, x_ref, sem = refs[16:]
+    step = pl.program_id(0)
+    width = down_ref.shape[2]
+    cols = w_ref.shape[1]
+    rows = x0.shape[0]
+
+    @pl.when(step == 0)
+    def _():
+        for k, piece in enumerate((x0, x1, x2, x3)):
+            x_ref[k * rows : (k + 1) * rows, :] = piece[...]
+        pick(slots_ref, blocks, down_ref, up_ref, sem, 0, 0)
+
+    per = width // cols
+    up = up_ref[step // per, :, pl.ds(pl.multiple_of((step % per) * cols, cols), cols)]
+    total = jnp.zeros(out_ref.shape, F32)
+    for i in range(SIDE):
+        merged = merged_rows(w_ref, down_ref, up, i, width)
+        total += jnp.dot(x_ref[:, i * width : (i + 1) * width], merged, preferred_element_type=F32)
+    out_ref[...] = total
+
+
+def merge_kernel(slots_ref, *refs):
+    blocks = refs[:16]
+    w_ref, out_ref, down_ref, up_ref, sem = refs[16:]
+    step = pl.program_id(0)
+    width = down_ref.shape[2]
+    cols = w_ref.shape[1]
+
+    @pl.when(step == 0)
+    def _():
+        pick(slots_ref, blocks, down_ref, up_ref, sem, 0, 0)
+
+    per = width // cols
+    up = up_ref[step // per, :, pl.ds(pl.multiple_of((step % per) * cols, cols), cols)]
+    for i in range(SIDE):
+        out_ref[i * width : (i + 1) * width, :] = merged_rows(w_ref, down_ref, up, i, width)
+
+
+def merge_call(kernel, slots, blocks, weight, pieces, out_rows, out_dtype, cols):
+    depth, width = weight.shape
+    rank, piece_cols = blocks[0].shape[1:]
+    any_spec = pl.BlockSpec(memory_space=pl.ANY)
+    scratch = [
+        pltpu.VMEM((SIDE, rank, piece_cols), BF16),
+        pltpu.VMEM((SIDE, rank, piece_cols), BF16),
+    ]
+    if pieces:
+        scratch.append(pltpu.VMEM((SIDE * pieces[0].shape[0], depth), BF16))
+    scratch.append(pltpu.SemaphoreType.DMA((2 * SIDE,)))
+    return pl.pallas_call(
+        kernel,
+        out_shape=jax.ShapeDtypeStruct((out_rows, width), out_dtype),
+        grid_spec=pltpu.PrefetchScalarGridSpec(
+            num_scalar_prefetch=1,
+            grid=(width // cols,),
+            in_specs=[any_spec] * 16
+            + [pl.BlockSpec((depth, cols), lambda j, s: (0, j))]
+            + [pl.BlockSpec(p.shape, lambda j, s: (0, 0)) for p in pieces],
+            out_specs=pl.BlockSpec((out_rows, cols), lambda j, s: (0, j)),
+            scratch_shapes=scratch,
+        ),
+        compiler_params=pltpu.CompilerParams(vmem_limit_bytes=24 * MIB),
+        cost_estimate=pl.CostEstimate(
+            flops=2 * depth * width * (rank + 64), bytes_accessed=2 * depth * width, transcendentals=0
+        ),
+    )(slots, *blocks, weight, *pieces)
+
+
+def attention_kernel(qa_ref, qb_ref, n0, n1, n2, n3, c0, c1, c2, c3, bias_ref, fresh_bias_ref, out_ref):
+    scale = HD ** (-0.5)
+    rows = qa_ref.shape[0]
+    kv_dev = c0.shape[2] // HD
+    group = qa_ref.shape[1] // HD // kv_dev
+    queries = (qa_ref[...] + qb_ref[...]).astype(BF16)
+    fresh = (n0[...] + n1[...] + n2[...] + n3[...]).astype(BF16)
+    contract_last = (((1,), (1,)), ((), ()))
+
+    def scores_of(q, keys, bias):
+        s = lax.dot_general(q, keys, contract_last, preferred_element_type=F32) * scale
+        s = s.reshape(group, rows, s.shape[1]) + bias[None]
+        return s.reshape(group * rows, s.shape[2])
+
+    def weighted(weights, values):
+        coarse = weights.astype(BF16)
+        rest = (weights - coarse.astype(F32)).astype(BF16)
+        return jnp.dot(coarse, values, preferred_element_type=F32) + jnp.dot(
+            rest, values, preferred_element_type=F32
+        )
+
+    for h in range(kv_dev):
+        lanes = slice(h * HD, (h + 1) * HD)
+        q = jnp.concatenate(
+            [queries[:, (h * group + g) * HD : (h * group + g + 1) * HD] for g in range(group)], axis=0
+        )
+        scores = [scores_of(q, c[0, :, lanes], bias_ref[k]) for k, c in enumerate((c0, c1, c2, c3))]
+        scores.append(scores_of(q, fresh[:, lanes], fresh_bias_ref[...]))
+        values = [c[1, :, lanes] for c in (c0, c1, c2, c3)]
+        values.append(fresh[:, (kv_dev + h) * HD : (kv_dev + h + 1) * HD])
+        top = functools.reduce(jnp.maximum, [jnp.max(s, axis=1, keepdims=True) for s in scores])
+        weights = [jnp.exp(s - top) for s in scores]
+        total = sum(jnp.sum(w, axis=1, keepdims=True) for w in weights)
+        summed = sum(weighted(w, v) for w, v in zip(weights, values))
+        attn = (summed / total).astype(BF16)
+        for g in range(group):
+            out_ref[:, (h * group + g) * HD : (h * group + g + 1) * HD] = attn[g * rows : (g + 1) * rows]
+
+
+def out_kernel(turn_ref, a0, a1, a2, a3, w_ref, first_ref, rest_ref, x_ref):
+    rows = a0.shape[0]
+
+    @pl.when(pl.program_id(0) == 0)
+    def _():
+        for k, piece in enumerate((a0, a1, a2, a3)):
+            at = pl.multiple_of((turn_ref[0] ^ k) * rows, rows)
+            x_ref[pl.ds(at, rows), :] = piece[...]
+
+    total = jnp.dot(x_ref[...], w_ref[...], preferred_element_type=F32)
+    first_ref[...] = total[:rows]
+    for m in range(1, SIDE):
+        rest_ref[m - 1] = total[m * rows : (m + 1) * rows].astype(BF16)
 
 
 def joined_2(array, axis, combine):
@@ -36,7 +214,7 @@
     return chosen.reshape(stacked.shape[1], count)
 
 
-def on_device(
+def general(
     tokens, lengths, cache_keys, cache_values, q_weight, kv_weight, o_weight, adapters, layout
 ):
     tp_index = lax.axis_index("tp")
@@ -151,9 +329,116 @@
     return mixed
 
 
+def on_device(
+    tokens, lengths, cache_keys, cache_values, q_weight, kv_weight, o_weight, adapters, layout
+):
+    t = lax.axis_index("tp")
+    d = lax.axis_index("dp")
+    steps, seq_dev, feat_dev = tokens.shape
+    rows = steps * seq_dev
+    span = cache_keys.shape[1]
+    kv_cols = cache_keys.shape[2] // SIDE
+    shards = layout.shape[0]
+    numbers = jnp.arange(shards, dtype=jnp.int32)
+    inverse = jnp.sum(jnp.where(layout[None, :] == numbers[:, None], numbers[None, :], 0), axis=1)
+    of_d = block_slots(inverse, d * SIDE, t, d)
+    of_t = block_slots(inverse, t * SIDE, t, d)
+    q_slots = jnp.concatenate([of_d, of_t])
+    o_slots = jnp.concatenate([of_t, of_d])
+    own = tokens.reshape(rows, feat_dev)
+
+    q_rows, q_blocks = all_blocks(adapters[:2])
+
+    by_feature = jnp.stack([own] + [along_tp(own, k) for k in range(1, SIDE)])
+
+    def features(block):
+        return lax.dynamic_index_in_dim(by_feature, (t - block) % SIDE, 0, keepdims=False)
+
+    pieces = [features(d)] + [across_dp(features(d ^ k), k) for k in range(1, SIDE)]
+
+    kv_part = jnp.dot(own, kv_weight, preferred_element_type=F32)
+
+    def kv_of(head):
+        halves = [
+            lax.dynamic_slice_in_dim(kv_part, base + head * kv_cols, kv_cols, 1)
+            for base in (0, kv_cols * SIDE)
+        ]
+        return jnp.concatenate(halves, axis=1)
+
+    kv_terms = [kv_of(t)] + [along_tp(kv_of((t + k) % SIDE), k) for k in range(1, SIDE)]
+
+    cache = jnp.stack([cache_keys, cache_values]).reshape(2, seq_dev * span, SIDE * kv_cols)
+
+    def cache_of(head):
+        return lax.dynamic_slice_in_dim(cache, head * kv_cols, kv_cols, 2)
+
+    caches = [cache_of(t)] + [along_tp(cache_of((t + k) % SIDE), k) for k in range(1, SIDE)]
+    o_rows, o_blocks = all_blocks(adapters[2:])
+
+    q_part = merge_call(merge_dot_kernel, q_slots, q_blocks, q_weight, pieces, SIDE * rows, F32, 256)
+    near = across_dp(jnp.concatenate([q_part[rows : 2 * rows], q_part[3 * rows :]]), 1)
+    q_near = q_part[:rows] + near[:rows]
+    q_far = across_dp(q_part[2 * rows : 3 * rows] + near[rows:], 2)
+
+    seq_of_row = jnp.arange(rows, dtype=jnp.int32) % seq_dev
+    step_of_row = jnp.arange(rows, dtype=jnp.int32) // seq_dev
+    column = jnp.arange(seq_dev * span, dtype=jnp.int32)
+    came_from = (t - jnp.arange(SIDE, dtype=jnp.int32)) % SIDE
+    position = came_from[:, None] * span + (column % span)[None, :]
+    inside = position < jnp.repeat(lengths, span)[None, :]
+    same = (column // span)[None, :] == seq_of_row[:, None]
+    bias = jnp.where(inside[:, None, :] & same[None], 0.0, -1e30).astype(F32)
+    causal = (step_of_row[None, :] <= step_of_row[:, None]) & (seq_of_row[None, :] == seq_of_row[:, None])
+    fresh_bias = jnp.where(causal, 0.0, -1e30).astype(F32)
+
+    attn = pl.pallas_call(
+        attention_kernel,
+        out_shape=jax.ShapeDtypeStruct((rows, q_weight.shape[1]), BF16),
+        compiler_params=pltpu.CompilerParams(vmem_limit_bytes=16 * MIB),
+    )(q_near, q_far, *kv_terms, *caches, bias, fresh_bias)
+
+    o_merged = merge_call(merge_kernel, o_slots, o_blocks, o_weight, [], o_weight.shape[0], BF16, 256)
+    attn_rows = [attn] + [across_dp(attn, k) for k in range(1, SIDE)]
+    depth, width = o_weight.shape
+    cols = 512
+    first, rest = pl.pallas_call(
+        out_kernel,
+        out_shape=(
+            jax.ShapeDtypeStruct((rows, width), F32),
+            jax.ShapeDtypeStruct((SIDE - 1, rows, width), BF16),
+        ),
+        grid_spec=pltpu.PrefetchScalarGridSpec(
+            num_scalar_prefetch=1,
+            grid=(width // cols,),
+            in_specs=[pl.BlockSpec((rows, depth), lambda j, s: (0, 0))] * SIDE
+            + [pl.BlockSpec((depth, cols), lambda j, s: (0, j))],
+            out_specs=(
+                pl.BlockSpec((rows, cols), lambda j, s: (0, j)),
+                pl.BlockSpec((SIDE - 1, rows, cols), lambda j, s: (0, 0, j)),
+            ),
+            scratch_shapes=[pltpu.VMEM((SIDE * rows, depth), BF16)],
+        ),
+        compiler_params=pltpu.CompilerParams(vmem_limit_bytes=16 * MIB),
+    )((t ^ d).reshape(1), *attn_rows, o_merged)
+    mixed = to_holder(first, 0)
+    for m in range(1, SIDE):
+        mixed = mixed + to_holder(rest[m - 1], m).astype(F32)
+    return mixed.astype(BF16).reshape(steps, seq_dev, width)
+
+
 def solution(mesh):
+    def fits(layout, cache_keys):
+        sides = mesh.shape["tp"] == SIDE and mesh.shape["dp"] == SIDE
+        return sides and layout.shape[0] == SIDE * SIDE
+
+    def run(tokens, lengths, cache_keys, cache_values, q_weight, kv_weight, o_weight, adapters, layout):
+        body = on_device if fits(layout, cache_keys) else general
+        return body(
+            tokens, lengths, cache_keys, cache_values, q_weight, kv_weight, o_weight, adapters, layout
+        )
+
     return jax.shard_map(
-        on_device,
+        run,
         mesh=mesh,
         in_specs=(
             P(None, ("groups", "dp"), "tp"),

time: 473 us -> 134 us (0.28)
  waiting for transfers between devices: 243 us -> 49.6 us
  blocking collectives: 157 us -> 0 us
  starting transfers between devices: 0.08 us -> 45 us
  matrix products: 34.9 us -> 4.58 us
  Pallas kernels: 0 us -> 22.4 us
  between operations: 13.6 us -> 0.5 us
  local copies, waits for them, and re-layouts: 17.8 us -> 9.53 us
    all_gather x3 -> x0, waiting for transfers between devices: 242 us -> none  [the longest x1 185 us: on_device(): lax.all_gather(q_merged, 'dp', axis=0, tiled=True)]
    unnamed x1 -> x0, blocking collectives: 71.8 us -> none
    all_gather x5 -> x0, blocking collectives: 60.2 us -> none  [the longest x2 26.4 us: joined_2(): everything = jax.tree.map(lambda part: lax.all_gather(part, axis), array)]
    ppermute x0 -> x51, waiting for transfers between devices: none -> 49.6 us  [the longest x15 25.3 us: along_tp(): return lax.ppermute(x, 'tp', [(i, (i + k) % SIDE) for i in range(SIDE)])]
    ppermute x0 -> x51, starting transfers between devices: none -> 45 us  [the longest x15 22.5 us: along_tp(): return lax.ppermute(x, 'tp', [(i, (i + k) % SIDE) for i in range(SIDE)])]
    dot_general x8 -> x1, matrix products: 34.9 us -> 4.58 us  [on_device(): kv_part = jnp.dot(own, kv_weight, preferred_element_type=F32)]
    psum x1 -> x0, blocking collectives: 25.2 us -> none  [on_device(): new_kv = lax.psum(kv_part, 'tp').astype(jnp.bfloat16)]
    pallas_call x0 -> x4, Pallas kernels: none -> 22.4 us  [the longest x2 18.3 us: merge_call(): pl.pallas_call(kernel, out_shape=jax.ShapeDtypeStruct((out_rows, width),...]
  transfers between devices with their start and end apart: 3 -> 51, of which waited for: 2 -> 14; matrix products, arithmetic and copies ran while one was open for 2% -> 6% of each run, Pallas kernels for 0% -> 15%
where the time goes in v1:
time: 134 us
  waiting for transfers between devices  49.6 us (37%)
  starting transfers between devices  45 us (34%)
  Pallas kernels  22.4 us (17%)
  local copies, waits for them, and re-layouts  9.53 us (7%)
  matrix products  4.58 us (3%)
  other arithmetic  1.94 us (1%)
    ppermute x15, waiting for transfers between devices, along_tp(): return lax.ppermute(x, 'tp', [(i, (i + k) % SIDE) for i in range(SIDE)])  25.3 us
    ppermute x15, starting transfers between devices, along_tp(): return lax.ppermute(x, 'tp', [(i, (i + k) % SIDE) for i in range(SIDE)])  22.5 us
    pallas_call x2, Pallas kernels, merge_call(): pl.pallas_call(kernel, out_shape=jax.ShapeDtypeStruct((out_rows, width),...  18.3 us
    ppermute x32, starting transfers between devices, across_dp(): return lax.ppermute(x, 'dp', [(i, i ^ k) for i in range(SIDE)])  14.3 us
    ppermute x32, waiting for transfers between devices, across_dp(): return lax.ppermute(x, 'dp', [(i, i ^ k) for i in range(SIDE)])  12.3 us
    ppermute x4, waiting for transfers between devices, to_holder(): return lax.ppermute(x, ('tp', 'dp'), pairs)  12.1 us
    ppermute x4, starting transfers between devices, to_holder(): return lax.ppermute(x, ('tp', 'dp'), pairs)  8.27 us
    unnamed x10, local copies, waits for them, and re-layouts  6.78 us
  transfers between devices with their start and end apart: 51, of which 14 were waited for; matrix products, arithmetic and copies ran while one was open for 6% of the time, Pallas kernels for 15%

profile of v1, /device:TPU:0, one launch (start us, length us, event | category | flops | bytes accessed | tf_op | source)
XLA Modules:
  0.0 133.6 jit_solution(5337943629642845687)
XLA Ops:
  0.9 5.1 %collective-permute-start.17 = (bf16[16,2048]{1,0:T(8,128)(2,1)S(1)}, bf16[16,2048]{1,0:T(8,128)(2,1)S(1)}, u32[]{:S(2)}, u32[]{:S(2)}) collective-permute-start(bf16[16,2048]{1,0:T(8,128)(2,1)S(1)} %reshape.162), channel_id=1, source_target_pairs={{0,12},{4,0},{8,4},{12,8},{1,13},{5,1},{9,5},{13,9},{2,14},{6,2},{... | collective-permute-start | bytes 196616 | tf_op jit(solution)/shard_map/ppermute | solution.py:18
  8.0 2.9 %collective-permute-start.11 = (bf16[2,64,512]{2,1,0:T(8,128)(2,1)S(1)}, bf16[2,64,512]{2,1,0:T(8,128)(2,1)S(1)}, u32[]{:S(2)}, u32[]{:S(2)}) collective-permute-start(bf16[2,64,512]{2,1,0:T(8,128)(2,1)S(1)} %get-tuple-element.18.refs_0_), channel_id=1, source_target_pairs={{0,12},{4,0},{8,4},{12,8},{1,13},{5,1},{9,5},{13,9},{2,14},{6,2},{... | collective-permute-start | bytes 393224 | tf_op jit(solution)/shard_map/ppermute | solution.py:18
  12.0 4.6 %fusion.17 = f32[16,2048]{1,0:T(8,128)S(1)} fusion(bf16[16,2048]{1,0:T(8,128)(2,1)S(1)} %reshape.162, bf16[2048,2048]{1,0:T(8,128)(2,1)} %param.14), kind=kOutput, calls=%fused_computation.86 | convolution fusion | flops 134217728 | bytes 8585216 | tf_op jit(solution)/shard_map/dot_general | solution.py:359
  17.0 1.6 %collective-permute-start.19 = (bf16[16,2048]{1,0:T(8,128)(2,1)S(1)}, bf16[16,2048]{1,0:T(8,128)(2,1)S(1)}, u32[]{:S(2)}, u32[]{:S(2)}) collective-permute-start(bf16[16,2048]{1,0:T(8,128)(2,1)S(1)} %get-tuple-element.20), channel_id=1, source_target_pairs={{0,2},{1,3},{2,0},{3,1},{4,6},{5,7},{6,4},{7,5},{8,10},{9,11},{10,... | collective-permute-start | bytes 196616 | tf_op jit(solution)/shard_map/ppermute | solution.py:22
  18.9 2.5 %collective-permute-done.20.refs_20_ = bf16[16,2048]{1,0:T(8,128)(2,1)S(1)} collective-permute-done((bf16[16,2048]{1,0:T(8,128)(2,1)S(1)}, bf16[16,2048]{1,0:T(8,128)(2,1)S(1)}, u32[]{:S(2)}, u32[]{:S(2)}) %collective-permute-start.20) | collective-permute-done | bytes 65568 | tf_op jit(solution)/shard_map/ppermute | solution.py:22
  21.4 1.7 %collective-permute-start.3 = (bf16[2,64,512]{2,1,0:T(8,128)(2,1)S(1)}, bf16[2,64,512]{2,1,0:T(8,128)(2,1)S(1)}, u32[]{:S(2)}, u32[]{:S(2)}) collective-permute-start(bf16[2,64,512]{2,1,0:T(8,128)(2,1)S(1)} %get-tuple-element.18.refs_0_), channel_id=1, source_target_pairs={{0,4},{4,8},{8,12},{12,0},{1,5},{5,9},{9,13},{13,1},{2,6},{6,10},{... | collective-permute-start | bytes 393224 | tf_op jit(solution)/shard_map/ppermute | solution.py:18
  25.5 3.2 %collective-permute-done.3.refs_4_ = bf16[2,64,512]{2,1,0:T(8,128)(2,1)S(1)} collective-permute-done((bf16[2,64,512]{2,1,0:T(8,128)(2,1)S(1)}, bf16[2,64,512]{2,1,0:T(8,128)(2,1)S(1)}, u32[]{:S(2)}, u32[]{:S(2)}) %collective-permute-start.3) | collective-permute-done | bytes 131104 | tf_op jit(solution)/shard_map/ppermute | solution.py:18
  32.1 3.0 %collective-permute-done.9.refs_10_ = bf16[2,64,512]{2,1,0:T(8,128)(2,1)S(1)} collective-permute-done((bf16[2,64,512]{2,1,0:T(8,128)(2,1)S(1)}, bf16[2,64,512]{2,1,0:T(8,128)(2,1)S(1)}, u32[]{:S(2)}, u32[]{:S(2)}) %collective-permute-start.9) | collective-permute-done | bytes 131104 | tf_op jit(solution)/shard_map/ppermute | solution.py:22
  37.0 2.5 %collective-permute-start.23 = (f32[16,512]{1,0:T(8,128)S(1)}, f32[16,512]{1,0:T(8,128)S(1)}, u32[]{:S(2)}, u32[]{:S(2)}) collective-permute-start(f32[16,512]{1,0:T(8,128)S(1)} %pad_maximum_fusion.3), channel_id=1, source_target_pairs={{0,4},{4,8},{8,12},{12,0},{1,5},{5,9},{9,13},{13,1},{2,6},{6,10},{... | collective-permute-start | bytes 98312 | tf_op jit(solution)/shard_map/ppermute | solution.py:18
  40.7 2.8 %collective-permute-start.25 = (f32[16,512]{1,0:T(8,128)S(1)}, f32[16,512]{1,0:T(8,128)S(1)}, u32[]{:S(2)}, u32[]{:S(2)}) collective-permute-start(f32[16,512]{1,0:T(8,128)S(1)} %pad_maximum_fusion.5), channel_id=1, source_target_pairs={{0,12},{4,0},{8,4},{12,8},{1,13},{5,1},{9,5},{13,9},{2,14},{6,2},{... | collective-permute-start | bytes 98312 | tf_op jit(solution)/shard_map/ppermute | solution.py:18
  43.9 3.4 %copy-done = bf16[2048,2048]{1,0:T(8,128)(2,1)S(1)} copy-done((bf16[2048,2048]{1,0:T(8,128)(2,1)S(1)}, bf16[2048,2048]{1,0:T(8,128)(2,1)}, u32[]{:S(2)}) %copy-start) | copy-done | bytes 8388632
  47.3 9.8 %shard_map.91 = f32[64,2048]{1,0:T(8,128)S(1)} custom-call(s32[8]{0:T(128)S(1)} %get-tuple-element.35.slots_ref, bf16[2,64,512]{2,1,0:T(8,128)(2,1)S(1)} %get-tuple-element.18.refs_0_, bf16[2,64,512]{2,1,0:T(8,128)(2,1)S(1)} %collective-permute-done.refs_1_, bf16[2,64,512]{2,1,0:T(8,128)(2,1)S(1)} %collective-permute-done.1.refs_2_, ...), custom_call_target="tpu_custom_call" | custom-call | flops 1073741824 | bytes 8388608 | tf_op jit(solution)/shard_map/pallas_call | solution.py:114
  61.2 8.5 %collective-permute-done.39.refs_8_ = bf16[2,64,512]{2,1,0:T(8,128)(2,1)S(1)} collective-permute-done((bf16[2,64,512]{2,1,0:T(8,128)(2,1)S(1)}, bf16[2,64,512]{2,1,0:T(8,128)(2,1)S(1)}, u32[]{:S(2)}, u32[]{:S(2)}) %collective-permute-start.39) | collective-permute-done | bytes 131104 | tf_op jit(solution)/shard_map/ppermute | solution.py:18
  69.7 2.0 %collective-permute-start.26 = (bf16[2,192,256]{2,1,0:T(8,128)(2,1)S(1)}, bf16[2,192,256]{2,1,0:T(8,128)(2,1)S(1)}, u32[]{:S(2)}, u32[]{:S(2)}) collective-permute-start(bf16[2,192,256]{2,1,0:T(8,128)(2,1)S(1)} %get-tuple-element.11), channel_id=1, source_target_pairs={{0,4},{4,8},{8,12},{12,0},{1,5},{5,9},{9,13},{13,1},{2,6},{6,10},{... | collective-permute-start | bytes 589832 | tf_op jit(solution)/shard_map/ppermute | solution.py:18
  72.5 8.9 %collective-permute-done.28.c3 = bf16[2,192,256]{2,1,0:T(8,128)(2,1)S(1)} collective-permute-done((bf16[2,192,256]{2,1,0:T(8,128)(2,1)S(1)}, bf16[2,192,256]{2,1,0:T(8,128)(2,1)S(1)}, u32[]{:S(2)}, u32[]{:S(2)}) %collective-permute-start.28) | collective-permute-done | bytes 196640 | tf_op jit(solution)/shard_map/ppermute | solution.py:18
  82.1 4.7 %collective-permute-done.27.c2 = bf16[2,192,256]{2,1,0:T(8,128)(2,1)S(1)} collective-permute-done((bf16[2,192,256]{2,1,0:T(8,128)(2,1)S(1)}, bf16[2,192,256]{2,1,0:T(8,128)(2,1)S(1)}, u32[]{:S(2)}, u32[]{:S(2)}) %collective-permute-start.27) | collective-permute-done | bytes 196640 | tf_op jit(solution)/shard_map/ppermute | solution.py:18
  89.5 3.2 %collective-permute-done.37.refs_6_ = bf16[2,64,512]{2,1,0:T(8,128)(2,1)S(1)} collective-permute-done((bf16[2,64,512]{2,1,0:T(8,128)(2,1)S(1)}, bf16[2,64,512]{2,1,0:T(8,128)(2,1)S(1)}, u32[]{:S(2)}, u32[]{:S(2)}) %collective-permute-start.37) | collective-permute-done | bytes 131104 | tf_op jit(solution)/shard_map/ppermute | solution.py:22
  97.8 3.4 %copy-done.1 = bf16[2048,2048]{1,0:T(8,128)(2,1)S(1)} copy-done((bf16[2048,2048]{1,0:T(8,128)(2,1)S(1)}, bf16[2048,2048]{1,0:T(8,128)(2,1)}, u32[]{:S(2)}) %copy-start.1) | copy-done | bytes 8388632
  101.2 8.5 %shard_map.93.w_ref = bf16[2048,2048]{1,0:T(8,128)(2,1)S(1)} custom-call(s32[8]{0:T(128)S(1)} %get-tuple-element.34.slots_ref, bf16[2,64,512]{2,1,0:T(8,128)(2,1)S(1)} %get-tuple-element.17.refs_0_, bf16[2,64,512]{2,1,0:T(8,128)(2,1)S(1)} %collective-permute-done.32.refs_1_, bf16[2,64,512]{2,1,0:T(8,128)(2,1)S(1)} %collective-permute-done.33.refs_2_, ...), custom_call_target="tpu_custom_call" | custom-call | flops 1073741824 | bytes 8388608 | tf_op jit(solution)/shard_map/pallas_call | solution.py:114
  109.8 2.7 %shard_map.94 = (f32[16,2048]{1,0:T(8,128)S(1)}, bf16[3,16,2048]{2,1,0:T(8,128)(2,1)S(1)}) custom-call(s32[1]{0:T(128)} %bitcast.turn_ref, bf16[16,2048]{1,0:T(8,128)(2,1)S(1)} %shard_map.92.a0, bf16[16,2048]{1,0:T(8,128)(2,1)S(1)} %collective-permute-done.29.a1, bf16[16,2048]{1,0:T(8,128)(2,1)S(1)} %collective-permute-done.30.a2, ...), custom_call_target="tpu_custom_call" | custom-call | tf_op jit(solution)/shard_map/pallas_call | solution.py:404
  113.2 3.6 %collective-permute-start.48 = (bf16[16,2048]{1,0:T(8,128)(2,1)S(1)}, bf16[16,2048]{1,0:T(8,128)(2,1)S(1)}, u32[]{:S(2)}, u32[]{:S(2)}) collective-permute-start(bf16[16,2048]{1,0:T(8,128)(2,1)S(1)} %get-tuple-element.23), channel_id=1, source_target_pairs={{0,1},{1,5},{2,9},{3,13},{4,0},{5,4},{6,8},{7,12},{8,3},{9,7},{10,... | collective-permute-start | bytes 196616 | tf_op jit(solution)/shard_map/ppermute | solution.py:27
  116.8 4.0 %collective-permute-start.50 = (bf16[16,2048]{1,0:T(8,128)(2,1)S(1)}, bf16[16,2048]{1,0:T(8,128)(2,1)S(1)}, u32[]{:S(2)}, u32[]{:S(2)}) collective-permute-start(bf16[16,2048]{1,0:T(8,128)(2,1)S(1)} %get-tuple-element.24), channel_id=1, source_target_pairs={{0,3},{1,7},{2,11},{3,15},{4,2},{5,6},{6,10},{7,14},{8,1},{9,5},{1... | collective-permute-start | bytes 196616 | tf_op jit(solution)/shard_map/ppermute | solution.py:27
  121.4 5.2 %collective-permute-done.50 = bf16[16,2048]{1,0:T(8,128)(2,1)S(1)} collective-permute-done((bf16[16,2048]{1,0:T(8,128)(2,1)S(1)}, bf16[16,2048]{1,0:T(8,128)(2,1)S(1)}, u32[]{:S(2)}, u32[]{:S(2)}) %collective-permute-start.50) | collective-permute-done | bytes 65568 | tf_op jit(solution)/shard_map/ppermute | solution.py:27
  126.7 6.2 %collective-permute-done.49 = bf16[16,2048]{1,0:T(8,128)(2,1)S(1)} collective-permute-done((bf16[16,2048]{1,0:T(8,128)(2,1)S(1)}, bf16[16,2048]{1,0:T(8,128)(2,1)S(1)}, u32[]{:S(2)}, u32[]{:S(2)}) %collective-permute-start.49) | collective-permute-done | bytes 65568 | tf_op jit(solution)/shard_map/ppermute | solution.py:27
  (121 shorter events, 29.1 us)
Async XLA Ops:
  0.9 16.0 %collective-permute-start.17 = (bf16[16,2048]{1,0:T(8,128)(2,1)S(1)}, bf16[16,2048]{1,0:T(8,128)(2,1)S(1)}, u32[]{:S(2)}, u32[]{:S(2)}) collective-permute-start(bf16[16,2048]{1,0:T(8,128)(2,1)S(1)} %reshape.162), channel_id=1, source_target_pairs={{0,12},{4,0},{8,4},{12,8},{1,13},{5,1},{9,5},{13,9},{2,14},{6,2},{... | collective-permute-start | bytes 196616 | tf_op jit(solution)/shard_map/ppermute | solution.py:18
  6.0 10.9 %collective-permute-start.16 = (bf16[16,2048]{1,0:T(8,128)(2,1)S(1)}, bf16[16,2048]{1,0:T(8,128)(2,1)S(1)}, u32[]{:S(2)}, u32[]{:S(2)}) collective-permute-start(bf16[16,2048]{1,0:T(8,128)(2,1)S(1)} %reshape.162), channel_id=1, source_target_pairs={{0,8},{4,12},{8,0},{12,4},{1,9},{5,13},{9,1},{13,5},{2,10},{6,14},... | collective-permute-start | bytes 196616 | tf_op jit(solution)/shard_map/ppermute | solution.py:18
  6.0 10.9 %collective-permute-start.15 = (bf16[16,2048]{1,0:T(8,128)(2,1)S(1)}, bf16[16,2048]{1,0:T(8,128)(2,1)S(1)}, u32[]{:S(2)}, u32[]{:S(2)}) collective-permute-start(bf16[16,2048]{1,0:T(8,128)(2,1)S(1)} %reshape.162), channel_id=1, source_target_pairs={{0,4},{4,8},{8,12},{12,0},{1,5},{5,9},{9,13},{13,1},{2,6},{6,10},{... | collective-permute-start | bytes 196616 | tf_op jit(solution)/shard_map/ppermute | solution.py:18
  8.0 16.1 %collective-permute-start.11 = (bf16[2,64,512]{2,1,0:T(8,128)(2,1)S(1)}, bf16[2,64,512]{2,1,0:T(8,128)(2,1)S(1)}, u32[]{:S(2)}, u32[]{:S(2)}) collective-permute-start(bf16[2,64,512]{2,1,0:T(8,128)(2,1)S(1)} %get-tuple-element.18.refs_0_), channel_id=1, source_target_pairs={{0,12},{4,0},{8,4},{12,8},{1,13},{5,1},{9,5},{13,9},{2,14},{6,2},{... | collective-permute-start | bytes 393224 | tf_op jit(solution)/shard_map/ppermute | solution.py:18
  10.8 14.4 %collective-permute-start.7 = (bf16[2,64,512]{2,1,0:T(8,128)(2,1)S(1)}, bf16[2,64,512]{2,1,0:T(8,128)(2,1)S(1)}, u32[]{:S(2)}, u32[]{:S(2)}) collective-permute-start(bf16[2,64,512]{2,1,0:T(8,128)(2,1)S(1)} %get-tuple-element.18.refs_0_), channel_id=1, source_target_pairs={{0,8},{4,12},{8,0},{12,4},{1,9},{5,13},{9,1},{13,5},{2,10},{6,14},... | collective-permute-start | bytes 393224 | tf_op jit(solution)/shard_map/ppermute | solution.py:18
  37.0 20.3 %collective-permute-start.23 = (f32[16,512]{1,0:T(8,128)S(1)}, f32[16,512]{1,0:T(8,128)S(1)}, u32[]{:S(2)}, u32[]{:S(2)}) collective-permute-start(f32[16,512]{1,0:T(8,128)S(1)} %pad_maximum_fusion.3), channel_id=1, source_target_pairs={{0,4},{4,8},{8,12},{12,0},{1,5},{5,9},{9,13},{13,1},{2,6},{6,10},{... | collective-permute-start | bytes 98312 | tf_op jit(solution)/shard_map/ppermute | solution.py:18
  39.5 18.1 %collective-permute-start.24 = (f32[16,512]{1,0:T(8,128)S(1)}, f32[16,512]{1,0:T(8,128)S(1)}, u32[]{:S(2)}, u32[]{:S(2)}) collective-permute-start(f32[16,512]{1,0:T(8,128)S(1)} %pad_maximum_fusion.4), channel_id=1, source_target_pairs={{0,8},{4,12},{8,0},{12,4},{1,9},{5,13},{9,1},{13,5},{2,10},{6,14},... | collective-permute-start | bytes 98312 | tf_op jit(solution)/shard_map/ppermute | solution.py:18
  40.7 18.3 %collective-permute-start.25 = (f32[16,512]{1,0:T(8,128)S(1)}, f32[16,512]{1,0:T(8,128)S(1)}, u32[]{:S(2)}, u32[]{:S(2)}) collective-permute-start(f32[16,512]{1,0:T(8,128)S(1)} %pad_maximum_fusion.5), channel_id=1, source_target_pairs={{0,12},{4,0},{8,4},{12,8},{1,13},{5,1},{9,5},{13,9},{2,14},{6,2},{... | collective-permute-start | bytes 98312 | tf_op jit(solution)/shard_map/ppermute | solution.py:18
  43.5 17.6 %collective-permute-start.43 = (bf16[2,64,512]{2,1,0:T(8,128)(2,1)S(1)}, bf16[2,64,512]{2,1,0:T(8,128)(2,1)S(1)}, u32[]{:S(2)}, u32[]{:S(2)}) collective-permute-start(bf16[2,64,512]{2,1,0:T(8,128)(2,1)S(1)} %get-tuple-element.17.refs_0_), channel_id=1, source_target_pairs={{0,12},{4,0},{8,4},{12,8},{1,13},{5,1},{9,5},{13,9},{2,14},{6,2},{... | collective-permute-start | bytes 393224 | tf_op jit(solution)/shard_map/ppermute | solution.py:18
  57.1 14.6 %collective-permute-start.21 = (f32[32,2048]{1,0:T(8,128)S(1)}, f32[32,2048]{1,0:T(8,128)S(1)}, u32[]{:S(2)}, u32[]{:S(2)}) collective-permute-start(f32[32,2048]{1,0:T(8,128)S(1)} %pad_maximum_fusion.1), channel_id=1, source_target_pairs={{0,1},{1,0},{2,3},{3,2},{4,5},{5,4},{6,7},{7,6},{8,9},{9,8},{10,11... | collective-permute-start | bytes 786440 | tf_op jit(solution)/shard_map/ppermute | solution.py:22
  57.3 12.4 %collective-permute-start.39 = (bf16[2,64,512]{2,1,0:T(8,128)(2,1)S(1)}, bf16[2,64,512]{2,1,0:T(8,128)(2,1)S(1)}, u32[]{:S(2)}, u32[]{:S(2)}) collective-permute-start(bf16[2,64,512]{2,1,0:T(8,128)(2,1)S(1)} %get-tuple-element.17.refs_0_), channel_id=1, source_target_pairs={{0,8},{4,12},{8,0},{12,4},{1,9},{5,13},{9,1},{13,5},{2,10},{6,14},... | collective-permute-start | bytes 393224 | tf_op jit(solution)/shard_map/ppermute | solution.py:18
  57.6 12.1 %collective-permute-start.35 = (bf16[2,64,512]{2,1,0:T(8,128)(2,1)S(1)}, bf16[2,64,512]{2,1,0:T(8,128)(2,1)S(1)}, u32[]{:S(2)}, u32[]{:S(2)}) collective-permute-start(bf16[2,64,512]{2,1,0:T(8,128)(2,1)S(1)} %get-tuple-element.17.refs_0_), channel_id=1, source_target_pairs={{0,4},{4,8},{8,12},{12,0},{1,5},{5,9},{9,13},{13,1},{2,6},{6,10},{... | collective-permute-start | bytes 393224 | tf_op jit(solution)/shard_map/ppermute | solution.py:18
  59.0 12.7 %collective-permute-start.33 = (bf16[2,64,512]{2,1,0:T(8,128)(2,1)S(1)}, bf16[2,64,512]{2,1,0:T(8,128)(2,1)S(1)}, u32[]{:S(2)}, u32[]{:S(2)}) collective-permute-start(bf16[2,64,512]{2,1,0:T(8,128)(2,1)S(1)} %get-tuple-element.17.refs_0_), channel_id=1, source_target_pairs={{0,2},{1,3},{2,0},{3,1},{4,6},{5,7},{6,4},{7,5},{8,10},{9,11},{10,... | collective-permute-start | bytes 393224 | tf_op jit(solution)/shard_map/ppermute | solution.py:22
  61.1 11.4 %collective-permute-start.32 = (bf16[2,64,512]{2,1,0:T(8,128)(2,1)S(1)}, bf16[2,64,512]{2,1,0:T(8,128)(2,1)S(1)}, u32[]{:S(2)}, u32[]{:S(2)}) collective-permute-start(bf16[2,64,512]{2,1,0:T(8,128)(2,1)S(1)} %get-tuple-element.17.refs_0_), channel_id=1, source_target_pairs={{0,1},{1,0},{2,3},{3,2},{4,5},{5,4},{6,7},{7,6},{8,9},{9,8},{10,11... | collective-permute-start | bytes 393224 | tf_op jit(solution)/shard_map/ppermute | solution.py:22
  69.7 11.7 %collective-permute-start.28 = (bf16[2,192,256]{2,1,0:T(8,128)(2,1)S(1)}, bf16[2,192,256]{2,1,0:T(8,128)(2,1)S(1)}, u32[]{:S(2)}, u32[]{:S(2)}) collective-permute-start(bf16[2,192,256]{2,1,0:T(8,128)(2,1)S(1)} %get-tuple-element.9), channel_id=1, source_target_pairs={{0,12},{4,0},{8,4},{12,8},{1,13},{5,1},{9,5},{13,9},{2,14},{6,2},{... | collective-permute-start | bytes 589832 | tf_op jit(solution)/shard_map/ppermute | solution.py:18
  69.7 12.4 %collective-permute-start.26 = (bf16[2,192,256]{2,1,0:T(8,128)(2,1)S(1)}, bf16[2,192,256]{2,1,0:T(8,128)(2,1)S(1)}, u32[]{:S(2)}, u32[]{:S(2)}) collective-permute-start(bf16[2,192,256]{2,1,0:T(8,128)(2,1)S(1)} %get-tuple-element.11), channel_id=1, source_target_pairs={{0,4},{4,8},{8,12},{12,0},{1,5},{5,9},{9,13},{13,1},{2,6},{6,10},{... | collective-permute-start | bytes 589832 | tf_op jit(solution)/shard_map/ppermute | solution.py:18
  71.7 15.0 %collective-permute-start.27 = (bf16[2,192,256]{2,1,0:T(8,128)(2,1)S(1)}, bf16[2,192,256]{2,1,0:T(8,128)(2,1)S(1)}, u32[]{:S(2)}, u32[]{:S(2)}) collective-permute-start(bf16[2,192,256]{2,1,0:T(8,128)(2,1)S(1)} %get-tuple-element.12), channel_id=1, source_target_pairs={{0,8},{4,12},{8,0},{12,4},{1,9},{5,13},{9,1},{13,5},{2,10},{6,14},... | collective-permute-start | bytes 589832 | tf_op jit(solution)/shard_map/ppermute | solution.py:18
  71.7 15.7 %collective-permute-start.45 = (bf16[2,64,512]{2,1,0:T(8,128)(2,1)S(1)}, bf16[2,64,512]{2,1,0:T(8,128)(2,1)S(1)}, u32[]{:S(2)}, u32[]{:S(2)}) collective-permute-start(bf16[2,64,512]{2,1,0:T(8,128)(2,1)S(1)} %collective-permute-done.43.refs_12_), channel_id=1, source_target_pairs={{0,2},{1,3},{2,0},{3,1},{4,6},{5,7},{6,4},{7,5},{8,10},{9,11},{10,... | collective-permute-start | bytes 393224 | tf_op jit(solution)/shard_map/ppermute | solution.py:22
  72.5 16.3 %collective-permute-start.44 = (bf16[2,64,512]{2,1,0:T(8,128)(2,1)S(1)}, bf16[2,64,512]{2,1,0:T(8,128)(2,1)S(1)}, u32[]{:S(2)}, u32[]{:S(2)}) collective-permute-start(bf16[2,64,512]{2,1,0:T(8,128)(2,1)S(1)} %collective-permute-done.43.refs_12_), channel_id=1, source_target_pairs={{0,1},{1,0},{2,3},{3,2},{4,5},{5,4},{6,7},{7,6},{8,9},{9,8},{10,11... | collective-permute-start | bytes 393224 | tf_op jit(solution)/shard_map/ppermute | solution.py:22
  95.6 14.2 %collective-permute-start.31 = (bf16[16,2048]{1,0:T(8,128)(2,1)S(1)}, bf16[16,2048]{1,0:T(8,128)(2,1)S(1)}, u32[]{:S(2)}, u32[]{:S(2)}) collective-permute-start(bf16[16,2048]{1,0:T(8,128)(2,1)S(1)} %shard_map.92.a0), channel_id=1, source_target_pairs={{0,3},{1,2},{2,1},{3,0},{4,7},{5,6},{6,5},{7,4},{8,11},{9,10},{10,... | collective-permute-start | bytes 196616 | tf_op jit(solution)/shard_map/ppermute | solution.py:22
  96.4 13.4 %collective-permute-start.30 = (bf16[16,2048]{1,0:T(8,128)(2,1)S(1)}, bf16[16,2048]{1,0:T(8,128)(2,1)S(1)}, u32[]{:S(2)}, u32[]{:S(2)}) collective-permute-start(bf16[16,2048]{1,0:T(8,128)(2,1)S(1)} %shard_map.92.a0), channel_id=1, source_target_pairs={{0,2},{1,3},{2,0},{3,1},{4,6},{5,7},{6,4},{7,5},{8,10},{9,11},{10,... | collective-permute-start | bytes 196616 | tf_op jit(solution)/shard_map/ppermute | solution.py:22
  97.8 12.0 %collective-permute-start.29 = (bf16[16,2048]{1,0:T(8,128)(2,1)S(1)}, bf16[16,2048]{1,0:T(8,128)(2,1)S(1)}, u32[]{:S(2)}, u32[]{:S(2)}) collective-permute-start(bf16[16,2048]{1,0:T(8,128)(2,1)S(1)} %shard_map.92.a0), channel_id=1, source_target_pairs={{0,1},{1,0},{2,3},{3,2},{4,5},{5,4},{6,7},{7,6},{8,9},{9,8},{10,11... | collective-permute-start | bytes 196616 | tf_op jit(solution)/shard_map/ppermute | solution.py:22
  112.5 20.4 %collective-permute-start.47 = (f32[16,2048]{1,0:T(8,128)S(1)}, f32[16,2048]{1,0:T(8,128)S(1)}, u32[]{:S(2)}, u32[]{:S(2)}) collective-permute-start(f32[16,2048]{1,0:T(8,128)S(1)} %get-tuple-element.7), channel_id=1, source_target_pairs={{0,0},{1,4},{2,8},{3,12},{4,1},{5,5},{6,9},{7,13},{8,2},{9,6},{10,... | collective-permute-start | bytes 393224 | tf_op jit(solution)/shard_map/ppermute | solution.py:27
  120.8 12.1 %collective-permute-start.49 = (bf16[16,2048]{1,0:T(8,128)(2,1)S(1)}, bf16[16,2048]{1,0:T(8,128)(2,1)S(1)}, u32[]{:S(2)}, u32[]{:S(2)}) collective-permute-start(bf16[16,2048]{1,0:T(8,128)(2,1)S(1)} %get-tuple-element.25), channel_id=1, source_target_pairs={{0,2},{1,6},{2,10},{3,14},{4,3},{5,7},{6,11},{7,15},{8,0},{9,4},{1... | collective-permute-start | bytes 196616 | tf_op jit(solution)/shard_map/ppermute | solution.py:27
  (32 other events, 239.1 us)

commit v2 on v0

--- a/solution.py
+++ b/solution.py
@@ -1,9 +1,386 @@
+import functools
+
 import jax
 import jax.numpy as jnp
 from jax import lax
+from jax.experimental import pallas as pl
+from jax.experimental.pallas import tpu as pltpu
 from jax.sharding import PartitionSpec as P
 
 HD = 128
+F32 = jnp.float32
+BF16 = jnp.bfloat16
+SIDE = 4
+BLOCK = 256
+PACK_COST = 64
+MIB = 1 << 20
+
+
+def after(x, *earlier):
+    return lax.optimization_barrier((x, *earlier))[0]
+
+
+def along_tp(x, k):
+    return lax.ppermute(x, "tp", [(i, (i + k) % SIDE) for i in range(SIDE)])
+
+
+def across_dp(x, k):
+    return lax.ppermute(x, "dp", [(i, i ^ k) for i in range(SIDE)])
+
+
+def across_groups(x):
+    return lax.ppermute(x, "groups", [(0, 1), (1, 0)])
+
+
+def to_holder(x, m):
+    pairs = [(t * SIDE + d, d * SIDE + (t ^ m)) for t in range(SIDE) for d in range(SIDE)]
+    return lax.ppermute(x, ("tp", "dp"), pairs)
+
+
+def pack_kernel(*refs):
+    out_ref, at = refs[-1], 0
+    for ref in refs[:-1]:
+        out_ref[at : at + ref.shape[0]] = ref[...]
+        at += ref.shape[0]
+
+
+def pack(parts, cost=1):
+    spec = pl.BlockSpec(memory_space=pltpu.VMEM)
+    shape = (sum(part.shape[0] for part in parts), *parts[0].shape[1:])
+    return pl.pallas_call(
+        pack_kernel,
+        out_shape=jax.ShapeDtypeStruct(shape, parts[0].dtype),
+        in_specs=[spec] * len(parts),
+        out_specs=spec,
+        compiler_params=pltpu.CompilerParams(vmem_limit_bytes=4 * MIB),
+        cost_estimate=pl.CostEstimate(flops=0, bytes_accessed=cost * MIB, transcendentals=0),
+    )(*parts)
+
+
+def small_call(kernel, scalars, arrays, out_shape, vmem=8 * MIB):
+    spec = pl.BlockSpec(memory_space=pltpu.VMEM)
+    return pl.pallas_call(
+        kernel,
+        out_shape=out_shape,
+        in_specs=[pl.BlockSpec(memory_space=pltpu.SMEM)] + [spec] * len(arrays),
+        out_specs=jax.tree.map(lambda _: spec, out_shape),
+        compiler_params=pltpu.CompilerParams(vmem_limit_bytes=vmem),
+    )(scalars, *arrays)
+
+
+def first_kernel(y_ref, adapters_ref, tokens_ref, out_ref):
+    half = adapters_ref.shape[2]
+    width = out_ref.shape[1]
+    rows = tokens_ref.shape[0]
+    for f in range(4):
+        out_ref[f * half : (f + 1) * half] = adapters_ref[f, y_ref[0]]
+    for j in range(tokens_ref.shape[1] // width):
+        at = 4 * half + j * rows
+        out_ref[at : at + rows] = tokens_ref[:, j * width : (j + 1) * width]
+
+
+def sort_kernel(from_ref, *refs):
+    held, (q_ref, o_ref, across_ref, *sends) = refs[:SIDE], refs[SIDE:]
+    half = q_ref.shape[1]
+    others = SIDE - 1
+    for k in range(1, SIDE):
+        for f in range(2):
+            unit = held[k][f * half : (f + 1) * half]
+            q_ref[f * others + k - 1] = unit
+            across_ref[f * others + k - 1] = unit
+            o_ref[f * others + k - 1] = held[k][(2 + f) * half : (3 + f) * half]
+    slab = sends[0].shape[0]
+    for k in range(SIDE):
+        for j, ref in enumerate(held):
+
+            @pl.when(from_ref[k] == j)
+            def _(ref=ref, k=k):
+                for u in range(slab):
+                    unit = ref[(4 + u) * half : (5 + u) * half]
+                    if k < 2:
+                        sends[k][u] = unit
+                    else:
+                        across_ref[2 * others + (k - 2) * slab + u] = unit
+
+
+def split_kernel(heads_ref, tokens_ref, keys_ref, values_ref, w_hbm, *refs):
+    outs, (w_ref, kv_ref, sem) = refs[:SIDE], refs[SIDE:]
+    row_parts = row_copies(w_hbm, w_ref, sem)
+    for copy in row_parts:
+        copy.start()
+    cached = keys_ref.shape[0]
+    rows, width = kv_ref.shape
+    cols = outs[0].shape[1]
+    places = [pl.multiple_of(heads_ref[k] * cols, cols) for k in range(SIDE)]
+    for at, out in zip(places, outs):
+        out[:cached] = keys_ref[:, pl.ds(at, cols)]
+        out[cached : 2 * cached] = values_ref[:, pl.ds(at, cols)]
+    for i in range(0, w_ref.shape[0], BLOCK):
+        row_parts[i // BLOCK].wait()
+        lanes = slice(i, i + BLOCK)
+        term = jnp.dot(tokens_ref[:, lanes], w_ref[lanes, :], preferred_element_type=F32)
+        if i == 0:
+            kv_ref[...] = term
+        else:
+            kv_ref[...] += term
+    for at, out in zip(places, outs):
+        for part in range(2):
+            term = kv_ref[:, pl.ds(pl.multiple_of(part * (width // 2) + at, cols), cols)]
+            coarse = term.astype(BF16)
+            row = 2 * cached + part * rows
+            out[row : row + rows] = coarse
+            out[row + 2 * rows : row + 3 * rows] = (term - coarse.astype(F32)).astype(BF16)
+
+
+def split_call(heads, own, keys, values, weight, out_shape):
+    spec = pl.BlockSpec(memory_space=pltpu.VMEM)
+    return pl.pallas_call(
+        split_kernel,
+        out_shape=[out_shape] * SIDE,
+        in_specs=[pl.BlockSpec(memory_space=pltpu.SMEM)]
+        + [spec] * 3
+        + [pl.BlockSpec(memory_space=pl.ANY)],
+        out_specs=[spec] * SIDE,
+        scratch_shapes=[
+            pltpu.VMEM(weight.shape, BF16),
+            pltpu.VMEM((own.shape[0], weight.shape[1]), F32),
+            pltpu.SemaphoreType.DMA((weight.shape[0] // BLOCK,)),
+        ],
+        compiler_params=pltpu.CompilerParams(vmem_limit_bytes=16 * MIB),
+        cost_estimate=pl.CostEstimate(
+            flops=2 * own.size * weight.shape[1], bytes_accessed=4 * weight.size, transcendentals=0
+        ),
+    )(heads, own, keys, values, pltpu.with_memory_space_constraint(weight, pltpu.HBM))
+
+
+def corners_of(mine_far, other):
+    half = other.shape[0] // 2
+    return [across_dp(other[:half], 2), across_groups(mine_far[half : 2 * half])]
+
+
+def with_sibling(packed, corners):
+    near = [packed, *corners]
+    return near + [across_dp(x, 1) for x in near]
+
+
+def block_places(inverse, first, t, d):
+    source = lax.dynamic_slice_in_dim(inverse, first, SIDE, 0)
+    return (t - source // SIDE) % SIDE, (source % SIDE) ^ d
+
+
+def pick(slots_ref, parts, other_at, down_ref, up_ref, sem):
+    y = slots_ref[4 * SIDE]
+    half = down_ref.shape[0] // 2
+    cols = down_ref.shape[1] // SIDE
+    others = SIDE - 1
+
+    def copy(n, source, h):
+        dst = down_ref if n < SIDE else up_ref
+        at = pl.multiple_of(h * half, half)
+        lanes = pl.ds((n % SIDE) * cols, cols)
+        return pltpu.make_async_copy(source, dst.at[pl.ds(at, half), lanes], sem.at[2 * n + h])
+
+    for n in range(2 * SIDE):
+        factor = n // SIDE
+        row, across = slots_ref[n], slots_ref[2 * SIDE + n]
+        far = across >> 1
+        in_row = factor * others + row - 1
+        at_mine = jnp.where(row == 0, far * 4 + factor * 2 + y, 8 + far * 2 * others + in_row)
+        at_other = jnp.where(row == 0, far * 4 + factor * 2 + 1 - y, other_at + in_row)
+        corner = (far == 1) & (row > 0)
+        for side in range(2):
+            packed, *corners = parts[side * 3 : side * 3 + 3]
+            here = (across & 1) == side
+
+            @pl.when(here)
+            def _(packed=packed, at_mine=at_mine, n=n):
+                copy(n, packed.at[at_mine], y).start()
+
+            @pl.when(here & jnp.logical_not(corner))
+            def _(packed=packed, at_other=at_other, n=n):
+                copy(n, packed.at[at_other], 1 - y).start()
+
+            @pl.when(here & corner)
+            def _(source=corners[factor], row=row, n=n):
+                copy(n, source.at[row - 1], 1 - y).start()
+
+    for n in range(2 * SIDE):
+        for h in range(2):
+            copy(n, parts[0].at[0], h).wait()
+
+
+def merged_rows(w, down_ref, up_ref, lanes):
+    delta = lax.dot_general(
+        down_ref[:, lanes], up_ref[...], (((0,), (0,)), ((), ())), preferred_element_type=F32
+    )
+    return (w.astype(F32) + delta).astype(BF16)
+
+
+def row_copies(src, dst, sem):
+    return [
+        pltpu.make_async_copy(src.at[pl.ds(i, BLOCK)], dst.at[pl.ds(i, BLOCK)], sem.at[i // BLOCK])
+        for i in range(0, src.shape[0], BLOCK)
+    ]
+
+
+def place_rows(turn, pieces, x_ref):
+    rows = pieces[0].shape[0]
+    for m, piece in enumerate(pieces):
+        x_ref[pl.ds(pl.multiple_of((turn ^ m) * rows, rows), rows), :] = piece[...]
+
+
+def merge_dot_kernel(slots_ref, *refs):
+    parts = refs[:6]
+    w_hbm, own_ref, across_ref, out_ref, down_ref, up_ref, w_ref, x_ref, tokens_ref = refs[6:15]
+    sem, token_sem, row_sem = refs[15:]
+    slab, half, width = own_ref.shape
+    total = parts[3].shape[0]
+    at = 2 * (SIDE - 1)
+    sources = [
+        own_ref,
+        parts[3].at[pl.ds(total - slab, slab)],
+        across_ref.at[pl.ds(at, slab)],
+        parts[3].at[pl.ds(total - 2 * slab - at, slab)],
+    ]
+    copies = [
+        pltpu.make_async_copy(source, tokens_ref.at[pl.ds(k * slab, slab)], token_sem.at[k])
+        for k, source in enumerate(sources)
+    ]
+    row_parts = row_copies(w_hbm, w_ref, row_sem)
+    for copy in copies + row_parts:
+        copy.start()
+    pick(slots_ref, parts, total - slab - at, down_ref, up_ref, sem)
+    for copy in copies:
+        copy.wait()
+    rows = slab * half * width // x_ref.shape[1]
+    for k in range(SIDE):
+        for j in range(x_ref.shape[1] // width):
+            u, row = divmod(j * rows, half)
+            term = tokens_ref[k * slab + u, row : row + rows, :]
+            x_ref[k * rows : (k + 1) * rows, j * width : (j + 1) * width] = term
+    for i in range(0, w_ref.shape[0], BLOCK):
+        row_parts[i // BLOCK].wait()
+        lanes = slice(i, i + BLOCK)
+        merged = merged_rows(w_ref[lanes, :], down_ref, up_ref, lanes)
+        term = jnp.dot(x_ref[:, lanes], merged, preferred_element_type=F32)
+        if i == 0:
+            out_ref[...] = term
+        else:
+            out_ref[...] += term
+
+
+def merge_kernel(slots_ref, *refs):
+    w_ref, out_ref, down_ref, up_ref, sem, row_sem = refs[6:]
+    copies = row_copies(w_ref, out_ref, row_sem)
+    for copy in copies:
+        copy.start()
+    pick(slots_ref, refs[:6], refs[0].shape[0] - 2 * (SIDE - 1), down_ref, up_ref, sem)
+    for i in range(0, w_ref.shape[0], BLOCK):
+        copies[i // BLOCK].wait()
+        lanes = slice(i, i + BLOCK)
+        out_ref[lanes, :] = merged_rows(out_ref[lanes, :], down_ref, up_ref, lanes)
+
+
+def merge_call(kernel, slots, parts, weight, pieces, out_shape, sems, rank, cost):
+    depth, width = weight.shape
+    piece_cols = parts[0].shape[-1]
+    vmem_spec = pl.BlockSpec(memory_space=pltpu.VMEM)
+    scratch = [pltpu.VMEM((rank, SIDE * piece_cols), BF16)] * 2
+    if pieces:
+        scratch.append(pltpu.VMEM(weight.shape, BF16))
+        scratch.append(pltpu.VMEM((out_shape.shape[0], depth), BF16))
+        slab, *unit = pieces[0].shape
+        scratch.append(pltpu.VMEM((SIDE * slab, *unit), BF16))
+    scratch += [pltpu.SemaphoreType.DMA((count,)) for count in sems]
+    return pl.pallas_call(
+        kernel,
+        out_shape=out_shape,
+        in_specs=[pl.BlockSpec(memory_space=pltpu.SMEM)]
+        + [pl.BlockSpec(memory_space=pl.ANY)] * len(parts)
+        + [pl.BlockSpec(memory_space=pl.ANY)]
+        + [vmem_spec] * len(pieces),
+        out_specs=vmem_spec,
+        scratch_shapes=scratch,
+        compiler_params=pltpu.CompilerParams(vmem_limit_bytes=16 * MIB),
+        cost_estimate=pl.CostEstimate(flops=0, bytes_accessed=cost * MIB, transcendentals=0),
+    )(slots, *parts, weight, *pieces)
+
+
+def attention_kernel(seqs, spots_ref, qa_ref, qb_ref, c0, c1, c3, keys_ref, rest_ref, out_ref):
+    scale = HD ** (-0.5)
+    rows = qa_ref.shape[0]
+    kv_dev = c0.shape[1] // HD
+    group = qa_ref.shape[1] // HD // kv_dev
+    span = (c0.shape[0] - 4 * rows) // (2 * seqs)
+    cached = seqs * span
+    queries = (qa_ref[...] + qb_ref[...]).astype(BF16)
+
+    row_seq = lax.broadcasted_iota(jnp.int32, (rows, cached), 0) % seqs
+    column = lax.broadcasted_iota(jnp.int32, (rows, cached), 1)
+    biases = []
+    for k in range(SIDE):
+        valid = column < 0
+        for b in range(seqs):
+            left = jnp.clip(spots_ref[SIDE + b] - spots_ref[k] * span, 0, span)
+            inside = (column >= b * span) & (column < b * span + left)
+            valid |= inside & (row_seq == b)
+        biases.append(jnp.where(valid, 0.0, -1e30))
+    row = lax.broadcasted_iota(jnp.int32, (rows, rows), 0)
+    earlier = lax.broadcasted_iota(jnp.int32, (rows, rows), 1)
+    causal = (earlier // seqs <= row // seqs) & (earlier % seqs == row % seqs)
+    fresh_bias = jnp.where(causal, 0.0, -1e30)
+
+    def fresh_part(part):
+        terms = []
+        for c in (c0, c1, rest_ref, c3):
+            at = c.shape[0] - 4 * rows + part * rows
+            terms.append(c[at : at + rows].astype(F32))
+            terms.append(c[at + 2 * rows : at + 3 * rows].astype(F32))
+        return sum(terms).astype(BF16)
+
+    fresh_keys, fresh_values = fresh_part(0), fresh_part(1)
+    contract_last = (((1,), (1,)), ((), ()))
+
+    def scores_of(q, keys, bias):
+        s = lax.dot_general(q, keys, contract_last, preferred_element_type=F32) * scale
+        s = s.reshape(group, rows, s.shape[1]) + bias[None]
+        return s.reshape(group * rows, s.shape[2])
+
+    def weighted(weights, values):
+        coarse = weights.astype(BF16)
+        rest = (weights - coarse.astype(F32)).astype(BF16)
+        return jnp.dot(coarse, values, preferred_element_type=F32) + jnp.dot(
+            rest, values, preferred_element_type=F32
+        )
+
+    for h in range(kv_dev):
+        lanes = slice(h * HD, (h + 1) * HD)
+        q = jnp.concatenate(
+            [queries[:, (h * group + g) * HD : (h * group + g + 1) * HD] for g in range(group)], axis=0
+        )
+        scores = [scores_of(q, c[:cached, lanes], biases[k]) for k, c in enumerate((c0, c1, keys_ref, c3))]
+        scores.append(scores_of(q, fresh_keys[:, lanes], fresh_bias))
+        values = [c[cached : 2 * cached, lanes] for c in (c0, c1)]
+        values += [rest_ref[:cached, lanes], c3[cached : 2 * cached, lanes]]
+        values.append(fresh_values[:, lanes])
+        top = functools.reduce(jnp.maximum, [jnp.max(s, axis=1, keepdims=True) for s in scores])
+        weights = [jnp.exp(s - top) for s in scores]
+        total = sum(jnp.sum(w, axis=1, keepdims=True) for w in weights)
+        summed = sum(weighted(w, v) for w, v in zip(weights, values))
+        attn = (summed / total).astype(BF16)
+        for g in range(group):
+            out_ref[:, (h * group + g) * HD : (h * group + g + 1) * HD] = attn[g * rows : (g + 1) * rows]
+
+
+def out_kernel(turn_ref, a0, a1, a2, a3, w_ref, first_ref, rest_ref, x_ref):
+    rows = a0.shape[0]
+    place_rows(turn_ref[0], (a0, a1, a2, a3), x_ref)
+    for j in range(0, w_ref.shape[1], 2 * BLOCK):
+        lanes = slice(j, j + 2 * BLOCK)
+        total = jnp.dot(x_ref[...], w_ref[:, lanes], preferred_element_type=F32)
+        first_ref[:, lanes] = total[:rows]
+        for m in range(1, SIDE):
+            rest_ref[m - 1, :, lanes] = total[m * rows : (m + 1) * rows].astype(BF16)
 
 
 def joined_2(array, axis, combine):
@@ -36,7 +413,7 @@
     return chosen.reshape(stacked.shape[1], count)
 
 
-def on_device(
+def general(
     tokens, lengths, cache_keys, cache_values, q_weight, kv_weight, o_weight, adapters, layout
 ):
     tp_index = lax.axis_index("tp")
@@ -151,9 +528,150 @@
     return mixed
 
 
+def on_device(
+    tokens, lengths, cache_keys, cache_values, q_weight, kv_weight, o_weight, adapters, layout
+):
+    t = lax.axis_index("tp")
+    d = lax.axis_index("dp")
+    steps, seq_dev, feat_dev = tokens.shape
+    rows = steps * seq_dev
+    span = cache_keys.shape[1]
+    kv_cols = cache_keys.shape[2] // SIDE
+    shards = layout.shape[0]
+    numbers = jnp.arange(shards, dtype=jnp.int32)
+    inverse = jnp.sum(jnp.where(layout[None, :] == numbers[:, None], numbers[None, :], 0), axis=1)
+    row_d, across_d = block_places(inverse, d * SIDE, t, d)
+    row_t, across_t = block_places(inverse, t * SIDE, t, d)
+    y = lax.axis_index("groups")
+    turn = t ^ d
+    q_slots = jnp.concatenate([row_d, row_t, across_d, across_t, jnp.stack([y, turn])])
+    o_slots = jnp.concatenate([row_t, row_d, across_t, across_d, jnp.stack([y, turn])])
+    own = tokens.reshape(rows, feat_dev)
+    rank = adapters.shape[1]
+    halves = adapters.reshape(4, 2, rank // 2, adapters.shape[2])
+
+    def shaped(*shape):
+        return jax.ShapeDtypeStruct(shape, BF16)
+
+    width = adapters.shape[2]
+    slab = rows * feat_dev // width
+    payload = small_call(first_kernel, y.reshape(1), [halves, own], shaped(2 * rank + slab, width))
+    held = [payload] + [along_tp(payload, k) for k in range(1, SIDE)]
+    halves_far = across_dp(after(halves, payload), 2)
+
+    ks = jnp.arange(SIDE, dtype=jnp.int32)
+    froms = (t - (d ^ ks)) % SIDE
+    spots = jnp.concatenate([(t - ks) % SIDE, lengths])
+    cached = seq_dev * span
+    cache_send = split_call(
+        (t + ks) % SIDE,
+        own,
+        cache_keys.reshape(cached, -1),
+        cache_values.reshape(cached, -1),
+        kv_weight,
+        shaped(2 * cached + 4 * rows, kv_cols),
+    )
+
+    held = after(held, *cache_send, q_slots, o_slots, spots, froms)
+    unit = (rank // 2, width)
+    slab = slab // unit[0]
+    others = 2 * (SIDE - 1)
+    q_mine, o_mine, across, own_rows, near_rows = small_call(
+        sort_kernel,
+        froms,
+        held,
+        [shaped(n, *unit) for n in (others, others, others + 2 * slab, slab, slab)],
+    )
+    q_far = across_dp(across, 2)
+    q_other = across_groups(q_mine)
+    next_send, last_send = after([cache_send[1], cache_send[3]], q_mine)
+    from_next, from_last = along_tp(next_send, 1), along_tp(last_send, 3)
+    q_far, q_other, from_next, from_last = lax.optimization_barrier(
+        (q_far, q_other, from_next, from_last)
+    )
+    middle_keys = along_tp(after(cache_send[2][:cached], q_far, q_other), 2)
+    own_rows, middle_keys = lax.optimization_barrier((own_rows, middle_keys))
+    q_corners = corners_of(q_far, q_other)
+    halves = halves.reshape(2, 4, *unit)
+    halves_far = halves_far.reshape(2, 4, *unit)
+    q_packed = pack([halves[0], halves_far[0], q_mine, q_far, q_other, near_rows], PACK_COST)
+    q_parts = with_sibling(q_packed, q_corners)
+    o_mine = after(o_mine, *q_corners)
+    o_far, o_other = across_dp(o_mine, 2), across_groups(o_mine)
+
+    q_part = merge_call(
+        merge_dot_kernel,
+        q_slots,
+        q_parts,
+        pltpu.with_memory_space_constraint(q_weight, pltpu.HBM),
+        [own_rows, q_far],
+        jax.ShapeDtypeStruct((SIDE * rows, q_weight.shape[1]), F32),
+        [4 * SIDE, SIDE, q_weight.shape[0] // BLOCK],
+        rank,
+        0,
+    )
+    near = across_dp(jnp.concatenate([q_part[rows : 2 * rows], q_part[3 * rows :]]), 1)
+    middle_rest = along_tp(after(cache_send[2][cached:], q_part), 2)
+    caches = [cache_send[0], from_next, from_last, middle_keys, middle_rest]
+    q_near_sum = q_part[:rows] + near[:rows]
+    q_far_sum = across_dp(q_part[2 * rows : 3 * rows] + near[rows:], 2)
+
+    o_corners = corners_of(*after((o_far, o_other), near))
+    o_packed = pack([halves[1], halves_far[1], o_mine, o_far, o_other])
+    o_parts = with_sibling(o_packed, o_corners)
+
+    vmem_spec = pl.BlockSpec(memory_space=pltpu.VMEM)
+    attn = pl.pallas_call(
+        functools.partial(attention_kernel, seq_dev),
+        out_shape=jax.ShapeDtypeStruct((rows, q_weight.shape[1]), BF16),
+        in_specs=[pl.BlockSpec(memory_space=pltpu.SMEM)] + [vmem_spec] * 7,
+        out_specs=vmem_spec,
+        compiler_params=pltpu.CompilerParams(vmem_limit_bytes=8 * MIB),
+    )(spots, q_near_sum, q_far_sum, *caches)
+
+    o_merged = merge_call(
+        merge_kernel,
+        o_slots,
+        o_parts,
+        pltpu.with_memory_space_constraint(o_weight, pltpu.HBM),
+        [],
+        pltpu.VMEM(o_weight.shape, BF16),
+        [4 * SIDE, o_weight.shape[0] // BLOCK],
+        rank,
+        16,
+    )
+    attn_rows = [attn] + [across_dp(attn, k) for k in range(1, SIDE)]
+    width = o_weight.shape[1]
+    first, rest = pl.pallas_call(
+        out_kernel,
+        out_shape=(
+            jax.ShapeDtypeStruct((rows, width), F32),
+            jax.ShapeDtypeStruct((SIDE - 1, rows, width), BF16),
+        ),
+        in_specs=[pl.BlockSpec(memory_space=pltpu.SMEM)] + [vmem_spec] * (SIDE + 1),
+        out_specs=(vmem_spec, vmem_spec),
+        scratch_shapes=[pltpu.VMEM((SIDE * rows, o_weight.shape[0]), BF16)],
+        compiler_params=pltpu.CompilerParams(vmem_limit_bytes=16 * MIB),
+    )(turn.reshape(1), *attn_rows, o_merged)
+    mixed = to_holder(first, 0)
+    for m in range(1, SIDE):
+        mixed = mixed + to_holder(rest[m - 1], m).astype(F32)
+    return mixed.astype(BF16).reshape(steps, seq_dev, width)
+
+
 def solution(mesh):
+    def fits(layout, cache_keys):
+        sides = mesh.shape["tp"] == SIDE and mesh.shape["dp"] == SIDE and mesh.shape["groups"] == 2
+        return sides and layout.shape[0] == SIDE * SIDE
+
+    def run(tokens, lengths, cache_keys, cache_values, q_weight, kv_weight, o_weight, adapters, layout):
+        body = on_device if fits(layout, cache_keys) else general
+        return body(
+            tokens, lengths, cache_keys, cache_values, q_weight, kv_weight, o_weight, adapters, layout
+        )
+
     return jax.shard_map(
-        on_device,
+        run,
         mesh=mesh,
         in_specs=(
             P(None, ("groups", "dp"), "tp"),

time: 473 us -> 100 us (0.21)
  waiting for transfers between devices: 243 us -> 38.4 us
  blocking collectives: 157 us -> 0 us
  matrix products: 34.9 us -> 0 us
  starting transfers between devices: 0.08 us -> 33.1 us
  Pallas kernels: 0 us -> 21.7 us
  between operations: 13.6 us -> 0.25 us
  local copies, waits for them, and re-layouts: 17.8 us -> 4.76 us
  other arithmetic: 6.45 us -> 1.71 us
    all_gather x3 -> x0, waiting for transfers between devices: 242 us -> none  [the longest x1 185 us: on_device(): lax.all_gather(q_merged, 'dp', axis=0, tiled=True)]
    unnamed x1 -> x0, blocking collectives: 71.8 us -> none
    all_gather x5 -> x0, blocking collectives: 60.2 us -> none  [the longest x2 26.4 us: joined_2(): everything = jax.tree.map(lambda part: lax.all_gather(part, axis), array)]
    ppermute x0 -> x31, waiting for transfers between devices: none -> 38.4 us  [the longest x7 16.2 us: along_tp(): return lax.ppermute(x, 'tp', [(i, (i + k) % SIDE) for i in range(SIDE)])]
    dot_general x8 -> x0, matrix products: 34.9 us -> none  [the longest x1 12.8 us: on_device(): jnp.dot(flat_tokens, lax.all_gather(q_merged, 'dp', axis=0, tiled=True),...]
    ppermute x0 -> x31, starting transfers between devices: none -> 33.1 us  [the longest x7 11.5 us: along_tp(): return lax.ppermute(x, 'tp', [(i, (i + k) % SIDE) for i in range(SIDE)])]
    psum x1 -> x0, blocking collectives: 25.2 us -> none  [on_device(): new_kv = lax.psum(kv_part, 'tp').astype(jnp.bfloat16)]
    pallas_call x0 -> x9, Pallas kernels: none -> 21.7 us  [the longest x2 12.1 us: merge_call(): pl.pallas_call(kernel, out_shape=out_shape, in_specs=[pl.BlockSpec(memory...]
  transfers between devices with their start and end apart: 3 -> 31, of which waited for: 2 -> 13; matrix products, arithmetic and copies ran while one was open for 2% -> 3% of each run, Pallas kernels for 0% -> 19%
where the time goes in v2:
time: 100 us
  waiting for transfers between devices  38.4 us (38%)
  starting transfers between devices  33.1 us (33%)
  Pallas kernels  21.7 us (22%)
  local copies, waits for them, and re-layouts  4.76 us (5%)
  other arithmetic  1.71 us (2%)
    ppermute x7, waiting for transfers between devices, along_tp(): return lax.ppermute(x, 'tp', [(i, (i + k) % SIDE) for i in range(SIDE)])  16.2 us
    ppermute x4, waiting for transfers between devices, to_holder(): return lax.ppermute(x, ('tp', 'dp'), pairs)  13 us
    pallas_call x2, Pallas kernels, merge_call(): pl.pallas_call(kernel, out_shape=out_shape, in_specs=[pl.BlockSpec(memory...  12.1 us
    ppermute x7, starting transfers between devices, along_tp(): return lax.ppermute(x, 'tp', [(i, (i + k) % SIDE) for i in range(SIDE)])  11.5 us
    ppermute x16, starting transfers between devices, across_dp(): return lax.ppermute(x, 'dp', [(i, i ^ k) for i in range(SIDE)])  10.4 us
    ppermute x4, starting transfers between devices, to_holder(): return lax.ppermute(x, ('tp', 'dp'), pairs)  6.17 us
    ppermute x16, waiting for transfers between devices, across_dp(): return lax.ppermute(x, 'dp', [(i, i ^ k) for i in range(SIDE)])  5.29 us
    ppermute x4, starting transfers between devices, across_groups(): return lax.ppermute(x, 'groups', [(0, 1), (1, 0)])  5.05 us
  transfers between devices with their start and end apart: 31, of which 13 were waited for; matrix products, arithmetic and copies ran while one was open for 3% of the time, Pallas kernels for 19%

profile of v2, /device:TPU:0, one launch (start us, length us, event | category | flops | bytes accessed | tf_op | source)
XLA Modules:
  0.0 100.0 jit_solution(9573726603707566412)
XLA Ops:
  1.8 5.1 %collective-permute-start.3 = (bf16[192,512]{1,0:T(8,128)(2,1)S(1)}, bf16[192,512]{1,0:T(8,128)(2,1)S(1)}, u32[]{:S(2)}, u32[]{:S(2)}) collective-permute-start(bf16[192,512]{1,0:T(8,128)(2,1)S(1)} %shard_map.91.refs_0_), channel_id=1, source_target_pairs={{0,12},{4,0},{8,4},{12,8},{1,13},{5,1},{9,5},{13,9},{2,14},{6,2},{... | collective-permute-start | bytes 589832 | tf_op jit(solution)/shard_map/ppermute | solution.py:24
  13.2 4.3 %shard_map.92 = (bf16[448,256]{1,0:T(8,128)(2,1)S(1)}, bf16[448,256]{1,0:T(8,128)(2,1)S(1)}, bf16[448,256]{1,0:T(8,128)(2,1)S(1)}, bf16[448,256]{1,0:T(8,128)(2,1)S(1)}) custom-call(s32[4]{0:T(128)S(1)} %get-tuple-element.78.heads_ref, bf16[16,2048]{1,0:T(8,128)(2,1)S(1)} %reshape.31.tokens_ref, bf16[192,1024]{1,0:T(8,128)(2,1)S(1)} %bitcast.19, ...), custom_call_target="tpu_custom_call" | custom-call | flops 134217728 | bytes 16777216 | tf_op jit(solution)/shard_map/pallas_call | solution.py:137
  17.5 6.1 %collective-permute-done.2.refs_2_ = bf16[192,512]{1,0:T(8,128)(2,1)S(1)} collective-permute-done((bf16[192,512]{1,0:T(8,128)(2,1)S(1)}, bf16[192,512]{1,0:T(8,128)(2,1)S(1)}, u32[]{:S(2)}, u32[]{:S(2)}) %collective-permute-start.2) | collective-permute-done | bytes 196640 | tf_op jit(solution)/shard_map/ppermute | solution.py:24
  24.3 1.6 %collective-permute-start.4 = (bf16[10,32,512]{2,1,0:T(8,128)(2,1)S(1)}, bf16[10,32,512]{2,1,0:T(8,128)(2,1)S(1)}, u32[]{:S(2)}, u32[]{:S(2)}) collective-permute-start(bf16[10,32,512]{2,1,0:T(8,128)(2,1)S(1)} %get-tuple-element.44), channel_id=1, source_target_pairs={{0,2},{1,3},{2,0},{3,1},{4,6},{5,7},{6,4},{7,5},{8,10},{9,11},{10,... | collective-permute-start | bytes 983048 | tf_op jit(solution)/shard_map/ppermute | solution.py:28
  26.9 1.6 %collective-permute-start.5 = (bf16[6,32,512]{2,1,0:T(8,128)(2,1)S(1)}, bf16[6,32,512]{2,1,0:T(8,128)(2,1)S(1)}, u32[]{:S(2)}, u32[]{:S(2)}) collective-permute-start(bf16[6,32,512]{2,1,0:T(8,128)(2,1)S(1)} %get-tuple-element.43.refs_2_), channel_id=1, source_target_pairs={{0,16},{16,0},{1,17},{17,1},{2,18},{18,2},{3,19},{19,3},{4,20},{20... | collective-permute-start | bytes 589832 | tf_op jit(solution)/shard_map/ppermute | solution.py:32
  29.3 2.9 %collective-permute-start.7 = (bf16[448,256]{1,0:T(8,128)(2,1)S(1)}, bf16[448,256]{1,0:T(8,128)(2,1)S(1)}, u32[]{:S(2)}, u32[]{:S(2)}) collective-permute-start(bf16[448,256]{1,0:T(8,128)(2,1)S(1)} %get-tuple-element.46), channel_id=1, source_target_pairs={{0,12},{4,0},{8,4},{12,8},{1,13},{5,1},{9,5},{13,9},{2,14},{6,2},{... | collective-permute-start | bytes 688136 | tf_op jit(solution)/shard_map/ppermute | solution.py:24
  32.6 6.2 %collective-permute-done.6.c1 = bf16[448,256]{1,0:T(8,128)(2,1)S(1)} collective-permute-done((bf16[448,256]{1,0:T(8,128)(2,1)S(1)}, bf16[448,256]{1,0:T(8,128)(2,1)S(1)}, u32[]{:S(2)}, u32[]{:S(2)}) %collective-permute-start.6) | collective-permute-done | bytes 229408 | tf_op jit(solution)/shard_map/ppermute | solution.py:24
  38.8 2.1 %collective-permute-done.7.c3 = bf16[448,256]{1,0:T(8,128)(2,1)S(1)} collective-permute-done((bf16[448,256]{1,0:T(8,128)(2,1)S(1)}, bf16[448,256]{1,0:T(8,128)(2,1)S(1)}, u32[]{:S(2)}, u32[]{:S(2)}) %collective-permute-start.7) | collective-permute-done | bytes 229408 | tf_op jit(solution)/shard_map/ppermute | solution.py:24
  42.3 1.5 %collective-permute-start.13 = (bf16[192,256]{1,0:T(8,128)(2,1)S(1)}, bf16[192,256]{1,0:T(8,128)(2,1)S(1)}, u32[]{:S(2)}, u32[]{:S(2)}) collective-permute-start(bf16[192,256]{1,0:T(8,128)(2,1)S(1)} %slice.65), channel_id=1, source_target_pairs={{0,8},{4,12},{8,0},{12,4},{1,9},{5,13},{9,1},{13,5},{2,10},{6,14},... | collective-permute-start | bytes 294920 | tf_op jit(solution)/shard_map/ppermute | solution.py:24
  43.8 2.5 %collective-permute-done.9.refs_2_ = bf16[3,32,512]{2,1,0:T(8,128)(2,1)S(1)} collective-permute-done((bf16[3,32,512]{2,1,0:T(8,128)(2,1)S(1)}, bf16[3,32,512]{2,1,0:T(8,128)(2,1)S(1)}, u32[]{:S(2)}, u32[]{:S(2)}) %collective-permute-start.9) | collective-permute-done | bytes 98336 | tf_op jit(solution)/shard_map/ppermute | solution.py:32
  48.1 1.8 %collective-permute-done.13.keys_ref = bf16[192,256]{1,0:T(8,128)(2,1)S(1)} collective-permute-done((bf16[192,256]{1,0:T(8,128)(2,1)S(1)}, bf16[192,256]{1,0:T(8,128)(2,1)S(1)}, u32[]{:S(2)}, u32[]{:S(2)}) %collective-permute-start.13) | collective-permute-done | bytes 98336 | tf_op jit(solution)/shard_map/ppermute | solution.py:24
  51.5 6.5 %shard_map.95 = f32[64,2048]{1,0:T(8,128)S(1)} custom-call(s32[18]{0:T(128)S(1)} %concatenate.13.slots_ref, bf16[32,32,512]{2,1,0:T(8,128)(2,1)S(1)} %shard_map.94.refs_0_, bf16[3,32,512]{2,1,0:T(8,128)(2,1)S(1)} %collective-permute-done.8.refs_1_, bf16[3,32,512]{2,1,0:T(8,128)(2,1)S(1)} %collective-permute-done.9.refs_2_, ...), custom_call_target="tpu_custom_call" | custom-call | tf_op jit(solution)/shard_map/pallas_call | solution.py:295
  59.6 1.6 %collective-permute-start.23 = (bf16[3,32,512]{2,1,0:T(8,128)(2,1)S(1)}, bf16[3,32,512]{2,1,0:T(8,128)(2,1)S(1)}, u32[]{:S(2)}, u32[]{:S(2)}) collective-permute-start(bf16[3,32,512]{2,1,0:T(8,128)(2,1)S(1)} %slice.76), channel_id=1, source_target_pairs={{0,16},{16,0},{1,17},{17,1},{2,18},{18,2},{3,19},{19,3},{4,20},{20... | collective-permute-start | bytes 294920 | tf_op jit(solution)/shard_map/ppermute | solution.py:32
  61.9 1.6 %collective-permute-start.22 = (bf16[3,32,512]{2,1,0:T(8,128)(2,1)S(1)}, bf16[3,32,512]{2,1,0:T(8,128)(2,1)S(1)}, u32[]{:S(2)}, u32[]{:S(2)}) collective-permute-start(bf16[3,32,512]{2,1,0:T(8,128)(2,1)S(1)} %slice.75), channel_id=1, source_target_pairs={{0,2},{1,3},{2,0},{3,1},{4,6},{5,7},{6,4},{7,5},{8,10},{9,11},{10,... | collective-permute-start | bytes 294920 | tf_op jit(solution)/shard_map/ppermute | solution.py:28
  64.5 4.2 %collective-permute-done.22.refs_1_ = bf16[3,32,512]{2,1,0:T(8,128)(2,1)S(1)} collective-permute-done((bf16[3,32,512]{2,1,0:T(8,128)(2,1)S(1)}, bf16[3,32,512]{2,1,0:T(8,128)(2,1)S(1)}, u32[]{:S(2)}, u32[]{:S(2)}) %collective-permute-start.22) | collective-permute-done | bytes 98336 | tf_op jit(solution)/shard_map/ppermute | solution.py:28
  68.7 1.9 %shard_map.96.a0 = bf16[16,2048]{1,0:T(8,128)(2,1)S(1)} custom-call(s32[8]{0:T(128)S(1)} %pad_add_fusion.spots_ref, f32[16,2048]{1,0:T(8,128)S(1)} %get-tuple-element.64.qa_ref, f32[16,2048]{1,0:T(8,128)S(1)} %collective-permute-done.15.qb_ref, bf16[448,256]{1,0:T(8,128)(2,1)S(1)} %get-tuple-element.35.c0, bf16[448,256]{1,0:T(8,128)(2,1)S(1)} %collective-permute-done.6.c1, ...), custom_call_target="tpu_custom_call" | custom-call | tf_op jit(solution)/shard_map/pallas_call | solution.py:624
  71.3 1.5 %collective-permute-start.18 = (bf16[16,2048]{1,0:T(8,128)(2,1)S(1)}, bf16[16,2048]{1,0:T(8,128)(2,1)S(1)}, u32[]{:S(2)}, u32[]{:S(2)}) collective-permute-start(bf16[16,2048]{1,0:T(8,128)(2,1)S(1)} %shard_map.96.a0), channel_id=1, source_target_pairs={{0,2},{1,3},{2,0},{3,1},{4,6},{5,7},{6,4},{7,5},{8,10},{9,11},{10,... | collective-permute-start | bytes 196616 | tf_op jit(solution)/shard_map/ppermute | solution.py:28
  72.8 5.6 %shard_map.98.w_ref = bf16[2048,2048]{1,0:T(8,128)(2,1)S(1)} custom-call(s32[18]{0:T(128)S(1)} %concatenate.14.slots_ref, bf16[26,32,512]{2,1,0:T(8,128)(2,1)S(1)} %shard_map.97.refs_0_, bf16[3,32,512]{2,1,0:T(8,128)(2,1)S(1)} %collective-permute-done.22.refs_1_, bf16[3,32,512]{2,1,0:T(8,128)(2,1)S(1)} %collective-permute-done.23.refs_2_, ...), custom_call_target="tpu_custom_call" | custom-call | bytes 16777216 | tf_op jit(solution)/shard_map/pallas_call | solution.py:295
  78.5 1.6 %shard_map.99 = (f32[16,2048]{1,0:T(8,128)S(1)}, bf16[3,16,2048]{2,1,0:T(8,128)(2,1)S(1)}) custom-call(s32[1]{0:T(128)} %bitcast.turn_ref, bf16[16,2048]{1,0:T(8,128)(2,1)S(1)} %shard_map.96.a0, bf16[16,2048]{1,0:T(8,128)(2,1)S(1)} %collective-permute-done.17.a1, bf16[16,2048]{1,0:T(8,128)(2,1)S(1)} %collective-permute-done.18.a2, ...), custom_call_target="tpu_custom_call" | custom-call | tf_op jit(solution)/shard_map/pallas_call | solution.py:645
  80.8 2.3 %collective-permute-start.28 = (bf16[16,2048]{1,0:T(8,128)(2,1)S(1)}, bf16[16,2048]{1,0:T(8,128)(2,1)S(1)}, u32[]{:S(2)}, u32[]{:S(2)}) collective-permute-start(bf16[16,2048]{1,0:T(8,128)(2,1)S(1)} %get-tuple-element.71), channel_id=1, source_target_pairs={{0,1},{1,5},{2,9},{3,13},{4,0},{5,4},{6,8},{7,12},{8,3},{9,7},{10,... | collective-permute-start | bytes 196616 | tf_op jit(solution)/shard_map/ppermute | solution.py:37
  83.1 3.2 %collective-permute-start.30 = (bf16[16,2048]{1,0:T(8,128)(2,1)S(1)}, bf16[16,2048]{1,0:T(8,128)(2,1)S(1)}, u32[]{:S(2)}, u32[]{:S(2)}) collective-permute-start(bf16[16,2048]{1,0:T(8,128)(2,1)S(1)} %get-tuple-element.72), channel_id=1, source_target_pairs={{0,3},{1,7},{2,11},{3,15},{4,2},{5,6},{6,10},{7,14},{8,1},{9,5},{1... | collective-permute-start | bytes 196616 | tf_op jit(solution)/shard_map/ppermute | solution.py:37
  86.3 1.7 %collective-permute-done.28 = bf16[16,2048]{1,0:T(8,128)(2,1)S(1)} collective-permute-done((bf16[16,2048]{1,0:T(8,128)(2,1)S(1)}, bf16[16,2048]{1,0:T(8,128)(2,1)S(1)}, u32[]{:S(2)}, u32[]{:S(2)}) %collective-permute-start.28) | collective-permute-done | bytes 65568 | tf_op jit(solution)/shard_map/ppermute | solution.py:37
  88.0 4.6 %collective-permute-done.30 = bf16[16,2048]{1,0:T(8,128)(2,1)S(1)} collective-permute-done((bf16[16,2048]{1,0:T(8,128)(2,1)S(1)}, bf16[16,2048]{1,0:T(8,128)(2,1)S(1)}, u32[]{:S(2)}, u32[]{:S(2)}) %collective-permute-start.30) | collective-permute-done | bytes 65568 | tf_op jit(solution)/shard_map/ppermute | solution.py:37
  92.7 6.6 %collective-permute-done.29 = bf16[16,2048]{1,0:T(8,128)(2,1)S(1)} collective-permute-done((bf16[16,2048]{1,0:T(8,128)(2,1)S(1)}, bf16[16,2048]{1,0:T(8,128)(2,1)S(1)}, u32[]{:S(2)}, u32[]{:S(2)}) %collective-permute-start.29) | collective-permute-done | bytes 65568 | tf_op jit(solution)/shard_map/ppermute | solution.py:37
  (72 shorter events, 21.1 us)
Async XLA Ops:
  1.8 15.7 %collective-permute-start.3 = (bf16[192,512]{1,0:T(8,128)(2,1)S(1)}, bf16[192,512]{1,0:T(8,128)(2,1)S(1)}, u32[]{:S(2)}, u32[]{:S(2)}) collective-permute-start(bf16[192,512]{1,0:T(8,128)(2,1)S(1)} %shard_map.91.refs_0_), channel_id=1, source_target_pairs={{0,12},{4,0},{8,4},{12,8},{1,13},{5,1},{9,5},{13,9},{2,14},{6,2},{... | collective-permute-start | bytes 589832 | tf_op jit(solution)/shard_map/ppermute | solution.py:24
  6.9 16.7 %collective-permute-start.2 = (bf16[192,512]{1,0:T(8,128)(2,1)S(1)}, bf16[192,512]{1,0:T(8,128)(2,1)S(1)}, u32[]{:S(2)}, u32[]{:S(2)}) collective-permute-start(bf16[192,512]{1,0:T(8,128)(2,1)S(1)} %shard_map.91.refs_0_), channel_id=1, source_target_pairs={{0,8},{4,12},{8,0},{12,4},{1,9},{5,13},{9,1},{13,5},{2,10},{6,14},... | collective-permute-start | bytes 589832 | tf_op jit(solution)/shard_map/ppermute | solution.py:24
  6.9 16.7 %collective-permute-start.1 = (bf16[192,512]{1,0:T(8,128)(2,1)S(1)}, bf16[192,512]{1,0:T(8,128)(2,1)S(1)}, u32[]{:S(2)}, u32[]{:S(2)}) collective-permute-start(bf16[192,512]{1,0:T(8,128)(2,1)S(1)} %shard_map.91.refs_0_), channel_id=1, source_target_pairs={{0,4},{4,8},{8,12},{12,0},{1,5},{5,9},{9,13},{13,1},{2,6},{6,10},{... | collective-permute-start | bytes 589832 | tf_op jit(solution)/shard_map/ppermute | solution.py:24
  7.9 24.3 %collective-permute-start = (bf16[4,2,32,512]{3,2,1,0:T(8,128)(2,1)}, bf16[4,2,32,512]{3,2,1,0:T(8,128)(2,1)S(1)}, u32[]{:S(2)}, u32[]{:S(2)}) collective-permute-start(bf16[4,2,32,512]{3,2,1,0:T(8,128)(2,1)} %bitcast.3.adapters_ref), channel_id=1, source_target_pairs={{0,2},{1,3},{2,0},{3,1},{4,6},{5,7},{6,4},{7,5},{8,10},{9,11},{10,... | collective-permute-start | bytes 786440 | tf_op jit(solution)/shard_map/ppermute | solution.py:28
  24.3 16.6 %collective-permute-start.4 = (bf16[10,32,512]{2,1,0:T(8,128)(2,1)S(1)}, bf16[10,32,512]{2,1,0:T(8,128)(2,1)S(1)}, u32[]{:S(2)}, u32[]{:S(2)}) collective-permute-start(bf16[10,32,512]{2,1,0:T(8,128)(2,1)S(1)} %get-tuple-element.44), channel_id=1, source_target_pairs={{0,2},{1,3},{2,0},{3,1},{4,6},{5,7},{6,4},{7,5},{8,10},{9,11},{10,... | collective-permute-start | bytes 983048 | tf_op jit(solution)/shard_map/ppermute | solution.py:28
  26.9 5.8 %collective-permute-start.5 = (bf16[6,32,512]{2,1,0:T(8,128)(2,1)S(1)}, bf16[6,32,512]{2,1,0:T(8,128)(2,1)S(1)}, u32[]{:S(2)}, u32[]{:S(2)}) collective-permute-start(bf16[6,32,512]{2,1,0:T(8,128)(2,1)S(1)} %get-tuple-element.43.refs_2_), channel_id=1, source_target_pairs={{0,16},{16,0},{1,17},{17,1},{2,18},{18,2},{3,19},{19,3},{4,20},{20... | collective-permute-start | bytes 589832 | tf_op jit(solution)/shard_map/ppermute | solution.py:32
  28.5 10.3 %collective-permute-start.6 = (bf16[448,256]{1,0:T(8,128)(2,1)S(1)}, bf16[448,256]{1,0:T(8,128)(2,1)S(1)}, u32[]{:S(2)}, u32[]{:S(2)}) collective-permute-start(bf16[448,256]{1,0:T(8,128)(2,1)S(1)} %get-tuple-element.45), channel_id=1, source_target_pairs={{0,4},{4,8},{8,12},{12,0},{1,5},{5,9},{9,13},{13,1},{2,6},{6,10},{... | collective-permute-start | bytes 688136 | tf_op jit(solution)/shard_map/ppermute | solution.py:24
  29.3 11.6 %collective-permute-start.7 = (bf16[448,256]{1,0:T(8,128)(2,1)S(1)}, bf16[448,256]{1,0:T(8,128)(2,1)S(1)}, u32[]{:S(2)}, u32[]{:S(2)}) collective-permute-start(bf16[448,256]{1,0:T(8,128)(2,1)S(1)} %get-tuple-element.46), channel_id=1, source_target_pairs={{0,12},{4,0},{8,4},{12,8},{1,13},{5,1},{9,5},{13,9},{2,14},{6,2},{... | collective-permute-start | bytes 688136 | tf_op jit(solution)/shard_map/ppermute | solution.py:24
  41.0 10.5 %collective-permute-start.10 = (bf16[32,32,512]{2,1,0:T(8,128)(2,1)S(1)}, bf16[32,32,512]{2,1,0:T(8,128)(2,1)S(1)}, u32[]{:S(2)}, u32[]{:S(2)}) collective-permute-start(bf16[32,32,512]{2,1,0:T(8,128)(2,1)S(1)} %shard_map.94.refs_0_), channel_id=1, source_target_pairs={{0,1},{1,0},{2,3},{3,2},{4,5},{5,4},{6,7},{7,6},{8,9},{9,8},{10,11... | collective-permute-start | bytes 3145736 | tf_op jit(solution)/shard_map/ppermute | solution.py:28
  42.3 7.7 %collective-permute-start.13 = (bf16[192,256]{1,0:T(8,128)(2,1)S(1)}, bf16[192,256]{1,0:T(8,128)(2,1)S(1)}, u32[]{:S(2)}, u32[]{:S(2)}) collective-permute-start(bf16[192,256]{1,0:T(8,128)(2,1)S(1)} %slice.65), channel_id=1, source_target_pairs={{0,8},{4,12},{8,0},{12,4},{1,9},{5,13},{9,1},{13,5},{2,10},{6,14},... | collective-permute-start | bytes 294920 | tf_op jit(solution)/shard_map/ppermute | solution.py:24
  46.8 11.3 %collective-permute-start.21 = (bf16[6,32,512]{2,1,0:T(8,128)(2,1)S(1)}, bf16[6,32,512]{2,1,0:T(8,128)(2,1)S(1)}, u32[]{:S(2)}, u32[]{:S(2)}) collective-permute-start(bf16[6,32,512]{2,1,0:T(8,128)(2,1)S(1)} %get-tuple-element.58.refs_2_), channel_id=1, source_target_pairs={{0,16},{16,0},{1,17},{17,1},{2,18},{18,2},{3,19},{19,3},{4,20},{20... | collective-permute-start | bytes 589832 | tf_op jit(solution)/shard_map/ppermute | solution.py:32
  49.9 8.2 %collective-permute-start.20 = (bf16[6,32,512]{2,1,0:T(8,128)(2,1)S(1)}, bf16[6,32,512]{2,1,0:T(8,128)(2,1)S(1)}, u32[]{:S(2)}, u32[]{:S(2)}) collective-permute-start(bf16[6,32,512]{2,1,0:T(8,128)(2,1)S(1)} %get-tuple-element.58.refs_2_), channel_id=1, source_target_pairs={{0,2},{1,3},{2,0},{3,1},{4,6},{5,7},{6,4},{7,5},{8,10},{9,11},{10,... | collective-permute-start | bytes 589832 | tf_op jit(solution)/shard_map/ppermute | solution.py:28
  58.2 14.6 %collective-permute-start.24 = (bf16[26,32,512]{2,1,0:T(8,128)(2,1)S(1)}, bf16[26,32,512]{2,1,0:T(8,128)(2,1)S(1)}, u32[]{:S(2)}, u32[]{:S(2)}) collective-permute-start(bf16[26,32,512]{2,1,0:T(8,128)(2,1)S(1)} %shard_map.97.refs_0_), channel_id=1, source_target_pairs={{0,1},{1,0},{2,3},{3,2},{4,5},{5,4},{6,7},{7,6},{8,9},{9,8},{10,11... | collective-permute-start | bytes 2555912 | tf_op jit(solution)/shard_map/ppermute | solution.py:28
  58.7 9.9 %collective-permute-start.16 = (bf16[256,256]{1,0:T(8,128)(2,1)S(1)}, bf16[256,256]{1,0:T(8,128)(2,1)S(1)}, u32[]{:S(2)}, u32[]{:S(2)}) collective-permute-start(bf16[256,256]{1,0:T(8,128)(2,1)S(1)} %slice.72), channel_id=1, source_target_pairs={{0,8},{4,12},{8,0},{12,4},{1,9},{5,13},{9,1},{13,5},{2,10},{6,14},... | collective-permute-start | bytes 393224 | tf_op jit(solution)/shard_map/ppermute | solution.py:24
  61.3 7.4 %collective-permute-start.15 = (f32[16,2048]{1,0:T(8,128)S(1)}, f32[16,2048]{1,0:T(8,128)S(1)}, u32[]{:S(2)}, u32[]{:S(2)}) collective-permute-start(f32[16,2048]{1,0:T(8,128)S(1)} %get-tuple-element.63), channel_id=1, source_target_pairs={{0,2},{1,3},{2,0},{3,1},{4,6},{5,7},{6,4},{7,5},{8,10},{9,11},{10,... | collective-permute-start | bytes 393224 | tf_op jit(solution)/shard_map/ppermute | solution.py:28
  61.9 6.8 %collective-permute-start.22 = (bf16[3,32,512]{2,1,0:T(8,128)(2,1)S(1)}, bf16[3,32,512]{2,1,0:T(8,128)(2,1)S(1)}, u32[]{:S(2)}, u32[]{:S(2)}) collective-permute-start(bf16[3,32,512]{2,1,0:T(8,128)(2,1)S(1)} %slice.75), channel_id=1, source_target_pairs={{0,2},{1,3},{2,0},{3,1},{4,6},{5,7},{6,4},{7,5},{8,10},{9,11},{10,... | collective-permute-start | bytes 294920 | tf_op jit(solution)/shard_map/ppermute | solution.py:28
  64.5 8.3 %collective-permute-start.26 = (bf16[3,32,512]{2,1,0:T(8,128)(2,1)S(1)}, bf16[3,32,512]{2,1,0:T(8,128)(2,1)S(1)}, u32[]{:S(2)}, u32[]{:S(2)}) collective-permute-start(bf16[3,32,512]{2,1,0:T(8,128)(2,1)S(1)} %collective-permute-done.23.refs_2_), channel_id=1, source_target_pairs={{0,1},{1,0},{2,3},{3,2},{4,5},{5,4},{6,7},{7,6},{8,9},{9,8},{10,11... | collective-permute-start | bytes 294920 | tf_op jit(solution)/shard_map/ppermute | solution.py:28
  70.6 7.9 %collective-permute-start.19 = (bf16[16,2048]{1,0:T(8,128)(2,1)S(1)}, bf16[16,2048]{1,0:T(8,128)(2,1)S(1)}, u32[]{:S(2)}, u32[]{:S(2)}) collective-permute-start(bf16[16,2048]{1,0:T(8,128)(2,1)S(1)} %shard_map.96.a0), channel_id=1, source_target_pairs={{0,3},{1,2},{2,1},{3,0},{4,7},{5,6},{6,5},{7,4},{8,11},{9,10},{10,... | collective-permute-start | bytes 196616 | tf_op jit(solution)/shard_map/ppermute | solution.py:28
  71.3 7.2 %collective-permute-start.18 = (bf16[16,2048]{1,0:T(8,128)(2,1)S(1)}, bf16[16,2048]{1,0:T(8,128)(2,1)S(1)}, u32[]{:S(2)}, u32[]{:S(2)}) collective-permute-start(bf16[16,2048]{1,0:T(8,128)(2,1)S(1)} %shard_map.96.a0), channel_id=1, source_target_pairs={{0,2},{1,3},{2,0},{3,1},{4,6},{5,7},{6,4},{7,5},{8,10},{9,11},{10,... | collective-permute-start | bytes 196616 | tf_op jit(solution)/shard_map/ppermute | solution.py:28
  72.8 5.7 %collective-permute-start.17 = (bf16[16,2048]{1,0:T(8,128)(2,1)S(1)}, bf16[16,2048]{1,0:T(8,128)(2,1)S(1)}, u32[]{:S(2)}, u32[]{:S(2)}) collective-permute-start(bf16[16,2048]{1,0:T(8,128)(2,1)S(1)} %shard_map.96.a0), channel_id=1, source_target_pairs={{0,1},{1,0},{2,3},{3,2},{4,5},{5,4},{6,7},{7,6},{8,9},{9,8},{10,11... | collective-permute-start | bytes 196616 | tf_op jit(solution)/shard_map/ppermute | solution.py:28
  80.1 19.2 %collective-permute-start.27 = (f32[16,2048]{1,0:T(8,128)S(1)}, f32[16,2048]{1,0:T(8,128)S(1)}, u32[]{:S(2)}, u32[]{:S(2)}) collective-permute-start(f32[16,2048]{1,0:T(8,128)S(1)} %get-tuple-element.61), channel_id=1, source_target_pairs={{0,0},{1,4},{2,8},{3,12},{4,1},{5,5},{6,9},{7,13},{8,2},{9,6},{10,... | collective-permute-start | bytes 393224 | tf_op jit(solution)/shard_map/ppermute | solution.py:37
  80.8 7.2 %collective-permute-start.28 = (bf16[16,2048]{1,0:T(8,128)(2,1)S(1)}, bf16[16,2048]{1,0:T(8,128)(2,1)S(1)}, u32[]{:S(2)}, u32[]{:S(2)}) collective-permute-start(bf16[16,2048]{1,0:T(8,128)(2,1)S(1)} %get-tuple-element.71), channel_id=1, source_target_pairs={{0,1},{1,5},{2,9},{3,13},{4,0},{5,4},{6,8},{7,12},{8,3},{9,7},{10,... | collective-permute-start | bytes 196616 | tf_op jit(solution)/shard_map/ppermute | solution.py:37
  83.1 9.6 %collective-permute-start.30 = (bf16[16,2048]{1,0:T(8,128)(2,1)S(1)}, bf16[16,2048]{1,0:T(8,128)(2,1)S(1)}, u32[]{:S(2)}, u32[]{:S(2)}) collective-permute-start(bf16[16,2048]{1,0:T(8,128)(2,1)S(1)} %get-tuple-element.72), channel_id=1, source_target_pairs={{0,3},{1,7},{2,11},{3,15},{4,2},{5,6},{6,10},{7,14},{8,1},{9,5},{1... | collective-permute-start | bytes 196616 | tf_op jit(solution)/shard_map/ppermute | solution.py:37
  86.3 13.0 %collective-permute-start.29 = (bf16[16,2048]{1,0:T(8,128)(2,1)S(1)}, bf16[16,2048]{1,0:T(8,128)(2,1)S(1)}, u32[]{:S(2)}, u32[]{:S(2)}) collective-permute-start(bf16[16,2048]{1,0:T(8,128)(2,1)S(1)} %get-tuple-element.73), channel_id=1, source_target_pairs={{0,2},{1,6},{2,10},{3,14},{4,3},{5,7},{6,11},{7,15},{8,0},{9,4},{1... | collective-permute-start | bytes 196616 | tf_op jit(solution)/shard_map/ppermute | solution.py:37
  (9 other events, 32.8 us)

commit v3 on v2

--- a/solution.py
+++ b/solution.py
@@ -12,7 +12,6 @@
 BF16 = jnp.bfloat16
 SIDE = 4
 BLOCK = 256
-PACK_COST = 64
 MIB = 1 << 20
 
 
@@ -37,24 +36,26 @@
     return lax.ppermute(x, ("tp", "dp"), pairs)
 
 
-def pack_kernel(*refs):
+def pack_kernel(spans, *refs):
     out_ref, at = refs[-1], 0
-    for ref in refs[:-1]:
-        out_ref[at : at + ref.shape[0]] = ref[...]
-        at += ref.shape[0]
-
-
-def pack(parts, cost=1):
+    for ref, (start, count) in zip(refs[:-1], spans):
+        out_ref[at : at + count] = ref[start : start + count]
+        at += count
+
+
+def pack(parts):
     spec = pl.BlockSpec(memory_space=pltpu.VMEM)
-    shape = (sum(part.shape[0] for part in parts), *parts[0].shape[1:])
+    parts = [part if isinstance(part, tuple) else (part, 0, part.shape[0]) for part in parts]
+    arrays = [array for array, _, _ in parts]
+    spans = [(start, count) for _, start, count in parts]
+    shape = (sum(count for _, count in spans), *arrays[0].shape[1:])
     return pl.pallas_call(
-        pack_kernel,
-        out_shape=jax.ShapeDtypeStruct(shape, parts[0].dtype),
+        functools.partial(pack_kernel, spans),
+        out_shape=jax.ShapeDtypeStruct(shape, arrays[0].dtype),
         in_specs=[spec] * len(parts),
         out_specs=spec,
         compiler_params=pltpu.CompilerParams(vmem_limit_bytes=4 * MIB),
-        cost_estimate=pl.CostEstimate(flops=0, bytes_accessed=cost * MIB, transcendentals=0),
-    )(*parts)
+    )(*arrays)
 
 
 def small_call(kernel, scalars, arrays, out_shape, vmem=8 * MIB):
@@ -572,6 +573,7 @@
         shaped(2 * cached + 4 * rows, kv_cols),
     )
 
+    *held, halves_far = lax.optimization_barrier((*held, halves_far))
     held = after(held, *cache_send, q_slots, o_slots, spots, froms)
     unit = (rank // 2, width)
     slab = slab // unit[0]
@@ -590,11 +592,10 @@
         (q_far, q_other, from_next, from_last)
     )
     middle_keys = along_tp(after(cache_send[2][:cached], q_far, q_other), 2)
-    own_rows, middle_keys = lax.optimization_barrier((own_rows, middle_keys))
     q_corners = corners_of(q_far, q_other)
-    halves = halves.reshape(2, 4, *unit)
-    halves_far = halves_far.reshape(2, 4, *unit)
-    q_packed = pack([halves[0], halves_far[0], q_mine, q_far, q_other, near_rows], PACK_COST)
+    halves = halves.reshape(8, *unit)
+    halves_far = halves_far.reshape(8, *unit)
+    q_packed = pack([(halves, 0, 4), (halves_far, 0, 4), q_mine, q_far, q_other, near_rows])
     q_parts = with_sibling(q_packed, q_corners)
     o_mine = after(o_mine, *q_corners)
     o_far, o_other = across_dp(o_mine, 2), across_groups(o_mine)
@@ -610,14 +611,18 @@
         rank,
         0,
     )
+    q_part, middle_keys, middle_send, o_far, o_other = lax.optimization_barrier(
+        (q_part, middle_keys, cache_send[2][cached:], o_far, o_other)
+    )
     near = across_dp(jnp.concatenate([q_part[rows : 2 * rows], q_part[3 * rows :]]), 1)
-    middle_rest = along_tp(after(cache_send[2][cached:], q_part), 2)
+    near, o_far, o_other = lax.optimization_barrier((near, o_far, o_other))
+    middle_rest = along_tp(middle_send, 2)
     caches = [cache_send[0], from_next, from_last, middle_keys, middle_rest]
     q_near_sum = q_part[:rows] + near[:rows]
     q_far_sum = across_dp(q_part[2 * rows : 3 * rows] + near[rows:], 2)
 
-    o_corners = corners_of(*after((o_far, o_other), near))
-    o_packed = pack([halves[1], halves_far[1], o_mine, o_far, o_other])
+    o_corners = corners_of(o_far, o_other)
+    o_packed = pack([(halves, 4, 4), (halves_far, 4, 4), o_mine, o_far, o_other])
     o_parts = with_sibling(o_packed, o_corners)
 
     vmem_spec = pl.BlockSpec(memory_space=pltpu.VMEM)

time: 100 us -> 100 us (level)
  Pallas kernels: 21.7 us -> 23.6 us
    ppermute x7, waiting for transfers between devices: 16.2 us -> 11.3 us  [along_tp(): return lax.ppermute(x, 'tp', [(i, (i + k) % SIDE) for i in range(SIDE)])]
    ppermute x4, waiting for transfers between devices: 3.94 us -> 8.47 us  [across_groups(): return lax.ppermute(x, 'groups', [(0, 1), (1, 0)])]
    pallas_call x2, Pallas kernels: 0.13 us -> 2.02 us  [pack(): pl.pallas_call(functools.partial(pack_kernel, spans), out_shape=jax.Shape...]
    ppermute x16, starting transfers between devices: 10.4 us -> 8.72 us  [across_dp(): return lax.ppermute(x, 'dp', [(i, i ^ k) for i in range(SIDE)])]
    ppermute x7, starting transfers between devices: 11.5 us -> 12.9 us  [along_tp(): return lax.ppermute(x, 'tp', [(i, (i + k) % SIDE) for i in range(SIDE)])]
    slice x3 -> x1, local copies, waits for them, and re-layouts: 1.01 us -> 0.01 us  [on_device(): cache_send[2][cached:]]
  transfers between devices with their start and end apart: 31 -> 31, of which waited for: 13 -> 14; matrix products, arithmetic and copies ran while one was open for 3% -> 1% of each run, Pallas kernels for 19% -> 18%
where the time goes in v3:
time: 100 us; the launch traced here: 99.6 us
  waiting for transfers between devices  37.9 us (38%)
  starting transfers between devices  33.1 us (33%)
  Pallas kernels  23.6 us (24%)
  local copies, waits for them, and re-layouts  3.77 us (4%)
  other arithmetic  1.06 us (1%)
    ppermute x4, waiting for transfers between devices, to_holder(): return lax.ppermute(x, ('tp', 'dp'), pairs)  13.5 us
    ppermute x7, starting transfers between devices, along_tp(): return lax.ppermute(x, 'tp', [(i, (i + k) % SIDE) for i in range(SIDE)])  12.9 us
    pallas_call x2, Pallas kernels, merge_call(): pl.pallas_call(kernel, out_shape=out_shape, in_specs=[pl.BlockSpec(memory...  12.1 us
    ppermute x7, waiting for transfers between devices, along_tp(): return lax.ppermute(x, 'tp', [(i, (i + k) % SIDE) for i in range(SIDE)])  11.3 us
    ppermute x16, starting transfers between devices, across_dp(): return lax.ppermute(x, 'dp', [(i, i ^ k) for i in range(SIDE)])  8.72 us
    ppermute x4, waiting for transfers between devices, across_groups(): return lax.ppermute(x, 'groups', [(0, 1), (1, 0)])  8.47 us
    ppermute x4, starting transfers between devices, to_holder(): return lax.ppermute(x, ('tp', 'dp'), pairs)  6.3 us
    ppermute x4, starting transfers between devices, across_groups(): return lax.ppermute(x, 'groups', [(0, 1), (1, 0)])  5.19 us
  transfers between devices with their start and end apart: 31, of which 14 were waited for; matrix products, arithmetic and copies ran while one was open for 1% of the time, Pallas kernels for 18%

profile of v3, /device:TPU:0, one launch (start us, length us, event | category | flops | bytes accessed | tf_op | source)
XLA Modules:
  0.0 99.6 jit_solution(11258204070219689257)
XLA Ops:
  1.8 5.1 %collective-permute-start.2 = (bf16[192,512]{1,0:T(8,128)(2,1)S(1)}, bf16[192,512]{1,0:T(8,128)(2,1)S(1)}, u32[]{:S(2)}, u32[]{:S(2)}) collective-permute-start(bf16[192,512]{1,0:T(8,128)(2,1)S(1)} %shard_map.91.refs_0_), channel_id=1, source_target_pairs={{0,12},{4,0},{8,4},{12,8},{1,13},{5,1},{9,5},{13,9},{2,14},{6,2},{... | collective-permute-start | bytes 589832 | tf_op jit(solution)/shard_map/ppermute | solution.py:23
  8.0 1.5 %collective-permute-start.3 = (bf16[4,2,32,512]{3,2,1,0:T(8,128)(2,1)}, bf16[4,2,32,512]{3,2,1,0:T(8,128)(2,1)S(1)}, u32[]{:S(2)}, u32[]{:S(2)}) collective-permute-start(bf16[4,2,32,512]{3,2,1,0:T(8,128)(2,1)} %bitcast.3.adapters_ref), channel_id=1, source_target_pairs={{0,2},{1,3},{2,0},{3,1},{4,6},{5,7},{6,4},{7,5},{8,10},{9,11},{10,... | collective-permute-start | bytes 786440 | tf_op jit(solution)/shard_map/ppermute | solution.py:27
  12.5 4.3 %shard_map.92 = (bf16[448,256]{1,0:T(8,128)(2,1)S(1)}, bf16[448,256]{1,0:T(8,128)(2,1)S(1)}, bf16[448,256]{1,0:T(8,128)(2,1)S(1)}, bf16[448,256]{1,0:T(8,128)(2,1)S(1)}) custom-call(s32[4]{0:T(128)S(1)} %and_select_fusion.heads_ref, bf16[16,2048]{1,0:T(8,128)(2,1)S(1)} %reshape.25.tokens_ref, bf16[192,1024]{1,0:T(8,128)(2,1)S(1)} %bitcast.15, ...), custom_call_target="tpu_custom_call" | custom-call | flops 134217728 | bytes 16777216 | tf_op jit(solution)/shard_map/pallas_call | solution.py:138
  16.9 6.7 %collective-permute-done.1.refs_2_ = bf16[192,512]{1,0:T(8,128)(2,1)S(1)} collective-permute-done((bf16[192,512]{1,0:T(8,128)(2,1)S(1)}, bf16[192,512]{1,0:T(8,128)(2,1)S(1)}, u32[]{:S(2)}, u32[]{:S(2)}) %collective-permute-start.1) | collective-permute-done | bytes 196640 | tf_op jit(solution)/shard_map/ppermute | solution.py:23
  24.4 1.6 %collective-permute-start.4 = (bf16[10,32,512]{2,1,0:T(8,128)(2,1)S(1)}, bf16[10,32,512]{2,1,0:T(8,128)(2,1)S(1)}, u32[]{:S(2)}, u32[]{:S(2)}) collective-permute-start(bf16[10,32,512]{2,1,0:T(8,128)(2,1)S(1)} %get-tuple-element.57), channel_id=1, source_target_pairs={{0,2},{1,3},{2,0},{3,1},{4,6},{5,7},{6,4},{7,5},{8,10},{9,11},{10,... | collective-permute-start | bytes 983048 | tf_op jit(solution)/shard_map/ppermute | solution.py:27
  26.8 2.9 %collective-permute-start.7 = (bf16[448,256]{1,0:T(8,128)(2,1)S(1)}, bf16[448,256]{1,0:T(8,128)(2,1)S(1)}, u32[]{:S(2)}, u32[]{:S(2)}) collective-permute-start(bf16[448,256]{1,0:T(8,128)(2,1)S(1)} %get-tuple-element.59), channel_id=1, source_target_pairs={{0,12},{4,0},{8,4},{12,8},{1,13},{5,1},{9,5},{13,9},{2,14},{6,2},{... | collective-permute-start | bytes 688136 | tf_op jit(solution)/shard_map/ppermute | solution.py:23
  29.7 1.5 %collective-permute-start.5 = (bf16[6,32,512]{2,1,0:T(8,128)(2,1)S(1)}, bf16[6,32,512]{2,1,0:T(8,128)(2,1)S(1)}, u32[]{:S(2)}, u32[]{:S(2)}) collective-permute-start(bf16[6,32,512]{2,1,0:T(8,128)(2,1)S(1)} %get-tuple-element.56.refs_2_), channel_id=1, source_target_pairs={{0,16},{16,0},{1,17},{17,1},{2,18},{18,2},{3,19},{19,3},{4,20},{20... | collective-permute-start | bytes 589832 | tf_op jit(solution)/shard_map/ppermute | solution.py:31
  31.3 4.2 %collective-permute-done.5.refs_4_ = bf16[6,32,512]{2,1,0:T(8,128)(2,1)S(1)} collective-permute-done((bf16[6,32,512]{2,1,0:T(8,128)(2,1)S(1)}, bf16[6,32,512]{2,1,0:T(8,128)(2,1)S(1)}, u32[]{:S(2)}, u32[]{:S(2)}) %collective-permute-start.5) | collective-permute-done | bytes 196640 | tf_op jit(solution)/shard_map/ppermute | solution.py:31
  36.3 2.3 %collective-permute-done.7.c3 = bf16[448,256]{1,0:T(8,128)(2,1)S(1)} collective-permute-done((bf16[448,256]{1,0:T(8,128)(2,1)S(1)}, bf16[448,256]{1,0:T(8,128)(2,1)S(1)}, u32[]{:S(2)}, u32[]{:S(2)}) %collective-permute-start.7) | collective-permute-done | bytes 229408 | tf_op jit(solution)/shard_map/ppermute | solution.py:23
  39.7 1.6 %collective-permute-start.9 = (bf16[3,32,512]{2,1,0:T(8,128)(2,1)S(1)}, bf16[3,32,512]{2,1,0:T(8,128)(2,1)S(1)}, u32[]{:S(2)}, u32[]{:S(2)}) collective-permute-start(bf16[3,32,512]{2,1,0:T(8,128)(2,1)S(1)} %slice.46), channel_id=1, source_target_pairs={{0,16},{16,0},{1,17},{17,1},{2,18},{18,2},{3,19},{19,3},{4,20},{20... | collective-permute-start | bytes 294920 | tf_op jit(solution)/shard_map/ppermute | solution.py:31
  41.9 3.1 %collective-permute-done.9.refs_2_ = bf16[3,32,512]{2,1,0:T(8,128)(2,1)S(1)} collective-permute-done((bf16[3,32,512]{2,1,0:T(8,128)(2,1)S(1)}, bf16[3,32,512]{2,1,0:T(8,128)(2,1)S(1)}, u32[]{:S(2)}, u32[]{:S(2)}) %collective-permute-start.9) | collective-permute-done | bytes 98336 | tf_op jit(solution)/shard_map/ppermute | solution.py:31
  47.4 1.5 %collective-permute-start.13 = (bf16[192,256]{1,0:T(8,128)(2,1)S(1)}, bf16[192,256]{1,0:T(8,128)(2,1)S(1)}, u32[]{:S(2)}, u32[]{:S(2)}) collective-permute-start(bf16[192,256]{1,0:T(8,128)(2,1)S(1)} %slice.47), channel_id=1, source_target_pairs={{0,8},{4,12},{8,0},{12,4},{1,9},{5,13},{9,1},{13,5},{2,10},{6,14},... | collective-permute-start | bytes 294920 | tf_op jit(solution)/shard_map/ppermute | solution.py:23
  49.0 6.5 %shard_map.95 = f32[64,2048]{1,0:T(8,128)S(1)} custom-call(s32[18]{0:T(128)S(1)} %concatenate.13.slots_ref, bf16[32,32,512]{2,1,0:T(8,128)(2,1)S(1)} %shard_map.94.refs_0_, bf16[3,32,512]{2,1,0:T(8,128)(2,1)S(1)} %collective-permute-done.8.refs_1_, bf16[3,32,512]{2,1,0:T(8,128)(2,1)S(1)} %collective-permute-done.9.refs_2_, ...), custom_call_target="tpu_custom_call" | custom-call | tf_op jit(solution)/shard_map/pallas_call | solution.py:296
  55.8 1.5 %collective-permute-done.16 = f32[32,2048]{1,0:T(8,128)S(1)} collective-permute-done((f32[32,2048]{1,0:T(8,128)S(1)}, f32[32,2048]{1,0:T(8,128)S(1)}, u32[]{:S(2)}, u32[]{:S(2)}) %collective-permute-start.16) | collective-permute-done | bytes 262176 | tf_op jit(solution)/shard_map/ppermute | solution.py:27
  59.9 1.5 %collective-permute-start.22 = (bf16[3,32,512]{2,1,0:T(8,128)(2,1)S(1)}, bf16[3,32,512]{2,1,0:T(8,128)(2,1)S(1)}, u32[]{:S(2)}, u32[]{:S(2)}) collective-permute-start(bf16[3,32,512]{2,1,0:T(8,128)(2,1)S(1)} %slice.55), channel_id=1, source_target_pairs={{0,2},{1,3},{2,0},{3,1},{4,6},{5,7},{6,4},{7,5},{8,10},{9,11},{10,... | collective-permute-start | bytes 294920 | tf_op jit(solution)/shard_map/ppermute | solution.py:27
  62.1 1.6 %collective-permute-start.23 = (bf16[3,32,512]{2,1,0:T(8,128)(2,1)S(1)}, bf16[3,32,512]{2,1,0:T(8,128)(2,1)S(1)}, u32[]{:S(2)}, u32[]{:S(2)}) collective-permute-start(bf16[3,32,512]{2,1,0:T(8,128)(2,1)S(1)} %slice.56), channel_id=1, source_target_pairs={{0,16},{16,0},{1,17},{17,1},{2,18},{18,2},{3,19},{19,3},{4,20},{20... | collective-permute-start | bytes 294920 | tf_op jit(solution)/shard_map/ppermute | solution.py:31
  63.7 1.8 %collective-permute-done.22.refs_1_ = bf16[3,32,512]{2,1,0:T(8,128)(2,1)S(1)} collective-permute-done((bf16[3,32,512]{2,1,0:T(8,128)(2,1)S(1)}, bf16[3,32,512]{2,1,0:T(8,128)(2,1)S(1)}, u32[]{:S(2)}, u32[]{:S(2)}) %collective-permute-start.22) | collective-permute-done | bytes 98336 | tf_op jit(solution)/shard_map/ppermute | solution.py:27
  68.0 1.9 %shard_map.96.a0 = bf16[16,2048]{1,0:T(8,128)(2,1)S(1)} custom-call(s32[8]{0:T(128)S(1)} %pad_add_fusion.spots_ref, f32[16,2048]{1,0:T(8,128)S(1)} %get-tuple-element.80.qa_ref, f32[16,2048]{1,0:T(8,128)S(1)} %collective-permute-done.17.qb_ref, bf16[448,256]{1,0:T(8,128)(2,1)S(1)} %get-tuple-element.48.c0, bf16[448,256]{1,0:T(8,128)(2,1)S(1)} %collective-permute-done.6.c1, ...), custom_call_target="tpu_custom_call" | custom-call | tf_op jit(solution)/shard_map/pallas_call | solution.py:629
  71.9 5.6 %shard_map.98.w_ref = bf16[2048,2048]{1,0:T(8,128)(2,1)S(1)} custom-call(s32[18]{0:T(128)S(1)} %concatenate.14.slots_ref, bf16[26,32,512]{2,1,0:T(8,128)(2,1)S(1)} %shard_map.97.refs_0_, bf16[3,32,512]{2,1,0:T(8,128)(2,1)S(1)} %collective-permute-done.22.refs_1_, bf16[3,32,512]{2,1,0:T(8,128)(2,1)S(1)} %collective-permute-done.23.refs_2_, ...), custom_call_target="tpu_custom_call" | custom-call | bytes 16777216 | tf_op jit(solution)/shard_map/pallas_call | solution.py:296
  77.5 1.6 %shard_map.99 = (f32[16,2048]{1,0:T(8,128)S(1)}, bf16[3,16,2048]{2,1,0:T(8,128)(2,1)S(1)}) custom-call(s32[1]{0:T(128)} %bitcast.turn_ref, bf16[16,2048]{1,0:T(8,128)(2,1)S(1)} %shard_map.96.a0, bf16[16,2048]{1,0:T(8,128)(2,1)S(1)} %collective-permute-done.19.a1, bf16[16,2048]{1,0:T(8,128)(2,1)S(1)} %collective-permute-done.20.a2, ...), custom_call_target="tpu_custom_call" | custom-call | tf_op jit(solution)/shard_map/pallas_call | solution.py:650
  79.8 1.9 %collective-permute-start.28 = (bf16[16,2048]{1,0:T(8,128)(2,1)S(1)}, bf16[16,2048]{1,0:T(8,128)(2,1)S(1)}, u32[]{:S(2)}, u32[]{:S(2)}) collective-permute-start(bf16[16,2048]{1,0:T(8,128)(2,1)S(1)} %get-tuple-element.83), channel_id=1, source_target_pairs={{0,1},{1,5},{2,9},{3,13},{4,0},{5,4},{6,8},{7,12},{8,3},{9,7},{10,... | collective-permute-start | bytes 196616 | tf_op jit(solution)/shard_map/ppermute | solution.py:36
  81.8 3.7 %collective-permute-start.30 = (bf16[16,2048]{1,0:T(8,128)(2,1)S(1)}, bf16[16,2048]{1,0:T(8,128)(2,1)S(1)}, u32[]{:S(2)}, u32[]{:S(2)}) collective-permute-start(bf16[16,2048]{1,0:T(8,128)(2,1)S(1)} %get-tuple-element.84), channel_id=1, source_target_pairs={{0,3},{1,7},{2,11},{3,15},{4,2},{5,6},{6,10},{7,14},{8,1},{9,5},{1... | collective-permute-start | bytes 196616 | tf_op jit(solution)/shard_map/ppermute | solution.py:36
  86.6 5.3 %collective-permute-done.30 = bf16[16,2048]{1,0:T(8,128)(2,1)S(1)} collective-permute-done((bf16[16,2048]{1,0:T(8,128)(2,1)S(1)}, bf16[16,2048]{1,0:T(8,128)(2,1)S(1)}, u32[]{:S(2)}, u32[]{:S(2)}) %collective-permute-start.30) | collective-permute-done | bytes 65568 | tf_op jit(solution)/shard_map/ppermute | solution.py:36
  91.8 7.1 %collective-permute-done.29 = bf16[16,2048]{1,0:T(8,128)(2,1)S(1)} collective-permute-done((bf16[16,2048]{1,0:T(8,128)(2,1)S(1)}, bf16[16,2048]{1,0:T(8,128)(2,1)S(1)}, u32[]{:S(2)}, u32[]{:S(2)}) %collective-permute-start.29) | collective-permute-done | bytes 65568 | tf_op jit(solution)/shard_map/ppermute | solution.py:36
  (73 shorter events, 23.0 us)
Async XLA Ops:
  1.8 15.1 %collective-permute-start.2 = (bf16[192,512]{1,0:T(8,128)(2,1)S(1)}, bf16[192,512]{1,0:T(8,128)(2,1)S(1)}, u32[]{:S(2)}, u32[]{:S(2)}) collective-permute-start(bf16[192,512]{1,0:T(8,128)(2,1)S(1)} %shard_map.91.refs_0_), channel_id=1, source_target_pairs={{0,12},{4,0},{8,4},{12,8},{1,13},{5,1},{9,5},{13,9},{2,14},{6,2},{... | collective-permute-start | bytes 589832 | tf_op jit(solution)/shard_map/ppermute | solution.py:23
  6.9 16.7 %collective-permute-start.1 = (bf16[192,512]{1,0:T(8,128)(2,1)S(1)}, bf16[192,512]{1,0:T(8,128)(2,1)S(1)}, u32[]{:S(2)}, u32[]{:S(2)}) collective-permute-start(bf16[192,512]{1,0:T(8,128)(2,1)S(1)} %shard_map.91.refs_0_), channel_id=1, source_target_pairs={{0,8},{4,12},{8,0},{12,4},{1,9},{5,13},{9,1},{13,5},{2,10},{6,14},... | collective-permute-start | bytes 589832 | tf_op jit(solution)/shard_map/ppermute | solution.py:23
  7.0 16.7 %collective-permute-start = (bf16[192,512]{1,0:T(8,128)(2,1)S(1)}, bf16[192,512]{1,0:T(8,128)(2,1)S(1)}, u32[]{:S(2)}, u32[]{:S(2)}) collective-permute-start(bf16[192,512]{1,0:T(8,128)(2,1)S(1)} %shard_map.91.refs_0_), channel_id=1, source_target_pairs={{0,4},{4,8},{8,12},{12,0},{1,5},{5,9},{9,13},{13,1},{2,6},{6,10},{... | collective-permute-start | bytes 589832 | tf_op jit(solution)/shard_map/ppermute | solution.py:23
  8.0 15.7 %collective-permute-start.3 = (bf16[4,2,32,512]{3,2,1,0:T(8,128)(2,1)}, bf16[4,2,32,512]{3,2,1,0:T(8,128)(2,1)S(1)}, u32[]{:S(2)}, u32[]{:S(2)}) collective-permute-start(bf16[4,2,32,512]{3,2,1,0:T(8,128)(2,1)} %bitcast.3.adapters_ref), channel_id=1, source_target_pairs={{0,2},{1,3},{2,0},{3,1},{4,6},{5,7},{6,4},{7,5},{8,10},{9,11},{10,... | collective-permute-start | bytes 786440 | tf_op jit(solution)/shard_map/ppermute | solution.py:27
  24.4 14.3 %collective-permute-start.4 = (bf16[10,32,512]{2,1,0:T(8,128)(2,1)S(1)}, bf16[10,32,512]{2,1,0:T(8,128)(2,1)S(1)}, u32[]{:S(2)}, u32[]{:S(2)}) collective-permute-start(bf16[10,32,512]{2,1,0:T(8,128)(2,1)S(1)} %get-tuple-element.57), channel_id=1, source_target_pairs={{0,2},{1,3},{2,0},{3,1},{4,6},{5,7},{6,4},{7,5},{8,10},{9,11},{10,... | collective-permute-start | bytes 983048 | tf_op jit(solution)/shard_map/ppermute | solution.py:27
  25.9 10.4 %collective-permute-start.6 = (bf16[448,256]{1,0:T(8,128)(2,1)S(1)}, bf16[448,256]{1,0:T(8,128)(2,1)S(1)}, u32[]{:S(2)}, u32[]{:S(2)}) collective-permute-start(bf16[448,256]{1,0:T(8,128)(2,1)S(1)} %get-tuple-element.58), channel_id=1, source_target_pairs={{0,4},{4,8},{8,12},{12,0},{1,5},{5,9},{9,13},{13,1},{2,6},{6,10},{... | collective-permute-start | bytes 688136 | tf_op jit(solution)/shard_map/ppermute | solution.py:23
  26.8 11.8 %collective-permute-start.7 = (bf16[448,256]{1,0:T(8,128)(2,1)S(1)}, bf16[448,256]{1,0:T(8,128)(2,1)S(1)}, u32[]{:S(2)}, u32[]{:S(2)}) collective-permute-start(bf16[448,256]{1,0:T(8,128)(2,1)S(1)} %get-tuple-element.59), channel_id=1, source_target_pairs={{0,12},{4,0},{8,4},{12,8},{1,13},{5,1},{9,5},{13,9},{2,14},{6,2},{... | collective-permute-start | bytes 688136 | tf_op jit(solution)/shard_map/ppermute | solution.py:23
  29.7 5.7 %collective-permute-start.5 = (bf16[6,32,512]{2,1,0:T(8,128)(2,1)S(1)}, bf16[6,32,512]{2,1,0:T(8,128)(2,1)S(1)}, u32[]{:S(2)}, u32[]{:S(2)}) collective-permute-start(bf16[6,32,512]{2,1,0:T(8,128)(2,1)S(1)} %get-tuple-element.56.refs_2_), channel_id=1, source_target_pairs={{0,16},{16,0},{1,17},{17,1},{2,18},{18,2},{3,19},{19,3},{4,20},{20... | collective-permute-start | bytes 589832 | tf_op jit(solution)/shard_map/ppermute | solution.py:31
  39.7 9.3 %collective-permute-start.10 = (bf16[32,32,512]{2,1,0:T(8,128)(2,1)S(1)}, bf16[32,32,512]{2,1,0:T(8,128)(2,1)S(1)}, u32[]{:S(2)}, u32[]{:S(2)}) collective-permute-start(bf16[32,32,512]{2,1,0:T(8,128)(2,1)S(1)} %shard_map.94.refs_0_), channel_id=1, source_target_pairs={{0,1},{1,0},{2,3},{3,2},{4,5},{5,4},{6,7},{7,6},{8,9},{9,8},{10,11... | collective-permute-start | bytes 3145736 | tf_op jit(solution)/shard_map/ppermute | solution.py:27
  46.3 9.3 %collective-permute-start.15 = (bf16[6,32,512]{2,1,0:T(8,128)(2,1)S(1)}, bf16[6,32,512]{2,1,0:T(8,128)(2,1)S(1)}, u32[]{:S(2)}, u32[]{:S(2)}) collective-permute-start(bf16[6,32,512]{2,1,0:T(8,128)(2,1)S(1)} %get-tuple-element.66.refs_2_), channel_id=1, source_target_pairs={{0,16},{16,0},{1,17},{17,1},{2,18},{18,2},{3,19},{19,3},{4,20},{20... | collective-permute-start | bytes 589832 | tf_op jit(solution)/shard_map/ppermute | solution.py:31
  46.8 8.8 %collective-permute-start.14 = (bf16[6,32,512]{2,1,0:T(8,128)(2,1)S(1)}, bf16[6,32,512]{2,1,0:T(8,128)(2,1)S(1)}, u32[]{:S(2)}, u32[]{:S(2)}) collective-permute-start(bf16[6,32,512]{2,1,0:T(8,128)(2,1)S(1)} %get-tuple-element.66.refs_2_), channel_id=1, source_target_pairs={{0,2},{1,3},{2,0},{3,1},{4,6},{5,7},{6,4},{7,5},{8,10},{9,11},{10,... | collective-permute-start | bytes 589832 | tf_op jit(solution)/shard_map/ppermute | solution.py:27
  47.4 8.2 %collective-permute-start.13 = (bf16[192,256]{1,0:T(8,128)(2,1)S(1)}, bf16[192,256]{1,0:T(8,128)(2,1)S(1)}, u32[]{:S(2)}, u32[]{:S(2)}) collective-permute-start(bf16[192,256]{1,0:T(8,128)(2,1)S(1)} %slice.47), channel_id=1, source_target_pairs={{0,8},{4,12},{8,0},{12,4},{1,9},{5,13},{9,1},{13,5},{2,10},{6,14},... | collective-permute-start | bytes 294920 | tf_op jit(solution)/shard_map/ppermute | solution.py:23
  58.3 13.5 %collective-permute-start.24 = (bf16[26,32,512]{2,1,0:T(8,128)(2,1)S(1)}, bf16[26,32,512]{2,1,0:T(8,128)(2,1)S(1)}, u32[]{:S(2)}, u32[]{:S(2)}) collective-permute-start(bf16[26,32,512]{2,1,0:T(8,128)(2,1)S(1)} %shard_map.97.refs_0_), channel_id=1, source_target_pairs={{0,1},{1,0},{2,3},{3,2},{4,5},{5,4},{6,7},{7,6},{8,9},{9,8},{10,11... | collective-permute-start | bytes 2555912 | tf_op jit(solution)/shard_map/ppermute | solution.py:27
  58.5 9.5 %collective-permute-start.18 = (bf16[256,256]{1,0:T(8,128)(2,1)S(1)}, bf16[256,256]{1,0:T(8,128)(2,1)S(1)}, u32[]{:S(2)}, u32[]{:S(2)}) collective-permute-start(bf16[256,256]{1,0:T(8,128)(2,1)S(1)} %slice.48), channel_id=1, source_target_pairs={{0,8},{4,12},{8,0},{12,4},{1,9},{5,13},{9,1},{13,5},{2,10},{6,14},... | collective-permute-start | bytes 393224 | tf_op jit(solution)/shard_map/ppermute | solution.py:23
  59.9 5.6 %collective-permute-start.22 = (bf16[3,32,512]{2,1,0:T(8,128)(2,1)S(1)}, bf16[3,32,512]{2,1,0:T(8,128)(2,1)S(1)}, u32[]{:S(2)}, u32[]{:S(2)}) collective-permute-start(bf16[3,32,512]{2,1,0:T(8,128)(2,1)S(1)} %slice.55), channel_id=1, source_target_pairs={{0,2},{1,3},{2,0},{3,1},{4,6},{5,7},{6,4},{7,5},{8,10},{9,11},{10,... | collective-permute-start | bytes 294920 | tf_op jit(solution)/shard_map/ppermute | solution.py:27
  61.5 6.5 %collective-permute-start.17 = (f32[16,2048]{1,0:T(8,128)S(1)}, f32[16,2048]{1,0:T(8,128)S(1)}, u32[]{:S(2)}, u32[]{:S(2)}) collective-permute-start(f32[16,2048]{1,0:T(8,128)S(1)} %get-tuple-element.79), channel_id=1, source_target_pairs={{0,2},{1,3},{2,0},{3,1},{4,6},{5,7},{6,4},{7,5},{8,10},{9,11},{10,... | collective-permute-start | bytes 393224 | tf_op jit(solution)/shard_map/ppermute | solution.py:27
  65.5 6.1 %collective-permute-start.25 = (bf16[3,32,512]{2,1,0:T(8,128)(2,1)S(1)}, bf16[3,32,512]{2,1,0:T(8,128)(2,1)S(1)}, u32[]{:S(2)}, u32[]{:S(2)}) collective-permute-start(bf16[3,32,512]{2,1,0:T(8,128)(2,1)S(1)} %collective-permute-done.22.refs_1_), channel_id=1, source_target_pairs={{0,1},{1,0},{2,3},{3,2},{4,5},{5,4},{6,7},{7,6},{8,9},{9,8},{10,11... | collective-permute-start | bytes 294920 | tf_op jit(solution)/shard_map/ppermute | solution.py:27
  69.9 7.6 %collective-permute-start.21 = (bf16[16,2048]{1,0:T(8,128)(2,1)S(1)}, bf16[16,2048]{1,0:T(8,128)(2,1)S(1)}, u32[]{:S(2)}, u32[]{:S(2)}) collective-permute-start(bf16[16,2048]{1,0:T(8,128)(2,1)S(1)} %shard_map.96.a0), channel_id=1, source_target_pairs={{0,3},{1,2},{2,1},{3,0},{4,7},{5,6},{6,5},{7,4},{8,11},{9,10},{10,... | collective-permute-start | bytes 196616 | tf_op jit(solution)/shard_map/ppermute | solution.py:27
  71.1 6.4 %collective-permute-start.20 = (bf16[16,2048]{1,0:T(8,128)(2,1)S(1)}, bf16[16,2048]{1,0:T(8,128)(2,1)S(1)}, u32[]{:S(2)}, u32[]{:S(2)}) collective-permute-start(bf16[16,2048]{1,0:T(8,128)(2,1)S(1)} %shard_map.96.a0), channel_id=1, source_target_pairs={{0,2},{1,3},{2,0},{3,1},{4,6},{5,7},{6,4},{7,5},{8,10},{9,11},{10,... | collective-permute-start | bytes 196616 | tf_op jit(solution)/shard_map/ppermute | solution.py:27
  71.6 5.9 %collective-permute-start.19 = (bf16[16,2048]{1,0:T(8,128)(2,1)S(1)}, bf16[16,2048]{1,0:T(8,128)(2,1)S(1)}, u32[]{:S(2)}, u32[]{:S(2)}) collective-permute-start(bf16[16,2048]{1,0:T(8,128)(2,1)S(1)} %shard_map.96.a0), channel_id=1, source_target_pairs={{0,1},{1,0},{2,3},{3,2},{4,5},{5,4},{6,7},{7,6},{8,9},{9,8},{10,11... | collective-permute-start | bytes 196616 | tf_op jit(solution)/shard_map/ppermute | solution.py:27
  79.1 19.8 %collective-permute-start.27 = (f32[16,2048]{1,0:T(8,128)S(1)}, f32[16,2048]{1,0:T(8,128)S(1)}, u32[]{:S(2)}, u32[]{:S(2)}) collective-permute-start(f32[16,2048]{1,0:T(8,128)S(1)} %get-tuple-element.77), channel_id=1, source_target_pairs={{0,0},{1,4},{2,8},{3,12},{4,1},{5,5},{6,9},{7,13},{8,2},{9,6},{10,... | collective-permute-start | bytes 393224 | tf_op jit(solution)/shard_map/ppermute | solution.py:36
  79.8 6.7 %collective-permute-start.28 = (bf16[16,2048]{1,0:T(8,128)(2,1)S(1)}, bf16[16,2048]{1,0:T(8,128)(2,1)S(1)}, u32[]{:S(2)}, u32[]{:S(2)}) collective-permute-start(bf16[16,2048]{1,0:T(8,128)(2,1)S(1)} %get-tuple-element.83), channel_id=1, source_target_pairs={{0,1},{1,5},{2,9},{3,13},{4,0},{5,4},{6,8},{7,12},{8,3},{9,7},{10,... | collective-permute-start | bytes 196616 | tf_op jit(solution)/shard_map/ppermute | solution.py:36
  81.8 10.1 %collective-permute-start.30 = (bf16[16,2048]{1,0:T(8,128)(2,1)S(1)}, bf16[16,2048]{1,0:T(8,128)(2,1)S(1)}, u32[]{:S(2)}, u32[]{:S(2)}) collective-permute-start(bf16[16,2048]{1,0:T(8,128)(2,1)S(1)} %get-tuple-element.84), channel_id=1, source_target_pairs={{0,3},{1,7},{2,11},{3,15},{4,2},{5,6},{6,10},{7,14},{8,1},{9,5},{1... | collective-permute-start | bytes 196616 | tf_op jit(solution)/shard_map/ppermute | solution.py:36
  85.5 13.5 %collective-permute-start.29 = (bf16[16,2048]{1,0:T(8,128)(2,1)S(1)}, bf16[16,2048]{1,0:T(8,128)(2,1)S(1)}, u32[]{:S(2)}, u32[]{:S(2)}) collective-permute-start(bf16[16,2048]{1,0:T(8,128)(2,1)S(1)} %get-tuple-element.85), channel_id=1, source_target_pairs={{0,2},{1,6},{2,10},{3,14},{4,3},{5,7},{6,11},{7,15},{8,0},{9,4},{1... | collective-permute-start | bytes 196616 | tf_op jit(solution)/shard_map/ppermute | solution.py:36
  (10 other events, 44.4 us)

commit v4 on v3

--- a/solution.py
+++ b/solution.py
@@ -69,15 +69,43 @@
     )(scalars, *arrays)
 
 
-def first_kernel(y_ref, adapters_ref, tokens_ref, out_ref):
+def first_kernel(y_ref, adapters_ref, tokens_ref, out_ref, held_ref, sem):
     half = adapters_ref.shape[2]
     width = out_ref.shape[1]
-    rows = tokens_ref.shape[0]
+    steps, seqs, depth = tokens_ref.shape
+    rows = steps * seqs
+    copies = [pltpu.make_async_copy(tokens_ref, held_ref, sem.at[4])]
     for f in range(4):
-        out_ref[f * half : (f + 1) * half] = adapters_ref[f, y_ref[0]]
-    for j in range(tokens_ref.shape[1] // width):
+        copies.append(
+            pltpu.make_async_copy(
+                adapters_ref.at[f, y_ref[0]], out_ref.at[pl.ds(f * half, half)], sem.at[f]
+            )
+        )
+    for copy in copies:
+        copy.start()
+    copies[0].wait()
+    flat_rows = jnp.concatenate([held_ref[s].astype(F32) for s in range(steps)], axis=0)
+    for j in range(depth // width):
         at = 4 * half + j * rows
-        out_ref[at : at + rows] = tokens_ref[:, j * width : (j + 1) * width]
+        out_ref[at : at + rows] = flat_rows[:, j * width : (j + 1) * width].astype(BF16)
+    for copy in copies[1:]:
+        copy.wait()
+
+
+def first_call(y, halves, tokens, out_shape):
+    any_spec = pl.BlockSpec(memory_space=pl.ANY)
+    return pl.pallas_call(
+        first_kernel,
+        out_shape=out_shape,
+        in_specs=[pl.BlockSpec(memory_space=pltpu.SMEM), any_spec, any_spec],
+        out_specs=pl.BlockSpec(memory_space=pltpu.VMEM),
+        scratch_shapes=[pltpu.VMEM(tokens.shape, BF16), pltpu.SemaphoreType.DMA((5,))],
+        compiler_params=pltpu.CompilerParams(vmem_limit_bytes=4 * MIB),
+    )(
+        y,
+        pltpu.with_memory_space_constraint(halves, pltpu.HBM),
+        pltpu.with_memory_space_constraint(tokens, pltpu.HBM),
+    )
 
 
 def sort_kernel(from_ref, *refs):
@@ -556,7 +584,7 @@
 
     width = adapters.shape[2]
     slab = rows * feat_dev // width
-    payload = small_call(first_kernel, y.reshape(1), [halves, own], shaped(2 * rank + slab, width))
+    payload = first_call(y.reshape(1), halves, tokens, shaped(2 * rank + slab, width))
     held = [payload] + [along_tp(payload, k) for k in range(1, SIDE)]
     halves_far = across_dp(after(halves, payload), 2)
 

time: 100 us -> 97.1 us (0.971)
  Pallas kernels: 23.6 us -> 21.7 us
    pallas_call x2, Pallas kernels: 2.02 us -> 0.12 us  [pack(): pl.pallas_call(functools.partial(pack_kernel, spans), out_shape=jax.Shape...]
  transfers between devices with their start and end apart: 31 -> 31, of which waited for: 14 -> 14; matrix products, arithmetic and copies ran while one was open for 1% -> 2% of each run, Pallas kernels for 18% -> 19%
where the time goes in v4:
time: 97.1 us; the launch traced here: 96.9 us
  waiting for transfers between devices  37 us (38%)
  starting transfers between devices  33.1 us (34%)
  Pallas kernels  21.7 us (22%)
  local copies, waits for them, and re-layouts  3.76 us (4%)
  other arithmetic  1.06 us (1%)
    ppermute x4, waiting for transfers between devices, to_holder(): return lax.ppermute(x, ('tp', 'dp'), pairs)  13.5 us
    ppermute x7, starting transfers between devices, along_tp(): return lax.ppermute(x, 'tp', [(i, (i + k) % SIDE) for i in range(SIDE)])  12.9 us
    pallas_call x2, Pallas kernels, merge_call(): pl.pallas_call(kernel, out_shape=out_shape, in_specs=[pl.BlockSpec(memory...  12.1 us
    ppermute x7, waiting for transfers between devices, along_tp(): return lax.ppermute(x, 'tp', [(i, (i + k) % SIDE) for i in range(SIDE)])  10.4 us
    ppermute x16, starting transfers between devices, across_dp(): return lax.ppermute(x, 'dp', [(i, i ^ k) for i in range(SIDE)])  8.73 us
    ppermute x4, waiting for transfers between devices, across_groups(): return lax.ppermute(x, 'groups', [(0, 1), (1, 0)])  8.47 us
    ppermute x4, starting transfers between devices, to_holder(): return lax.ppermute(x, ('tp', 'dp'), pairs)  6.33 us
    ppermute x4, starting transfers between devices, across_groups(): return lax.ppermute(x, 'groups', [(0, 1), (1, 0)])  5.19 us
  transfers between devices with their start and end apart: 31, of which 14 were waited for; matrix products, arithmetic and copies ran while one was open for 2% of the time, Pallas kernels for 19%

profile of v4, /device:TPU:0, one launch (start us, length us, event | category | flops | bytes accessed | tf_op | source)
XLA Modules:
  0.0 96.9 jit_solution(14681707322008767277)
XLA Ops:
  1.0 5.1 %collective-permute-start.2 = (bf16[192,512]{1,0:T(8,128)(2,1)S(1)}, bf16[192,512]{1,0:T(8,128)(2,1)S(1)}, u32[]{:S(2)}, u32[]{:S(2)}) collective-permute-start(bf16[192,512]{1,0:T(8,128)(2,1)S(1)} %shard_map.91.refs_0_), channel_id=1, source_target_pairs={{0,12},{4,0},{8,4},{12,8},{1,13},{5,1},{9,5},{13,9},{2,14},{6,2},{... | collective-permute-start | bytes 589832 | tf_op jit(solution)/shard_map/ppermute | solution.py:23
  7.1 1.5 %collective-permute-start.3 = (bf16[4,2,32,512]{3,2,1,0:T(8,128)(2,1)}, bf16[4,2,32,512]{3,2,1,0:T(8,128)(2,1)S(1)}, u32[]{:S(2)}, u32[]{:S(2)}) collective-permute-start(bf16[4,2,32,512]{3,2,1,0:T(8,128)(2,1)} %bitcast.14), channel_id=1, source_target_pairs={{0,2},{1,3},{2,0},{3,1},{4,6},{5,7},{6,4},{7,5},{8,10},{9,11},{10,... | collective-permute-start | bytes 786440 | tf_op jit(solution)/shard_map/ppermute | solution.py:27
  12.5 4.3 %shard_map.92 = (bf16[448,256]{1,0:T(8,128)(2,1)S(1)}, bf16[448,256]{1,0:T(8,128)(2,1)S(1)}, bf16[448,256]{1,0:T(8,128)(2,1)S(1)}, bf16[448,256]{1,0:T(8,128)(2,1)S(1)}) custom-call(s32[4]{0:T(128)S(1)} %and_select_fusion.heads_ref, bf16[16,2048]{1,0:T(8,128)(2,1)S(1)} %reshape.26.tokens_ref, bf16[192,1024]{1,0:T(8,128)(2,1)S(1)} %bitcast.19, ...), custom_call_target="tpu_custom_call" | custom-call | flops 134217728 | bytes 16777216 | tf_op jit(solution)/shard_map/pallas_call | solution.py:166
  16.9 5.9 %collective-permute-done.1.refs_2_ = bf16[192,512]{1,0:T(8,128)(2,1)S(1)} collective-permute-done((bf16[192,512]{1,0:T(8,128)(2,1)S(1)}, bf16[192,512]{1,0:T(8,128)(2,1)S(1)}, u32[]{:S(2)}, u32[]{:S(2)}) %collective-permute-start.1) | collective-permute-done | bytes 196640 | tf_op jit(solution)/shard_map/ppermute | solution.py:23
  23.5 1.6 %collective-permute-start.4 = (bf16[10,32,512]{2,1,0:T(8,128)(2,1)S(1)}, bf16[10,32,512]{2,1,0:T(8,128)(2,1)S(1)}, u32[]{:S(2)}, u32[]{:S(2)}) collective-permute-start(bf16[10,32,512]{2,1,0:T(8,128)(2,1)S(1)} %get-tuple-element.57), channel_id=1, source_target_pairs={{0,2},{1,3},{2,0},{3,1},{4,6},{5,7},{6,4},{7,5},{8,10},{9,11},{10,... | collective-permute-start | bytes 983048 | tf_op jit(solution)/shard_map/ppermute | solution.py:27
  25.9 2.9 %collective-permute-start.7 = (bf16[448,256]{1,0:T(8,128)(2,1)S(1)}, bf16[448,256]{1,0:T(8,128)(2,1)S(1)}, u32[]{:S(2)}, u32[]{:S(2)}) collective-permute-start(bf16[448,256]{1,0:T(8,128)(2,1)S(1)} %get-tuple-element.59), channel_id=1, source_target_pairs={{0,12},{4,0},{8,4},{12,8},{1,13},{5,1},{9,5},{13,9},{2,14},{6,2},{... | collective-permute-start | bytes 688136 | tf_op jit(solution)/shard_map/ppermute | solution.py:23
  28.9 1.5 %collective-permute-start.5 = (bf16[6,32,512]{2,1,0:T(8,128)(2,1)S(1)}, bf16[6,32,512]{2,1,0:T(8,128)(2,1)S(1)}, u32[]{:S(2)}, u32[]{:S(2)}) collective-permute-start(bf16[6,32,512]{2,1,0:T(8,128)(2,1)S(1)} %get-tuple-element.56.refs_2_), channel_id=1, source_target_pairs={{0,16},{16,0},{1,17},{17,1},{2,18},{18,2},{3,19},{19,3},{4,20},{20... | collective-permute-start | bytes 589832 | tf_op jit(solution)/shard_map/ppermute | solution.py:31
  30.4 4.2 %collective-permute-done.5.refs_4_ = bf16[6,32,512]{2,1,0:T(8,128)(2,1)S(1)} collective-permute-done((bf16[6,32,512]{2,1,0:T(8,128)(2,1)S(1)}, bf16[6,32,512]{2,1,0:T(8,128)(2,1)S(1)}, u32[]{:S(2)}, u32[]{:S(2)}) %collective-permute-start.5) | collective-permute-done | bytes 196640 | tf_op jit(solution)/shard_map/ppermute | solution.py:31
  35.4 2.3 %collective-permute-done.7.c3 = bf16[448,256]{1,0:T(8,128)(2,1)S(1)} collective-permute-done((bf16[448,256]{1,0:T(8,128)(2,1)S(1)}, bf16[448,256]{1,0:T(8,128)(2,1)S(1)}, u32[]{:S(2)}, u32[]{:S(2)}) %collective-permute-start.7) | collective-permute-done | bytes 229408 | tf_op jit(solution)/shard_map/ppermute | solution.py:23
  37.9 1.6 %collective-permute-start.9 = (bf16[3,32,512]{2,1,0:T(8,128)(2,1)S(1)}, bf16[3,32,512]{2,1,0:T(8,128)(2,1)S(1)}, u32[]{:S(2)}, u32[]{:S(2)}) collective-permute-start(bf16[3,32,512]{2,1,0:T(8,128)(2,1)S(1)} %slice.46), channel_id=1, source_target_pairs={{0,16},{16,0},{1,17},{17,1},{2,18},{18,2},{3,19},{19,3},{4,20},{20... | collective-permute-start | bytes 294920 | tf_op jit(solution)/shard_map/ppermute | solution.py:31
  40.1 3.1 %collective-permute-done.9.refs_2_ = bf16[3,32,512]{2,1,0:T(8,128)(2,1)S(1)} collective-permute-done((bf16[3,32,512]{2,1,0:T(8,128)(2,1)S(1)}, bf16[3,32,512]{2,1,0:T(8,128)(2,1)S(1)}, u32[]{:S(2)}, u32[]{:S(2)}) %collective-permute-start.9) | collective-permute-done | bytes 98336 | tf_op jit(solution)/shard_map/ppermute | solution.py:31
  45.6 1.5 %collective-permute-start.13 = (bf16[192,256]{1,0:T(8,128)(2,1)S(1)}, bf16[192,256]{1,0:T(8,128)(2,1)S(1)}, u32[]{:S(2)}, u32[]{:S(2)}) collective-permute-start(bf16[192,256]{1,0:T(8,128)(2,1)S(1)} %slice.47), channel_id=1, source_target_pairs={{0,8},{4,12},{8,0},{12,4},{1,9},{5,13},{9,1},{13,5},{2,10},{6,14},... | collective-permute-start | bytes 294920 | tf_op jit(solution)/shard_map/ppermute | solution.py:23
  47.2 6.5 %shard_map.95 = f32[64,2048]{1,0:T(8,128)S(1)} custom-call(s32[18]{0:T(128)S(1)} %concatenate.13.slots_ref, bf16[32,32,512]{2,1,0:T(8,128)(2,1)S(1)} %shard_map.94.refs_0_, bf16[3,32,512]{2,1,0:T(8,128)(2,1)S(1)} %collective-permute-done.8.refs_1_, bf16[3,32,512]{2,1,0:T(8,128)(2,1)S(1)} %collective-permute-done.9.refs_2_, ...), custom_call_target="tpu_custom_call" | custom-call | tf_op jit(solution)/shard_map/pallas_call | solution.py:324
  54.0 1.5 %collective-permute-done.16 = f32[32,2048]{1,0:T(8,128)S(1)} collective-permute-done((f32[32,2048]{1,0:T(8,128)S(1)}, f32[32,2048]{1,0:T(8,128)S(1)}, u32[]{:S(2)}, u32[]{:S(2)}) %collective-permute-start.16) | collective-permute-done | bytes 262176 | tf_op jit(solution)/shard_map/ppermute | solution.py:27
  57.2 1.6 %collective-permute-start.22 = (bf16[3,32,512]{2,1,0:T(8,128)(2,1)S(1)}, bf16[3,32,512]{2,1,0:T(8,128)(2,1)S(1)}, u32[]{:S(2)}, u32[]{:S(2)}) collective-permute-start(bf16[3,32,512]{2,1,0:T(8,128)(2,1)S(1)} %slice.55), channel_id=1, source_target_pairs={{0,2},{1,3},{2,0},{3,1},{4,6},{5,7},{6,4},{7,5},{8,10},{9,11},{10,... | collective-permute-start | bytes 294920 | tf_op jit(solution)/shard_map/ppermute | solution.py:27
  59.4 1.6 %collective-permute-start.23 = (bf16[3,32,512]{2,1,0:T(8,128)(2,1)S(1)}, bf16[3,32,512]{2,1,0:T(8,128)(2,1)S(1)}, u32[]{:S(2)}, u32[]{:S(2)}) collective-permute-start(bf16[3,32,512]{2,1,0:T(8,128)(2,1)S(1)} %slice.56), channel_id=1, source_target_pairs={{0,16},{16,0},{1,17},{17,1},{2,18},{18,2},{3,19},{19,3},{4,20},{20... | collective-permute-start | bytes 294920 | tf_op jit(solution)/shard_map/ppermute | solution.py:31
  60.9 1.8 %collective-permute-done.22.refs_1_ = bf16[3,32,512]{2,1,0:T(8,128)(2,1)S(1)} collective-permute-done((bf16[3,32,512]{2,1,0:T(8,128)(2,1)S(1)}, bf16[3,32,512]{2,1,0:T(8,128)(2,1)S(1)}, u32[]{:S(2)}, u32[]{:S(2)}) %collective-permute-start.22) | collective-permute-done | bytes 98336 | tf_op jit(solution)/shard_map/ppermute | solution.py:27
  65.2 1.9 %shard_map.96.a0 = bf16[16,2048]{1,0:T(8,128)(2,1)S(1)} custom-call(s32[8]{0:T(128)S(1)} %pad_add_fusion.spots_ref, f32[16,2048]{1,0:T(8,128)S(1)} %get-tuple-element.80.qa_ref, f32[16,2048]{1,0:T(8,128)S(1)} %collective-permute-done.17.qb_ref, bf16[448,256]{1,0:T(8,128)(2,1)S(1)} %get-tuple-element.48.c0, bf16[448,256]{1,0:T(8,128)(2,1)S(1)} %collective-permute-done.6.c1, ...), custom_call_target="tpu_custom_call" | custom-call | tf_op jit(solution)/shard_map/pallas_call | solution.py:657
  69.1 5.6 %shard_map.98.w_ref = bf16[2048,2048]{1,0:T(8,128)(2,1)S(1)} custom-call(s32[18]{0:T(128)S(1)} %concatenate.14.slots_ref, bf16[26,32,512]{2,1,0:T(8,128)(2,1)S(1)} %shard_map.97.refs_0_, bf16[3,32,512]{2,1,0:T(8,128)(2,1)S(1)} %collective-permute-done.22.refs_1_, bf16[3,32,512]{2,1,0:T(8,128)(2,1)S(1)} %collective-permute-done.23.refs_2_, ...), custom_call_target="tpu_custom_call" | custom-call | bytes 16777216 | tf_op jit(solution)/shard_map/pallas_call | solution.py:324
  74.8 1.6 %shard_map.99 = (f32[16,2048]{1,0:T(8,128)S(1)}, bf16[3,16,2048]{2,1,0:T(8,128)(2,1)S(1)}) custom-call(s32[1]{0:T(128)} %bitcast.turn_ref, bf16[16,2048]{1,0:T(8,128)(2,1)S(1)} %shard_map.96.a0, bf16[16,2048]{1,0:T(8,128)(2,1)S(1)} %collective-permute-done.19.a1, bf16[16,2048]{1,0:T(8,128)(2,1)S(1)} %collective-permute-done.20.a2, ...), custom_call_target="tpu_custom_call" | custom-call | tf_op jit(solution)/shard_map/pallas_call | solution.py:678
  77.1 1.9 %collective-permute-start.28 = (bf16[16,2048]{1,0:T(8,128)(2,1)S(1)}, bf16[16,2048]{1,0:T(8,128)(2,1)S(1)}, u32[]{:S(2)}, u32[]{:S(2)}) collective-permute-start(bf16[16,2048]{1,0:T(8,128)(2,1)S(1)} %get-tuple-element.83), channel_id=1, source_target_pairs={{0,1},{1,5},{2,9},{3,13},{4,0},{5,4},{6,8},{7,12},{8,3},{9,7},{10,... | collective-permute-start | bytes 196616 | tf_op jit(solution)/shard_map/ppermute | solution.py:36
  79.0 3.7 %collective-permute-start.30 = (bf16[16,2048]{1,0:T(8,128)(2,1)S(1)}, bf16[16,2048]{1,0:T(8,128)(2,1)S(1)}, u32[]{:S(2)}, u32[]{:S(2)}) collective-permute-start(bf16[16,2048]{1,0:T(8,128)(2,1)S(1)} %get-tuple-element.84), channel_id=1, source_target_pairs={{0,3},{1,7},{2,11},{3,15},{4,2},{5,6},{6,10},{7,14},{8,1},{9,5},{1... | collective-permute-start | bytes 196616 | tf_op jit(solution)/shard_map/ppermute | solution.py:36
  83.8 5.3 %collective-permute-done.30 = bf16[16,2048]{1,0:T(8,128)(2,1)S(1)} collective-permute-done((bf16[16,2048]{1,0:T(8,128)(2,1)S(1)}, bf16[16,2048]{1,0:T(8,128)(2,1)S(1)}, u32[]{:S(2)}, u32[]{:S(2)}) %collective-permute-start.30) | collective-permute-done | bytes 65568 | tf_op jit(solution)/shard_map/ppermute | solution.py:36
  89.1 7.1 %collective-permute-done.29 = bf16[16,2048]{1,0:T(8,128)(2,1)S(1)} collective-permute-done((bf16[16,2048]{1,0:T(8,128)(2,1)S(1)}, bf16[16,2048]{1,0:T(8,128)(2,1)S(1)}, u32[]{:S(2)}, u32[]{:S(2)}) %collective-permute-start.29) | collective-permute-done | bytes 65568 | tf_op jit(solution)/shard_map/ppermute | solution.py:36
  (75 shorter events, 21.1 us)
Async XLA Ops:
  1.0 15.9 %collective-permute-start.2 = (bf16[192,512]{1,0:T(8,128)(2,1)S(1)}, bf16[192,512]{1,0:T(8,128)(2,1)S(1)}, u32[]{:S(2)}, u32[]{:S(2)}) collective-permute-start(bf16[192,512]{1,0:T(8,128)(2,1)S(1)} %shard_map.91.refs_0_), channel_id=1, source_target_pairs={{0,12},{4,0},{8,4},{12,8},{1,13},{5,1},{9,5},{13,9},{2,14},{6,2},{... | collective-permute-start | bytes 589832 | tf_op jit(solution)/shard_map/ppermute | solution.py:23
  6.1 16.7 %collective-permute-start.1 = (bf16[192,512]{1,0:T(8,128)(2,1)S(1)}, bf16[192,512]{1,0:T(8,128)(2,1)S(1)}, u32[]{:S(2)}, u32[]{:S(2)}) collective-permute-start(bf16[192,512]{1,0:T(8,128)(2,1)S(1)} %shard_map.91.refs_0_), channel_id=1, source_target_pairs={{0,8},{4,12},{8,0},{12,4},{1,9},{5,13},{9,1},{13,5},{2,10},{6,14},... | collective-permute-start | bytes 589832 | tf_op jit(solution)/shard_map/ppermute | solution.py:23
  6.1 16.7 %collective-permute-start = (bf16[192,512]{1,0:T(8,128)(2,1)S(1)}, bf16[192,512]{1,0:T(8,128)(2,1)S(1)}, u32[]{:S(2)}, u32[]{:S(2)}) collective-permute-start(bf16[192,512]{1,0:T(8,128)(2,1)S(1)} %shard_map.91.refs_0_), channel_id=1, source_target_pairs={{0,4},{4,8},{8,12},{12,0},{1,5},{5,9},{9,13},{13,1},{2,6},{6,10},{... | collective-permute-start | bytes 589832 | tf_op jit(solution)/shard_map/ppermute | solution.py:23
  7.1 15.7 %collective-permute-start.3 = (bf16[4,2,32,512]{3,2,1,0:T(8,128)(2,1)}, bf16[4,2,32,512]{3,2,1,0:T(8,128)(2,1)S(1)}, u32[]{:S(2)}, u32[]{:S(2)}) collective-permute-start(bf16[4,2,32,512]{3,2,1,0:T(8,128)(2,1)} %bitcast.14), channel_id=1, source_target_pairs={{0,2},{1,3},{2,0},{3,1},{4,6},{5,7},{6,4},{7,5},{8,10},{9,11},{10,... | collective-permute-start | bytes 786440 | tf_op jit(solution)/shard_map/ppermute | solution.py:27
  23.5 14.3 %collective-permute-start.4 = (bf16[10,32,512]{2,1,0:T(8,128)(2,1)S(1)}, bf16[10,32,512]{2,1,0:T(8,128)(2,1)S(1)}, u32[]{:S(2)}, u32[]{:S(2)}) collective-permute-start(bf16[10,32,512]{2,1,0:T(8,128)(2,1)S(1)} %get-tuple-element.57), channel_id=1, source_target_pairs={{0,2},{1,3},{2,0},{3,1},{4,6},{5,7},{6,4},{7,5},{8,10},{9,11},{10,... | collective-permute-start | bytes 983048 | tf_op jit(solution)/shard_map/ppermute | solution.py:27
  25.0 10.4 %collective-permute-start.6 = (bf16[448,256]{1,0:T(8,128)(2,1)S(1)}, bf16[448,256]{1,0:T(8,128)(2,1)S(1)}, u32[]{:S(2)}, u32[]{:S(2)}) collective-permute-start(bf16[448,256]{1,0:T(8,128)(2,1)S(1)} %get-tuple-element.58), channel_id=1, source_target_pairs={{0,4},{4,8},{8,12},{12,0},{1,5},{5,9},{9,13},{13,1},{2,6},{6,10},{... | collective-permute-start | bytes 688136 | tf_op jit(solution)/shard_map/ppermute | solution.py:23
  25.9 11.8 %collective-permute-start.7 = (bf16[448,256]{1,0:T(8,128)(2,1)S(1)}, bf16[448,256]{1,0:T(8,128)(2,1)S(1)}, u32[]{:S(2)}, u32[]{:S(2)}) collective-permute-start(bf16[448,256]{1,0:T(8,128)(2,1)S(1)} %get-tuple-element.59), channel_id=1, source_target_pairs={{0,12},{4,0},{8,4},{12,8},{1,13},{5,1},{9,5},{13,9},{2,14},{6,2},{... | collective-permute-start | bytes 688136 | tf_op jit(solution)/shard_map/ppermute | solution.py:23
  28.9 5.7 %collective-permute-start.5 = (bf16[6,32,512]{2,1,0:T(8,128)(2,1)S(1)}, bf16[6,32,512]{2,1,0:T(8,128)(2,1)S(1)}, u32[]{:S(2)}, u32[]{:S(2)}) collective-permute-start(bf16[6,32,512]{2,1,0:T(8,128)(2,1)S(1)} %get-tuple-element.56.refs_2_), channel_id=1, source_target_pairs={{0,16},{16,0},{1,17},{17,1},{2,18},{18,2},{3,19},{19,3},{4,20},{20... | collective-permute-start | bytes 589832 | tf_op jit(solution)/shard_map/ppermute | solution.py:31
  37.8 9.3 %collective-permute-start.10 = (bf16[32,32,512]{2,1,0:T(8,128)(2,1)S(1)}, bf16[32,32,512]{2,1,0:T(8,128)(2,1)S(1)}, u32[]{:S(2)}, u32[]{:S(2)}) collective-permute-start(bf16[32,32,512]{2,1,0:T(8,128)(2,1)S(1)} %shard_map.94.refs_0_), channel_id=1, source_target_pairs={{0,1},{1,0},{2,3},{3,2},{4,5},{5,4},{6,7},{7,6},{8,9},{9,8},{10,11... | collective-permute-start | bytes 3145736 | tf_op jit(solution)/shard_map/ppermute | solution.py:27
  44.5 9.3 %collective-permute-start.15 = (bf16[6,32,512]{2,1,0:T(8,128)(2,1)S(1)}, bf16[6,32,512]{2,1,0:T(8,128)(2,1)S(1)}, u32[]{:S(2)}, u32[]{:S(2)}) collective-permute-start(bf16[6,32,512]{2,1,0:T(8,128)(2,1)S(1)} %get-tuple-element.66.refs_2_), channel_id=1, source_target_pairs={{0,16},{16,0},{1,17},{17,1},{2,18},{18,2},{3,19},{19,3},{4,20},{20... | collective-permute-start | bytes 589832 | tf_op jit(solution)/shard_map/ppermute | solution.py:31
  45.0 8.8 %collective-permute-start.14 = (bf16[6,32,512]{2,1,0:T(8,128)(2,1)S(1)}, bf16[6,32,512]{2,1,0:T(8,128)(2,1)S(1)}, u32[]{:S(2)}, u32[]{:S(2)}) collective-permute-start(bf16[6,32,512]{2,1,0:T(8,128)(2,1)S(1)} %get-tuple-element.66.refs_2_), channel_id=1, source_target_pairs={{0,2},{1,3},{2,0},{3,1},{4,6},{5,7},{6,4},{7,5},{8,10},{9,11},{10,... | collective-permute-start | bytes 589832 | tf_op jit(solution)/shard_map/ppermute | solution.py:27
  45.6 8.2 %collective-permute-start.13 = (bf16[192,256]{1,0:T(8,128)(2,1)S(1)}, bf16[192,256]{1,0:T(8,128)(2,1)S(1)}, u32[]{:S(2)}, u32[]{:S(2)}) collective-permute-start(bf16[192,256]{1,0:T(8,128)(2,1)S(1)} %slice.47), channel_id=1, source_target_pairs={{0,8},{4,12},{8,0},{12,4},{1,9},{5,13},{9,1},{13,5},{2,10},{6,14},... | collective-permute-start | bytes 294920 | tf_op jit(solution)/shard_map/ppermute | solution.py:23
  55.6 13.5 %collective-permute-start.24 = (bf16[26,32,512]{2,1,0:T(8,128)(2,1)S(1)}, bf16[26,32,512]{2,1,0:T(8,128)(2,1)S(1)}, u32[]{:S(2)}, u32[]{:S(2)}) collective-permute-start(bf16[26,32,512]{2,1,0:T(8,128)(2,1)S(1)} %shard_map.97.refs_0_), channel_id=1, source_target_pairs={{0,1},{1,0},{2,3},{3,2},{4,5},{5,4},{6,7},{7,6},{8,9},{9,8},{10,11... | collective-permute-start | bytes 2555912 | tf_op jit(solution)/shard_map/ppermute | solution.py:27
  55.8 9.5 %collective-permute-start.18 = (bf16[256,256]{1,0:T(8,128)(2,1)S(1)}, bf16[256,256]{1,0:T(8,128)(2,1)S(1)}, u32[]{:S(2)}, u32[]{:S(2)}) collective-permute-start(bf16[256,256]{1,0:T(8,128)(2,1)S(1)} %slice.48), channel_id=1, source_target_pairs={{0,8},{4,12},{8,0},{12,4},{1,9},{5,13},{9,1},{13,5},{2,10},{6,14},... | collective-permute-start | bytes 393224 | tf_op jit(solution)/shard_map/ppermute | solution.py:23
  57.2 5.6 %collective-permute-start.22 = (bf16[3,32,512]{2,1,0:T(8,128)(2,1)S(1)}, bf16[3,32,512]{2,1,0:T(8,128)(2,1)S(1)}, u32[]{:S(2)}, u32[]{:S(2)}) collective-permute-start(bf16[3,32,512]{2,1,0:T(8,128)(2,1)S(1)} %slice.55), channel_id=1, source_target_pairs={{0,2},{1,3},{2,0},{3,1},{4,6},{5,7},{6,4},{7,5},{8,10},{9,11},{10,... | collective-permute-start | bytes 294920 | tf_op jit(solution)/shard_map/ppermute | solution.py:27
  58.8 6.5 %collective-permute-start.17 = (f32[16,2048]{1,0:T(8,128)S(1)}, f32[16,2048]{1,0:T(8,128)S(1)}, u32[]{:S(2)}, u32[]{:S(2)}) collective-permute-start(f32[16,2048]{1,0:T(8,128)S(1)} %get-tuple-element.79), channel_id=1, source_target_pairs={{0,2},{1,3},{2,0},{3,1},{4,6},{5,7},{6,4},{7,5},{8,10},{9,11},{10,... | collective-permute-start | bytes 393224 | tf_op jit(solution)/shard_map/ppermute | solution.py:27
  62.8 6.1 %collective-permute-start.25 = (bf16[3,32,512]{2,1,0:T(8,128)(2,1)S(1)}, bf16[3,32,512]{2,1,0:T(8,128)(2,1)S(1)}, u32[]{:S(2)}, u32[]{:S(2)}) collective-permute-start(bf16[3,32,512]{2,1,0:T(8,128)(2,1)S(1)} %collective-permute-done.22.refs_1_), channel_id=1, source_target_pairs={{0,1},{1,0},{2,3},{3,2},{4,5},{5,4},{6,7},{7,6},{8,9},{9,8},{10,11... | collective-permute-start | bytes 294920 | tf_op jit(solution)/shard_map/ppermute | solution.py:27
  67.2 7.6 %collective-permute-start.21 = (bf16[16,2048]{1,0:T(8,128)(2,1)S(1)}, bf16[16,2048]{1,0:T(8,128)(2,1)S(1)}, u32[]{:S(2)}, u32[]{:S(2)}) collective-permute-start(bf16[16,2048]{1,0:T(8,128)(2,1)S(1)} %shard_map.96.a0), channel_id=1, source_target_pairs={{0,3},{1,2},{2,1},{3,0},{4,7},{5,6},{6,5},{7,4},{8,11},{9,10},{10,... | collective-permute-start | bytes 196616 | tf_op jit(solution)/shard_map/ppermute | solution.py:27
  68.3 6.4 %collective-permute-start.20 = (bf16[16,2048]{1,0:T(8,128)(2,1)S(1)}, bf16[16,2048]{1,0:T(8,128)(2,1)S(1)}, u32[]{:S(2)}, u32[]{:S(2)}) collective-permute-start(bf16[16,2048]{1,0:T(8,128)(2,1)S(1)} %shard_map.96.a0), channel_id=1, source_target_pairs={{0,2},{1,3},{2,0},{3,1},{4,6},{5,7},{6,4},{7,5},{8,10},{9,11},{10,... | collective-permute-start | bytes 196616 | tf_op jit(solution)/shard_map/ppermute | solution.py:27
  68.9 5.9 %collective-permute-start.19 = (bf16[16,2048]{1,0:T(8,128)(2,1)S(1)}, bf16[16,2048]{1,0:T(8,128)(2,1)S(1)}, u32[]{:S(2)}, u32[]{:S(2)}) collective-permute-start(bf16[16,2048]{1,0:T(8,128)(2,1)S(1)} %shard_map.96.a0), channel_id=1, source_target_pairs={{0,1},{1,0},{2,3},{3,2},{4,5},{5,4},{6,7},{7,6},{8,9},{9,8},{10,11... | collective-permute-start | bytes 196616 | tf_op jit(solution)/shard_map/ppermute | solution.py:27
  76.4 19.8 %collective-permute-start.27 = (f32[16,2048]{1,0:T(8,128)S(1)}, f32[16,2048]{1,0:T(8,128)S(1)}, u32[]{:S(2)}, u32[]{:S(2)}) collective-permute-start(f32[16,2048]{1,0:T(8,128)S(1)} %get-tuple-element.77), channel_id=1, source_target_pairs={{0,0},{1,4},{2,8},{3,12},{4,1},{5,5},{6,9},{7,13},{8,2},{9,6},{10,... | collective-permute-start | bytes 393224 | tf_op jit(solution)/shard_map/ppermute | solution.py:36
  77.1 6.8 %collective-permute-start.28 = (bf16[16,2048]{1,0:T(8,128)(2,1)S(1)}, bf16[16,2048]{1,0:T(8,128)(2,1)S(1)}, u32[]{:S(2)}, u32[]{:S(2)}) collective-permute-start(bf16[16,2048]{1,0:T(8,128)(2,1)S(1)} %get-tuple-element.83), channel_id=1, source_target_pairs={{0,1},{1,5},{2,9},{3,13},{4,0},{5,4},{6,8},{7,12},{8,3},{9,7},{10,... | collective-permute-start | bytes 196616 | tf_op jit(solution)/shard_map/ppermute | solution.py:36
  79.0 10.1 %collective-permute-start.30 = (bf16[16,2048]{1,0:T(8,128)(2,1)S(1)}, bf16[16,2048]{1,0:T(8,128)(2,1)S(1)}, u32[]{:S(2)}, u32[]{:S(2)}) collective-permute-start(bf16[16,2048]{1,0:T(8,128)(2,1)S(1)} %get-tuple-element.84), channel_id=1, source_target_pairs={{0,3},{1,7},{2,11},{3,15},{4,2},{5,6},{6,10},{7,14},{8,1},{9,5},{1... | collective-permute-start | bytes 196616 | tf_op jit(solution)/shard_map/ppermute | solution.py:36
  82.7 13.5 %collective-permute-start.29 = (bf16[16,2048]{1,0:T(8,128)(2,1)S(1)}, bf16[16,2048]{1,0:T(8,128)(2,1)S(1)}, u32[]{:S(2)}, u32[]{:S(2)}) collective-permute-start(bf16[16,2048]{1,0:T(8,128)(2,1)S(1)} %get-tuple-element.85), channel_id=1, source_target_pairs={{0,2},{1,6},{2,10},{3,14},{4,3},{5,7},{6,11},{7,15},{8,0},{9,4},{1... | collective-permute-start | bytes 196616 | tf_op jit(solution)/shard_map/ppermute | solution.py:36
  (11 other events, 82.2 us)

commit v5 on v4

--- a/solution.py
+++ b/solution.py
@@ -335,29 +335,31 @@
     )(slots, *parts, weight, *pieces)
 
 
-def attention_kernel(seqs, spots_ref, qa_ref, qb_ref, c0, c1, c3, keys_ref, rest_ref, out_ref):
-    scale = HD ** (-0.5)
-    rows = qa_ref.shape[0]
-    kv_dev = c0.shape[1] // HD
-    group = qa_ref.shape[1] // HD // kv_dev
-    span = (c0.shape[0] - 4 * rows) // (2 * seqs)
-    cached = seqs * span
-    queries = (qa_ref[...] + qb_ref[...]).astype(BF16)
-
+def bias_kernel(seqs, spots_ref, bias_ref, fresh_ref):
+    rows, cached = bias_ref.shape[1:]
+    span = cached // seqs
     row_seq = lax.broadcasted_iota(jnp.int32, (rows, cached), 0) % seqs
     column = lax.broadcasted_iota(jnp.int32, (rows, cached), 1)
-    biases = []
     for k in range(SIDE):
         valid = column < 0
         for b in range(seqs):
             left = jnp.clip(spots_ref[SIDE + b] - spots_ref[k] * span, 0, span)
             inside = (column >= b * span) & (column < b * span + left)
             valid |= inside & (row_seq == b)
-        biases.append(jnp.where(valid, 0.0, -1e30))
+        bias_ref[k] = jnp.where(valid, 0.0, -1e30)
     row = lax.broadcasted_iota(jnp.int32, (rows, rows), 0)
     earlier = lax.broadcasted_iota(jnp.int32, (rows, rows), 1)
     causal = (earlier // seqs <= row // seqs) & (earlier % seqs == row % seqs)
-    fresh_bias = jnp.where(causal, 0.0, -1e30)
+    fresh_ref[...] = jnp.where(causal, 0.0, -1e30)
+
+
+def attention_kernel(bias_ref, fresh_ref, qa_ref, qb_ref, c0, c1, c3, keys_ref, rest_ref, out_ref):
+    scale = HD ** (-0.5)
+    rows = qa_ref.shape[0]
+    kv_dev = c0.shape[1] // HD
+    group = qa_ref.shape[1] // HD // kv_dev
+    cached = bias_ref.shape[2]
+    queries = (qa_ref[...] + qb_ref[...]).astype(BF16)
 
     def fresh_part(part):
         terms = []
@@ -387,8 +389,8 @@
         q = jnp.concatenate(
             [queries[:, (h * group + g) * HD : (h * group + g + 1) * HD] for g in range(group)], axis=0
         )
-        scores = [scores_of(q, c[:cached, lanes], biases[k]) for k, c in enumerate((c0, c1, keys_ref, c3))]
-        scores.append(scores_of(q, fresh_keys[:, lanes], fresh_bias))
+        scores = [scores_of(q, c[:cached, lanes], bias_ref[k]) for k, c in enumerate((c0, c1, keys_ref, c3))]
+        scores.append(scores_of(q, fresh_keys[:, lanes], fresh_ref[...]))
         values = [c[cached : 2 * cached, lanes] for c in (c0, c1)]
         values += [rest_ref[:cached, lanes], c3[cached : 2 * cached, lanes]]
         values.append(fresh_values[:, lanes])
@@ -601,7 +603,18 @@
         shaped(2 * cached + 4 * rows, kv_cols),
     )
 
-    *held, halves_far = lax.optimization_barrier((*held, halves_far))
+    bias, fresh_bias = small_call(
+        functools.partial(bias_kernel, seq_dev),
+        spots,
+        [],
+        [
+            jax.ShapeDtypeStruct((SIDE, rows, seq_dev * span), F32),
+            jax.ShapeDtypeStruct((rows, rows), F32),
+        ],
+    )
+    *held, halves_far, bias, fresh_bias = lax.optimization_barrier(
+        (*held, halves_far, bias, fresh_bias)
+    )
     held = after(held, *cache_send, q_slots, o_slots, spots, froms)
     unit = (rank // 2, width)
     slab = slab // unit[0]
@@ -655,12 +668,12 @@
 
     vmem_spec = pl.BlockSpec(memory_space=pltpu.VMEM)
     attn = pl.pallas_call(
-        functools.partial(attention_kernel, seq_dev),
+        attention_kernel,
         out_shape=jax.ShapeDtypeStruct((rows, q_weight.shape[1]), BF16),
-        in_specs=[pl.BlockSpec(memory_space=pltpu.SMEM)] + [vmem_spec] * 7,
+        in_specs=[vmem_spec] * 9,
         out_specs=vmem_spec,
         compiler_params=pltpu.CompilerParams(vmem_limit_bytes=8 * MIB),
-    )(spots, q_near_sum, q_far_sum, *caches)
+    )(bias, fresh_bias, q_near_sum, q_far_sum, *caches)
 
     o_merged = merge_call(
         merge_kernel,

time: 97.1 us -> 96.6 us (level)
  waiting for transfers between devices: 37 us -> 35.7 us
    ppermute x7, waiting for transfers between devices: 10.4 us -> 9.16 us  [along_tp(): return lax.ppermute(x, 'tp', [(i, (i + k) % SIDE) for i in range(SIDE)])]
    unnamed x8 -> x6, local copies, waits for them, and re-layouts: 1.99 us -> 1.99 us
  transfers between devices with their start and end apart: 31 -> 31, of which waited for: 14 -> 14; matrix products, arithmetic and copies ran while one was open for 2% -> 3% of each run, Pallas kernels for 19% -> 19%
where the time goes in v5:
time: 96.6 us; the launch traced here: 96.3 us
  waiting for transfers between devices  35.7 us (37%)
  starting transfers between devices  33.1 us (34%)
  Pallas kernels  21.8 us (23%)
  local copies, waits for them, and re-layouts  3.76 us (4%)
  other arithmetic  1.7 us (2%)
    ppermute x4, waiting for transfers between devices, to_holder(): return lax.ppermute(x, ('tp', 'dp'), pairs)  13.5 us
    ppermute x7, starting transfers between devices, along_tp(): return lax.ppermute(x, 'tp', [(i, (i + k) % SIDE) for i in range(SIDE)])  12.9 us
    pallas_call x2, Pallas kernels, merge_call(): pl.pallas_call(kernel, out_shape=out_shape, in_specs=[pl.BlockSpec(memory...  12.1 us
    ppermute x7, waiting for transfers between devices, along_tp(): return lax.ppermute(x, 'tp', [(i, (i + k) % SIDE) for i in range(SIDE)])  9.16 us
    ppermute x16, starting transfers between devices, across_dp(): return lax.ppermute(x, 'dp', [(i, i ^ k) for i in range(SIDE)])  8.73 us
    ppermute x4, waiting for transfers between devices, across_groups(): return lax.ppermute(x, 'groups', [(0, 1), (1, 0)])  8.45 us
    ppermute x4, starting transfers between devices, to_holder(): return lax.ppermute(x, ('tp', 'dp'), pairs)  6.31 us
    ppermute x4, starting transfers between devices, across_groups(): return lax.ppermute(x, 'groups', [(0, 1), (1, 0)])  5.2 us
  transfers between devices with their start and end apart: 31, of which 14 were waited for; matrix products, arithmetic and copies ran while one was open for 3% of the time, Pallas kernels for 19%

profile of v5, /device:TPU:0, one launch (start us, length us, event | category | flops | bytes accessed | tf_op | source)
XLA Modules:
  0.0 96.3 jit_solution(11841038706965020761)
XLA Ops:
  1.0 5.1 %collective-permute-start.2 = (bf16[192,512]{1,0:T(8,128)(2,1)S(1)}, bf16[192,512]{1,0:T(8,128)(2,1)S(1)}, u32[]{:S(2)}, u32[]{:S(2)}) collective-permute-start(bf16[192,512]{1,0:T(8,128)(2,1)S(1)} %shard_map.91.refs_0_), channel_id=1, source_target_pairs={{0,12},{4,0},{8,4},{12,8},{1,13},{5,1},{9,5},{13,9},{2,14},{6,2},{... | collective-permute-start | bytes 589832 | tf_op jit(solution)/shard_map/ppermute | solution.py:23
  7.1 1.5 %collective-permute-start.3 = (bf16[4,2,32,512]{3,2,1,0:T(8,128)(2,1)}, bf16[4,2,32,512]{3,2,1,0:T(8,128)(2,1)S(1)}, u32[]{:S(2)}, u32[]{:S(2)}) collective-permute-start(bf16[4,2,32,512]{3,2,1,0:T(8,128)(2,1)} %bitcast.14), channel_id=1, source_target_pairs={{0,2},{1,3},{2,0},{3,1},{4,6},{5,7},{6,4},{7,5},{8,10},{9,11},{10,... | collective-permute-start | bytes 786440 | tf_op jit(solution)/shard_map/ppermute | solution.py:27
  13.8 4.3 %shard_map.93 = (bf16[448,256]{1,0:T(8,128)(2,1)S(1)}, bf16[448,256]{1,0:T(8,128)(2,1)S(1)}, bf16[448,256]{1,0:T(8,128)(2,1)S(1)}, bf16[448,256]{1,0:T(8,128)(2,1)S(1)}) custom-call(s32[4]{0:T(128)S(1)} %and_select_fusion.heads_ref, bf16[16,2048]{1,0:T(8,128)(2,1)S(1)} %reshape.29.tokens_ref, bf16[192,1024]{1,0:T(8,128)(2,1)S(1)} %bitcast.19, ...), custom_call_target="tpu_custom_call" | custom-call | flops 134217728 | bytes 16777216 | tf_op jit(solution)/shard_map/pallas_call | solution.py:166
  18.1 4.6 %collective-permute-done.1.refs_2_ = bf16[192,512]{1,0:T(8,128)(2,1)S(1)} collective-permute-done((bf16[192,512]{1,0:T(8,128)(2,1)S(1)}, bf16[192,512]{1,0:T(8,128)(2,1)S(1)}, u32[]{:S(2)}, u32[]{:S(2)}) %collective-permute-start.1) | collective-permute-done | bytes 196640 | tf_op jit(solution)/shard_map/ppermute | solution.py:23
  23.5 1.6 %collective-permute-start.4 = (bf16[10,32,512]{2,1,0:T(8,128)(2,1)S(1)}, bf16[10,32,512]{2,1,0:T(8,128)(2,1)S(1)}, u32[]{:S(2)}, u32[]{:S(2)}) collective-permute-start(bf16[10,32,512]{2,1,0:T(8,128)(2,1)S(1)} %get-tuple-element.65), channel_id=1, source_target_pairs={{0,2},{1,3},{2,0},{3,1},{4,6},{5,7},{6,4},{7,5},{8,10},{9,11},{10,... | collective-permute-start | bytes 983048 | tf_op jit(solution)/shard_map/ppermute | solution.py:27
  25.9 2.9 %collective-permute-start.7 = (bf16[448,256]{1,0:T(8,128)(2,1)S(1)}, bf16[448,256]{1,0:T(8,128)(2,1)S(1)}, u32[]{:S(2)}, u32[]{:S(2)}) collective-permute-start(bf16[448,256]{1,0:T(8,128)(2,1)S(1)} %get-tuple-element.67), channel_id=1, source_target_pairs={{0,12},{4,0},{8,4},{12,8},{1,13},{5,1},{9,5},{13,9},{2,14},{6,2},{... | collective-permute-start | bytes 688136 | tf_op jit(solution)/shard_map/ppermute | solution.py:23
  28.9 1.5 %collective-permute-start.5 = (bf16[6,32,512]{2,1,0:T(8,128)(2,1)S(1)}, bf16[6,32,512]{2,1,0:T(8,128)(2,1)S(1)}, u32[]{:S(2)}, u32[]{:S(2)}) collective-permute-start(bf16[6,32,512]{2,1,0:T(8,128)(2,1)S(1)} %get-tuple-element.64.refs_2_), channel_id=1, source_target_pairs={{0,16},{16,0},{1,17},{17,1},{2,18},{18,2},{3,19},{19,3},{4,20},{20... | collective-permute-start | bytes 589832 | tf_op jit(solution)/shard_map/ppermute | solution.py:31
  30.4 4.2 %collective-permute-done.5.refs_4_ = bf16[6,32,512]{2,1,0:T(8,128)(2,1)S(1)} collective-permute-done((bf16[6,32,512]{2,1,0:T(8,128)(2,1)S(1)}, bf16[6,32,512]{2,1,0:T(8,128)(2,1)S(1)}, u32[]{:S(2)}, u32[]{:S(2)}) %collective-permute-start.5) | collective-permute-done | bytes 196640 | tf_op jit(solution)/shard_map/ppermute | solution.py:31
  35.4 2.3 %collective-permute-done.7.c3 = bf16[448,256]{1,0:T(8,128)(2,1)S(1)} collective-permute-done((bf16[448,256]{1,0:T(8,128)(2,1)S(1)}, bf16[448,256]{1,0:T(8,128)(2,1)S(1)}, u32[]{:S(2)}, u32[]{:S(2)}) %collective-permute-start.7) | collective-permute-done | bytes 229408 | tf_op jit(solution)/shard_map/ppermute | solution.py:23
  37.9 1.6 %collective-permute-start.9 = (bf16[3,32,512]{2,1,0:T(8,128)(2,1)S(1)}, bf16[3,32,512]{2,1,0:T(8,128)(2,1)S(1)}, u32[]{:S(2)}, u32[]{:S(2)}) collective-permute-start(bf16[3,32,512]{2,1,0:T(8,128)(2,1)S(1)} %slice.46), channel_id=1, source_target_pairs={{0,16},{16,0},{1,17},{17,1},{2,18},{18,2},{3,19},{19,3},{4,20},{20... | collective-permute-start | bytes 294920 | tf_op jit(solution)/shard_map/ppermute | solution.py:31
  40.1 3.1 %collective-permute-done.9.refs_2_ = bf16[3,32,512]{2,1,0:T(8,128)(2,1)S(1)} collective-permute-done((bf16[3,32,512]{2,1,0:T(8,128)(2,1)S(1)}, bf16[3,32,512]{2,1,0:T(8,128)(2,1)S(1)}, u32[]{:S(2)}, u32[]{:S(2)}) %collective-permute-start.9) | collective-permute-done | bytes 98336 | tf_op jit(solution)/shard_map/ppermute | solution.py:31
  45.6 1.5 %collective-permute-start.13 = (bf16[192,256]{1,0:T(8,128)(2,1)S(1)}, bf16[192,256]{1,0:T(8,128)(2,1)S(1)}, u32[]{:S(2)}, u32[]{:S(2)}) collective-permute-start(bf16[192,256]{1,0:T(8,128)(2,1)S(1)} %slice.47), channel_id=1, source_target_pairs={{0,8},{4,12},{8,0},{12,4},{1,9},{5,13},{9,1},{13,5},{2,10},{6,14},... | collective-permute-start | bytes 294920 | tf_op jit(solution)/shard_map/ppermute | solution.py:23
  47.2 6.5 %shard_map.96 = f32[64,2048]{1,0:T(8,128)S(1)} custom-call(s32[18]{0:T(128)S(1)} %concatenate.13.slots_ref, bf16[32,32,512]{2,1,0:T(8,128)(2,1)S(1)} %shard_map.95.refs_0_, bf16[3,32,512]{2,1,0:T(8,128)(2,1)S(1)} %collective-permute-done.8.refs_1_, bf16[3,32,512]{2,1,0:T(8,128)(2,1)S(1)} %collective-permute-done.9.refs_2_, ...), custom_call_target="tpu_custom_call" | custom-call | tf_op jit(solution)/shard_map/pallas_call | solution.py:324
  54.0 1.5 %collective-permute-done.16 = f32[32,2048]{1,0:T(8,128)S(1)} collective-permute-done((f32[32,2048]{1,0:T(8,128)S(1)}, f32[32,2048]{1,0:T(8,128)S(1)}, u32[]{:S(2)}, u32[]{:S(2)}) %collective-permute-start.16) | collective-permute-done | bytes 262176 | tf_op jit(solution)/shard_map/ppermute | solution.py:27
  55.7 1.4 %collective-permute-start.18 = (bf16[256,256]{1,0:T(8,128)(2,1)S(1)}, bf16[256,256]{1,0:T(8,128)(2,1)S(1)}, u32[]{:S(2)}, u32[]{:S(2)}) collective-permute-start(bf16[256,256]{1,0:T(8,128)(2,1)S(1)} %slice.48), channel_id=1, source_target_pairs={{0,8},{4,12},{8,0},{12,4},{1,9},{5,13},{9,1},{13,5},{2,10},{6,14},... | collective-permute-start | bytes 393224 | tf_op jit(solution)/shard_map/ppermute | solution.py:23
  57.1 1.6 %collective-permute-start.22 = (bf16[3,32,512]{2,1,0:T(8,128)(2,1)S(1)}, bf16[3,32,512]{2,1,0:T(8,128)(2,1)S(1)}, u32[]{:S(2)}, u32[]{:S(2)}) collective-permute-start(bf16[3,32,512]{2,1,0:T(8,128)(2,1)S(1)} %slice.55), channel_id=1, source_target_pairs={{0,2},{1,3},{2,0},{3,1},{4,6},{5,7},{6,4},{7,5},{8,10},{9,11},{10,... | collective-permute-start | bytes 294920 | tf_op jit(solution)/shard_map/ppermute | solution.py:27
  59.3 1.6 %collective-permute-start.23 = (bf16[3,32,512]{2,1,0:T(8,128)(2,1)S(1)}, bf16[3,32,512]{2,1,0:T(8,128)(2,1)S(1)}, u32[]{:S(2)}, u32[]{:S(2)}) collective-permute-start(bf16[3,32,512]{2,1,0:T(8,128)(2,1)S(1)} %slice.56), channel_id=1, source_target_pairs={{0,16},{16,0},{1,17},{17,1},{2,18},{18,2},{3,19},{19,3},{4,20},{20... | collective-permute-start | bytes 294920 | tf_op jit(solution)/shard_map/ppermute | solution.py:31
  60.9 1.8 %collective-permute-done.22.refs_1_ = bf16[3,32,512]{2,1,0:T(8,128)(2,1)S(1)} collective-permute-done((bf16[3,32,512]{2,1,0:T(8,128)(2,1)S(1)}, bf16[3,32,512]{2,1,0:T(8,128)(2,1)S(1)}, u32[]{:S(2)}, u32[]{:S(2)}) %collective-permute-start.22) | collective-permute-done | bytes 98336 | tf_op jit(solution)/shard_map/ppermute | solution.py:27
  68.5 5.6 %shard_map.99.w_ref = bf16[2048,2048]{1,0:T(8,128)(2,1)S(1)} custom-call(s32[18]{0:T(128)S(1)} %concatenate.14.slots_ref, bf16[26,32,512]{2,1,0:T(8,128)(2,1)S(1)} %shard_map.98.refs_0_, bf16[3,32,512]{2,1,0:T(8,128)(2,1)S(1)} %collective-permute-done.22.refs_1_, bf16[3,32,512]{2,1,0:T(8,128)(2,1)S(1)} %collective-permute-done.23.refs_2_, ...), custom_call_target="tpu_custom_call" | custom-call | bytes 16777216 | tf_op jit(solution)/shard_map/pallas_call | solution.py:324
  74.2 1.6 %shard_map.100 = (f32[16,2048]{1,0:T(8,128)S(1)}, bf16[3,16,2048]{2,1,0:T(8,128)(2,1)S(1)}) custom-call(s32[1]{0:T(128)} %bitcast.turn_ref, bf16[16,2048]{1,0:T(8,128)(2,1)S(1)} %shard_map.97.a0, bf16[16,2048]{1,0:T(8,128)(2,1)S(1)} %collective-permute-done.19.a1, bf16[16,2048]{1,0:T(8,128)(2,1)S(1)} %collective-permute-done.20.a2, ...), custom_call_target="tpu_custom_call" | custom-call | tf_op jit(solution)/shard_map/pallas_call | solution.py:691
  76.5 1.9 %collective-permute-start.28 = (bf16[16,2048]{1,0:T(8,128)(2,1)S(1)}, bf16[16,2048]{1,0:T(8,128)(2,1)S(1)}, u32[]{:S(2)}, u32[]{:S(2)}) collective-permute-start(bf16[16,2048]{1,0:T(8,128)(2,1)S(1)} %get-tuple-element.91), channel_id=1, source_target_pairs={{0,1},{1,5},{2,9},{3,13},{4,0},{5,4},{6,8},{7,12},{8,3},{9,7},{10,... | collective-permute-start | bytes 196616 | tf_op jit(solution)/shard_map/ppermute | solution.py:36
  78.4 3.7 %collective-permute-start.30 = (bf16[16,2048]{1,0:T(8,128)(2,1)S(1)}, bf16[16,2048]{1,0:T(8,128)(2,1)S(1)}, u32[]{:S(2)}, u32[]{:S(2)}) collective-permute-start(bf16[16,2048]{1,0:T(8,128)(2,1)S(1)} %get-tuple-element.92), channel_id=1, source_target_pairs={{0,3},{1,7},{2,11},{3,15},{4,2},{5,6},{6,10},{7,14},{8,1},{9,5},{1... | collective-permute-start | bytes 196616 | tf_op jit(solution)/shard_map/ppermute | solution.py:36
  83.2 5.3 %collective-permute-done.30 = bf16[16,2048]{1,0:T(8,128)(2,1)S(1)} collective-permute-done((bf16[16,2048]{1,0:T(8,128)(2,1)S(1)}, bf16[16,2048]{1,0:T(8,128)(2,1)S(1)}, u32[]{:S(2)}, u32[]{:S(2)}) %collective-permute-start.30) | collective-permute-done | bytes 65568 | tf_op jit(solution)/shard_map/ppermute | solution.py:36
  88.5 7.1 %collective-permute-done.29 = bf16[16,2048]{1,0:T(8,128)(2,1)S(1)} collective-permute-done((bf16[16,2048]{1,0:T(8,128)(2,1)S(1)}, bf16[16,2048]{1,0:T(8,128)(2,1)S(1)}, u32[]{:S(2)}, u32[]{:S(2)}) %collective-permute-start.29) | collective-permute-done | bytes 65568 | tf_op jit(solution)/shard_map/ppermute | solution.py:36
  (74 shorter events, 22.3 us)
Async XLA Ops:
  1.0 17.2 %collective-permute-start.2 = (bf16[192,512]{1,0:T(8,128)(2,1)S(1)}, bf16[192,512]{1,0:T(8,128)(2,1)S(1)}, u32[]{:S(2)}, u32[]{:S(2)}) collective-permute-start(bf16[192,512]{1,0:T(8,128)(2,1)S(1)} %shard_map.91.refs_0_), channel_id=1, source_target_pairs={{0,12},{4,0},{8,4},{12,8},{1,13},{5,1},{9,5},{13,9},{2,14},{6,2},{... | collective-permute-start | bytes 589832 | tf_op jit(solution)/shard_map/ppermute | solution.py:23
  6.1 16.7 %collective-permute-start.1 = (bf16[192,512]{1,0:T(8,128)(2,1)S(1)}, bf16[192,512]{1,0:T(8,128)(2,1)S(1)}, u32[]{:S(2)}, u32[]{:S(2)}) collective-permute-start(bf16[192,512]{1,0:T(8,128)(2,1)S(1)} %shard_map.91.refs_0_), channel_id=1, source_target_pairs={{0,8},{4,12},{8,0},{12,4},{1,9},{5,13},{9,1},{13,5},{2,10},{6,14},... | collective-permute-start | bytes 589832 | tf_op jit(solution)/shard_map/ppermute | solution.py:23
  6.1 16.7 %collective-permute-start = (bf16[192,512]{1,0:T(8,128)(2,1)S(1)}, bf16[192,512]{1,0:T(8,128)(2,1)S(1)}, u32[]{:S(2)}, u32[]{:S(2)}) collective-permute-start(bf16[192,512]{1,0:T(8,128)(2,1)S(1)} %shard_map.91.refs_0_), channel_id=1, source_target_pairs={{0,4},{4,8},{8,12},{12,0},{1,5},{5,9},{9,13},{13,1},{2,6},{6,10},{... | collective-permute-start | bytes 589832 | tf_op jit(solution)/shard_map/ppermute | solution.py:23
  7.1 15.7 %collective-permute-start.3 = (bf16[4,2,32,512]{3,2,1,0:T(8,128)(2,1)}, bf16[4,2,32,512]{3,2,1,0:T(8,128)(2,1)S(1)}, u32[]{:S(2)}, u32[]{:S(2)}) collective-permute-start(bf16[4,2,32,512]{3,2,1,0:T(8,128)(2,1)} %bitcast.14), channel_id=1, source_target_pairs={{0,2},{1,3},{2,0},{3,1},{4,6},{5,7},{6,4},{7,5},{8,10},{9,11},{10,... | collective-permute-start | bytes 786440 | tf_op jit(solution)/shard_map/ppermute | solution.py:27
  23.5 14.3 %collective-permute-start.4 = (bf16[10,32,512]{2,1,0:T(8,128)(2,1)S(1)}, bf16[10,32,512]{2,1,0:T(8,128)(2,1)S(1)}, u32[]{:S(2)}, u32[]{:S(2)}) collective-permute-start(bf16[10,32,512]{2,1,0:T(8,128)(2,1)S(1)} %get-tuple-element.65), channel_id=1, source_target_pairs={{0,2},{1,3},{2,0},{3,1},{4,6},{5,7},{6,4},{7,5},{8,10},{9,11},{10,... | collective-permute-start | bytes 983048 | tf_op jit(solution)/shard_map/ppermute | solution.py:27
  25.0 10.4 %collective-permute-start.6 = (bf16[448,256]{1,0:T(8,128)(2,1)S(1)}, bf16[448,256]{1,0:T(8,128)(2,1)S(1)}, u32[]{:S(2)}, u32[]{:S(2)}) collective-permute-start(bf16[448,256]{1,0:T(8,128)(2,1)S(1)} %get-tuple-element.66), channel_id=1, source_target_pairs={{0,4},{4,8},{8,12},{12,0},{1,5},{5,9},{9,13},{13,1},{2,6},{6,10},{... | collective-permute-start | bytes 688136 | tf_op jit(solution)/shard_map/ppermute | solution.py:23
  25.9 11.8 %collective-permute-start.7 = (bf16[448,256]{1,0:T(8,128)(2,1)S(1)}, bf16[448,256]{1,0:T(8,128)(2,1)S(1)}, u32[]{:S(2)}, u32[]{:S(2)}) collective-permute-start(bf16[448,256]{1,0:T(8,128)(2,1)S(1)} %get-tuple-element.67), channel_id=1, source_target_pairs={{0,12},{4,0},{8,4},{12,8},{1,13},{5,1},{9,5},{13,9},{2,14},{6,2},{... | collective-permute-start | bytes 688136 | tf_op jit(solution)/shard_map/ppermute | solution.py:23
  28.9 5.7 %collective-permute-start.5 = (bf16[6,32,512]{2,1,0:T(8,128)(2,1)S(1)}, bf16[6,32,512]{2,1,0:T(8,128)(2,1)S(1)}, u32[]{:S(2)}, u32[]{:S(2)}) collective-permute-start(bf16[6,32,512]{2,1,0:T(8,128)(2,1)S(1)} %get-tuple-element.64.refs_2_), channel_id=1, source_target_pairs={{0,16},{16,0},{1,17},{17,1},{2,18},{18,2},{3,19},{19,3},{4,20},{20... | collective-permute-start | bytes 589832 | tf_op jit(solution)/shard_map/ppermute | solution.py:31
  37.8 9.3 %collective-permute-start.10 = (bf16[32,32,512]{2,1,0:T(8,128)(2,1)S(1)}, bf16[32,32,512]{2,1,0:T(8,128)(2,1)S(1)}, u32[]{:S(2)}, u32[]{:S(2)}) collective-permute-start(bf16[32,32,512]{2,1,0:T(8,128)(2,1)S(1)} %shard_map.95.refs_0_), channel_id=1, source_target_pairs={{0,1},{1,0},{2,3},{3,2},{4,5},{5,4},{6,7},{7,6},{8,9},{9,8},{10,11... | collective-permute-start | bytes 3145736 | tf_op jit(solution)/shard_map/ppermute | solution.py:27
  44.5 9.3 %collective-permute-start.15 = (bf16[6,32,512]{2,1,0:T(8,128)(2,1)S(1)}, bf16[6,32,512]{2,1,0:T(8,128)(2,1)S(1)}, u32[]{:S(2)}, u32[]{:S(2)}) collective-permute-start(bf16[6,32,512]{2,1,0:T(8,128)(2,1)S(1)} %get-tuple-element.74.refs_2_), channel_id=1, source_target_pairs={{0,16},{16,0},{1,17},{17,1},{2,18},{18,2},{3,19},{19,3},{4,20},{20... | collective-permute-start | bytes 589832 | tf_op jit(solution)/shard_map/ppermute | solution.py:31
  45.0 8.8 %collective-permute-start.14 = (bf16[6,32,512]{2,1,0:T(8,128)(2,1)S(1)}, bf16[6,32,512]{2,1,0:T(8,128)(2,1)S(1)}, u32[]{:S(2)}, u32[]{:S(2)}) collective-permute-start(bf16[6,32,512]{2,1,0:T(8,128)(2,1)S(1)} %get-tuple-element.74.refs_2_), channel_id=1, source_target_pairs={{0,2},{1,3},{2,0},{3,1},{4,6},{5,7},{6,4},{7,5},{8,10},{9,11},{10,... | collective-permute-start | bytes 589832 | tf_op jit(solution)/shard_map/ppermute | solution.py:27
  45.6 8.2 %collective-permute-start.13 = (bf16[192,256]{1,0:T(8,128)(2,1)S(1)}, bf16[192,256]{1,0:T(8,128)(2,1)S(1)}, u32[]{:S(2)}, u32[]{:S(2)}) collective-permute-start(bf16[192,256]{1,0:T(8,128)(2,1)S(1)} %slice.47), channel_id=1, source_target_pairs={{0,8},{4,12},{8,0},{12,4},{1,9},{5,13},{9,1},{13,5},{2,10},{6,14},... | collective-permute-start | bytes 294920 | tf_op jit(solution)/shard_map/ppermute | solution.py:23
  55.5 13.0 %collective-permute-start.24 = (bf16[26,32,512]{2,1,0:T(8,128)(2,1)S(1)}, bf16[26,32,512]{2,1,0:T(8,128)(2,1)S(1)}, u32[]{:S(2)}, u32[]{:S(2)}) collective-permute-start(bf16[26,32,512]{2,1,0:T(8,128)(2,1)S(1)} %shard_map.98.refs_0_), channel_id=1, source_target_pairs={{0,1},{1,0},{2,3},{3,2},{4,5},{5,4},{6,7},{7,6},{8,9},{9,8},{10,11... | collective-permute-start | bytes 2555912 | tf_op jit(solution)/shard_map/ppermute | solution.py:27
  55.7 9.5 %collective-permute-start.18 = (bf16[256,256]{1,0:T(8,128)(2,1)S(1)}, bf16[256,256]{1,0:T(8,128)(2,1)S(1)}, u32[]{:S(2)}, u32[]{:S(2)}) collective-permute-start(bf16[256,256]{1,0:T(8,128)(2,1)S(1)} %slice.48), channel_id=1, source_target_pairs={{0,8},{4,12},{8,0},{12,4},{1,9},{5,13},{9,1},{13,5},{2,10},{6,14},... | collective-permute-start | bytes 393224 | tf_op jit(solution)/shard_map/ppermute | solution.py:23
  57.1 5.6 %collective-permute-start.22 = (bf16[3,32,512]{2,1,0:T(8,128)(2,1)S(1)}, bf16[3,32,512]{2,1,0:T(8,128)(2,1)S(1)}, u32[]{:S(2)}, u32[]{:S(2)}) collective-permute-start(bf16[3,32,512]{2,1,0:T(8,128)(2,1)S(1)} %slice.55), channel_id=1, source_target_pairs={{0,2},{1,3},{2,0},{3,1},{4,6},{5,7},{6,4},{7,5},{8,10},{9,11},{10,... | collective-permute-start | bytes 294920 | tf_op jit(solution)/shard_map/ppermute | solution.py:27
  58.7 6.5 %collective-permute-start.17 = (f32[16,2048]{1,0:T(8,128)S(1)}, f32[16,2048]{1,0:T(8,128)S(1)}, u32[]{:S(2)}, u32[]{:S(2)}) collective-permute-start(f32[16,2048]{1,0:T(8,128)S(1)} %get-tuple-element.87), channel_id=1, source_target_pairs={{0,2},{1,3},{2,0},{3,1},{4,6},{5,7},{6,4},{7,5},{8,10},{9,11},{10,... | collective-permute-start | bytes 393224 | tf_op jit(solution)/shard_map/ppermute | solution.py:27
  62.8 5.5 %collective-permute-start.25 = (bf16[3,32,512]{2,1,0:T(8,128)(2,1)S(1)}, bf16[3,32,512]{2,1,0:T(8,128)(2,1)S(1)}, u32[]{:S(2)}, u32[]{:S(2)}) collective-permute-start(bf16[3,32,512]{2,1,0:T(8,128)(2,1)S(1)} %collective-permute-done.22.refs_1_), channel_id=1, source_target_pairs={{0,1},{1,0},{2,3},{3,2},{4,5},{5,4},{6,7},{7,6},{8,9},{9,8},{10,11... | collective-permute-start | bytes 294920 | tf_op jit(solution)/shard_map/ppermute | solution.py:27
  66.6 7.6 %collective-permute-start.21 = (bf16[16,2048]{1,0:T(8,128)(2,1)S(1)}, bf16[16,2048]{1,0:T(8,128)(2,1)S(1)}, u32[]{:S(2)}, u32[]{:S(2)}) collective-permute-start(bf16[16,2048]{1,0:T(8,128)(2,1)S(1)} %shard_map.97.a0), channel_id=1, source_target_pairs={{0,3},{1,2},{2,1},{3,0},{4,7},{5,6},{6,5},{7,4},{8,11},{9,10},{10,... | collective-permute-start | bytes 196616 | tf_op jit(solution)/shard_map/ppermute | solution.py:27
  67.8 6.4 %collective-permute-start.20 = (bf16[16,2048]{1,0:T(8,128)(2,1)S(1)}, bf16[16,2048]{1,0:T(8,128)(2,1)S(1)}, u32[]{:S(2)}, u32[]{:S(2)}) collective-permute-start(bf16[16,2048]{1,0:T(8,128)(2,1)S(1)} %shard_map.97.a0), channel_id=1, source_target_pairs={{0,2},{1,3},{2,0},{3,1},{4,6},{5,7},{6,4},{7,5},{8,10},{9,11},{10,... | collective-permute-start | bytes 196616 | tf_op jit(solution)/shard_map/ppermute | solution.py:27
  68.3 5.9 %collective-permute-start.19 = (bf16[16,2048]{1,0:T(8,128)(2,1)S(1)}, bf16[16,2048]{1,0:T(8,128)(2,1)S(1)}, u32[]{:S(2)}, u32[]{:S(2)}) collective-permute-start(bf16[16,2048]{1,0:T(8,128)(2,1)S(1)} %shard_map.97.a0), channel_id=1, source_target_pairs={{0,1},{1,0},{2,3},{3,2},{4,5},{5,4},{6,7},{7,6},{8,9},{9,8},{10,11... | collective-permute-start | bytes 196616 | tf_op jit(solution)/shard_map/ppermute | solution.py:27
  75.8 19.8 %collective-permute-start.27 = (f32[16,2048]{1,0:T(8,128)S(1)}, f32[16,2048]{1,0:T(8,128)S(1)}, u32[]{:S(2)}, u32[]{:S(2)}) collective-permute-start(f32[16,2048]{1,0:T(8,128)S(1)} %get-tuple-element.85), channel_id=1, source_target_pairs={{0,0},{1,4},{2,8},{3,12},{4,1},{5,5},{6,9},{7,13},{8,2},{9,6},{10,... | collective-permute-start | bytes 393224 | tf_op jit(solution)/shard_map/ppermute | solution.py:36
  76.5 6.7 %collective-permute-start.28 = (bf16[16,2048]{1,0:T(8,128)(2,1)S(1)}, bf16[16,2048]{1,0:T(8,128)(2,1)S(1)}, u32[]{:S(2)}, u32[]{:S(2)}) collective-permute-start(bf16[16,2048]{1,0:T(8,128)(2,1)S(1)} %get-tuple-element.91), channel_id=1, source_target_pairs={{0,1},{1,5},{2,9},{3,13},{4,0},{5,4},{6,8},{7,12},{8,3},{9,7},{10,... | collective-permute-start | bytes 196616 | tf_op jit(solution)/shard_map/ppermute | solution.py:36
  78.4 10.1 %collective-permute-start.30 = (bf16[16,2048]{1,0:T(8,128)(2,1)S(1)}, bf16[16,2048]{1,0:T(8,128)(2,1)S(1)}, u32[]{:S(2)}, u32[]{:S(2)}) collective-permute-start(bf16[16,2048]{1,0:T(8,128)(2,1)S(1)} %get-tuple-element.92), channel_id=1, source_target_pairs={{0,3},{1,7},{2,11},{3,15},{4,2},{5,6},{6,10},{7,14},{8,1},{9,5},{1... | collective-permute-start | bytes 196616 | tf_op jit(solution)/shard_map/ppermute | solution.py:36
  82.1 13.5 %collective-permute-start.29 = (bf16[16,2048]{1,0:T(8,128)(2,1)S(1)}, bf16[16,2048]{1,0:T(8,128)(2,1)S(1)}, u32[]{:S(2)}, u32[]{:S(2)}) collective-permute-start(bf16[16,2048]{1,0:T(8,128)(2,1)S(1)} %get-tuple-element.93), channel_id=1, source_target_pairs={{0,2},{1,6},{2,10},{3,14},{4,3},{5,7},{6,11},{7,15},{8,0},{9,4},{1... | collective-permute-start | bytes 196616 | tf_op jit(solution)/shard_map/ppermute | solution.py:36
  (10 other events, 64.8 us)
